TPU v7x, 32 devices: a whole 2x2x4 slice. The times are simulated.
32 devices in a mesh: dp: 4 (over y, x), expert: 8 (over z, core).
Axes of the slice: x: 2, y: 2, z: 4, core: 2. Of those that a mesh axis runs over, the one named last changes fastest.
Arguments:
- tokens: bfloat16 [64, 4096], P('expert', 'dp'), may hold values from -6 to 6
- output_gradient: bfloat16 [64, 4096], P('expert', 'dp'), may hold values from -6 to 6
- routes: int32 [64, 2], P('expert'), may hold values from 0 to 3, all different within a row; in each aligned block of 8 rows (0 to 7, 8 to 15, ...) at most 8 rows name the same one
- router_expert_weight: bfloat16 [64, 2], P('expert'), may hold values from 0.049804688 to 0.5
- tenant: int32 [64], P('expert'), may hold values from 0 to 3
- gate_weight: bfloat16 [8, 4096, 512], P('expert', 'dp'), may hold values from -0.09375 to 0.09375
- up_weight: bfloat16 [8, 4096, 512], P('expert', 'dp'), may hold values from -0.09375 to 0.09375
- down_weight: bfloat16 [8, 512, 4096], P('expert', None, 'dp'), may hold values from -0.09375 to 0.09375
- adapter_input_maps: bfloat16 [8, 4096, 2, 4, 8], P('expert', 'dp'), may hold values from -0.09375 to 0.09375
- adapter_output_maps: bfloat16 [8, 2, 4, 16, 512], P('expert'), may hold values from -0.359375 to 0.359375
Outputs:
- input_grad: bfloat16 [64, 4096], P('expert', 'dp')
- adapter_a_grad: float32 [8, 4096, 2, 4, 8], P('expert', 'dp')
- adapter_b_grad: float32 [8, 2, 4, 16, 512], P('expert')
Inputs may be any that keep to these rules, and one draw needn't show every extreme that they name: `routes`: among the 8 tokens of each aligned block of rows (the tokens of one index of the expert axis), no expert is chosen more than 8 times, a bound that some block reaches; a token's choices are distinct.
All inputs are finite; a program needn't handle non-finite values.
Results may differ from a plain program's by a relative error of at most 0.0065.
Values may be sent and summed in bfloat16 or wider, within the bound.
No kernel may reach another device: no remote copies, remote signals or barrier semaphores. Data moves between devices by JAX's collectives and lax.ppermute only.
A program may use at most 64 MiB of HBM per device.

v0:
```python
import jax
import jax.numpy as jnp
from jax import lax
from jax.sharding import PartitionSpec as P

ADAPTER_SCALE = 2.0


def partner(shard, axis, bit):
    return lax.ppermute(shard, axis, [(i, i ^ 1 << bit) for i in range(lax.axis_size(axis))])


def product_leading(left, right):
    return lax.dot_general(
        left, right, (((0,), (0,)), ((), ())), preferred_element_type=jnp.float32
    )


def product_trailing(left, right):
    return lax.dot_general(
        left, right, (((1,), (1,)), ((), ())), preferred_element_type=jnp.float32
    )


def order_halves(mine, other, upper):
    return (jnp.where(upper, other, mine), jnp.where(upper, mine, other))


def spread(values, tenant_mask, tenant_list, adapter_rank_width):
    count = values.shape[0]
    wide = tenant_mask[:, None, :, None] * values.astype(jnp.float32).reshape(
        count, 2, 1, adapter_rank_width
    )
    return wide.reshape(count, 2, tenant_list * adapter_rank_width).astype(jnp.bfloat16)


def shards(
    tokens,
    output_gradient,
    routes,
    router_expert_weight,
    tenant,
    gate_weight,
    up_weight,
    down_weight,
    adapter_input_maps,
    adapter_output_maps,
):
    devices = lax.axis_size("expert")
    experts = devices // 2
    tok_col, quarter = tokens.shape
    topk = routes.shape[1]
    tenant_list = adapter_output_maps.shape[2]
    adapter_rank_width = adapter_output_maps.shape[3]
    hidden_halfway = adapter_output_maps.shape[4]
    rank_halfway = adapter_rank_width // 2
    capacity = 2 * tok_col * topk // experts
    half_cap = capacity // 2
    slots = devices * capacity
    upper = lax.axis_index("expert") % 2 == 1
    flat_route = routes.reshape(-1)
    expert_hot = (flat_route[:, None] == jnp.arange(experts, dtype=jnp.int32)[None, :]).astype(
        jnp.int32
    )
    earlier = jnp.cumsum(expert_hot, axis=0) - expert_hot
    position = jnp.sum(earlier * expert_hot, axis=1)
    slot_of = (flat_route * capacity + position).reshape(tok_col, topk)
    slot_range = jnp.arange(experts * capacity, dtype=jnp.int32)
    hits = (slot_range[:, None, None] == slot_of[None, :, :]).astype(jnp.float32)
    select_tok = jnp.sum(hits, axis=2)
    prob_tok = jnp.sum(hits * router_expert_weight.astype(jnp.float32)[None, :, :], axis=2)
    tenant_hot = (tenant[:, None] == jnp.arange(tenant_list, dtype=jnp.int32)[None, :]).astype(
        jnp.float32
    )
    select_bf = select_tok.astype(jnp.bfloat16)
    send_rows = jnp.dot(select_bf, tokens, preferred_element_type=jnp.float32).astype(jnp.bfloat16)
    send_grad = jnp.dot(select_bf, output_gradient, preferred_element_type=jnp.float32).astype(
        jnp.bfloat16
    )
    send_tag = jnp.dot(prob_tok, tenant_hot, precision=lax.Precision.HIGHEST).astype(jnp.bfloat16)

    def doubled(block):
        wide = block.reshape(experts, 1, capacity, block.shape[1])
        return jnp.broadcast_to(wide, (experts, 2, capacity, block.shape[1])).reshape(
            devices, capacity, block.shape[1]
        )

    got_rows, got_grad, got_tag = (
        lax.all_to_all(doubled(send_rows), "expert", split_axis=0, concat_axis=0, tiled=True),
        lax.all_to_all(doubled(send_grad), "expert", split_axis=0, concat_axis=0, tiled=True),
        lax.all_to_all(doubled(send_tag), "expert", split_axis=0, concat_axis=0, tiled=True),
    )
    input_rows = got_rows.reshape(slots, quarter)
    rows_dy = got_grad.reshape(slots, quarter)
    tags = got_tag.reshape(slots, tenant_list).astype(jnp.float32)
    tenant_mask = (tags > 0).astype(jnp.float32)
    slot_prob = jnp.sum(tags, axis=1)
    adapter_local = adapter_input_maps[0]
    adapter_other = partner(adapter_local, "expert", 0)
    low_rank, high_rank = order_halves(adapter_local, adapter_other, upper)
    adapter_cols = jnp.concatenate([low_rank, high_rank], axis=-1).reshape(
        quarter, 2 * tenant_list * adapter_rank_width
    )
    gate_output_map = adapter_output_maps[0, 0].reshape(
        tenant_list * adapter_rank_width, hidden_halfway
    )
    up_output_map = adapter_output_maps[0, 1].reshape(
        tenant_list * adapter_rank_width, hidden_halfway
    )
    gate_part = jnp.dot(input_rows, gate_weight[0], preferred_element_type=jnp.float32)
    up_part = jnp.dot(input_rows, up_weight[0], preferred_element_type=jnp.float32)
    act_part = product_trailing(rows_dy, down_weight[0])
    proj_all = jnp.dot(input_rows, adapter_cols, preferred_element_type=jnp.float32).reshape(
        slots, 2, tenant_list, adapter_rank_width
    )
    proj_part = jnp.sum(proj_all * tenant_mask[:, None, :, None], axis=2).reshape(
        slots, 2 * adapter_rank_width
    )
    gate_total, up_total, act_sum, proj_sum = lax.psum(
        (gate_part, up_part, act_part, proj_part), "dp"
    )
    proj_low = proj_sum.astype(jnp.bfloat16)
    spread_in = spread(proj_low, tenant_mask, tenant_list, adapter_rank_width)
    gate_preactivation = gate_total + ADAPTER_SCALE * jnp.dot(
        spread_in[:, 0], gate_output_map, preferred_element_type=jnp.float32
    )
    up_preactivation = up_total + ADAPTER_SCALE * jnp.dot(
        spread_in[:, 1], up_output_map, preferred_element_type=jnp.float32
    )
    act_grad = slot_prob[:, None] * act_sum
    gate_sig = jax.nn.sigmoid(gate_preactivation)
    gate_gradient = (
        act_grad * up_preactivation * gate_sig * (1.0 + gate_preactivation * (1.0 - gate_sig))
    ).astype(jnp.bfloat16)
    up_gradient = (act_grad * gate_preactivation * gate_sig).astype(jnp.bfloat16)
    gate_gradient, up_gradient, proj_low = (gate_gradient, up_gradient, proj_low)
    projection_spread = spread(proj_low, tenant_mask, tenant_list, adapter_rank_width)
    gate_output_map_gradient = ADAPTER_SCALE * product_leading(
        projection_spread[:, 0], gate_gradient
    )
    up_output_map_gradient = ADAPTER_SCALE * product_leading(projection_spread[:, 1], up_gradient)
    adapter_b_grad = jnp.stack([gate_output_map_gradient, up_output_map_gradient]).reshape(
        1, 2, tenant_list, adapter_rank_width, hidden_halfway
    )
    backward_total = ADAPTER_SCALE * jnp.stack(
        [
            product_trailing(gate_gradient, gate_output_map),
            product_trailing(up_gradient, up_output_map),
        ],
        axis=1,
    )
    back_part = jnp.sum(
        backward_total.reshape(slots, 2, tenant_list, adapter_rank_width)
        * tenant_mask[:, None, :, None],
        axis=2,
    ).reshape(slots, 2 * adapter_rank_width)
    input_part = product_trailing(gate_gradient, gate_weight[0]) + product_trailing(
        up_gradient, up_weight[0]
    )
    by_source = input_part.reshape(devices, capacity, quarter)
    first_half = by_source[:, :half_cap]
    second_half = by_source[:, half_cap:]
    keep_half = jnp.where(upper, second_half, first_half)
    give_half = jnp.where(upper, first_half, second_half)
    taken_half, back_other = partner((give_half, back_part), "expert", 0)
    input_half = keep_half + taken_half
    back_low = (back_part + back_other).astype(jnp.bfloat16)
    back_spread = spread(back_low, tenant_mask, tenant_list, adapter_rank_width)
    spread_rows = back_spread.reshape(devices, capacity, 2 * tenant_list * adapter_rank_width)
    spread_half = jnp.where(upper, spread_rows[:, half_cap:], spread_rows[:, :half_cap]).reshape(
        devices * half_cap, 2 * tenant_list * adapter_rank_width
    )
    adapter_term = product_trailing(spread_half, adapter_cols).reshape(devices, half_cap, quarter)
    slot_grad = (input_half + adapter_term).astype(jnp.bfloat16)
    spread_ranks = back_spread.reshape(slots, 2, tenant_list, adapter_rank_width)
    mine_cols = jnp.where(
        upper, spread_ranks[..., rank_halfway:], spread_ranks[..., :rank_halfway]
    ).reshape(slots, 2 * tenant_list * rank_halfway)
    adapter_a_grad = product_leading(input_rows, mine_cols).reshape(
        1, quarter, 2, tenant_list, rank_halfway
    )
    returned = lax.all_to_all(slot_grad, "expert", split_axis=0, concat_axis=0, tiled=True)
    slot_rows = returned.reshape(experts * capacity, quarter)
    input_grad = product_leading(select_bf, slot_rows).astype(jnp.bfloat16)
    return (input_grad, adapter_a_grad, adapter_b_grad)


def solution(mesh):
    placed = (
        P("expert", "dp"),
        P("expert", "dp"),
        P("expert", None),
        P("expert", None),
        P("expert"),
        P("expert", "dp", None),
        P("expert", "dp", None),
        P("expert", None, "dp"),
        P("expert", "dp", None, None, None),
        P("expert", None, None, None, None),
    )
    return jax.shard_map(
        shards,
        mesh=mesh,
        in_specs=placed,
        out_specs=(
            P("expert", "dp"),
            P("expert", "dp", None, None, None),
            P("expert", None, None, None, None),
        ),
        check_vma=False,
    )
```

profile of v0, /device:TPU:0, one launch (start us, length us, event | category | flops | bytes accessed | tf_op | source)
XLA Modules:
  0.0 113.5 jit_solution(13938264504517218432)
XLA Ops:
  7.2 0.8 convert_element_type.76
  8.1 0.1 eq.47
  8.3 0.2 select_reduce_fusion.1
  8.6 0.1 copy.64
  8.7 0.9 convolution_convert_fusion.3
  9.6 0.1 broadcast_in_dim.12
  9.7 0.6 broadcast_in_dim.13
  10.3 6.3 %all-to-all-start = ((bf16[8,8,4]{1,2,0:T(4,128)(2,1)}), bf16[8,8,4]{1,2,0:T(4,128)(2,1)S(1)}, u32[]{:S(2)}, u32[]{:S(2)}) async-start(bf16[8,8,4]{1,2,0:T(4,128)(2,1)} %bitcast), calls=%async_computation | async-start | bytes 16384 | tf_op jit(solution)/shard_map/all_to_all | solution.py:91
  16.7 0.5 collective-permute-start
  17.2 0.9 fusion.8
  18.1 0.9 fusion.7
  19.0 1.5 %fusion.48 = (bf16[1,1,4,16,512]{4,3,2,1,0:T(8,128)(2,1)}, bf16[1,1,4,16,512]{4,3,2,1,0:T(8,128)(2,1)S(1)}) fusion(bf16[1,2,4,16,512]{4,3,2,1,0:T(8,128)(2,1)} %param.19), kind=kLoop, calls=%fused_computation.85 | loop fusion | bytes 262144 | tf_op jit(solution)/shard_map/slice | solution.py:104
  20.5 1.8 %all-to-all-done = bf16[8,8,4]{1,2,0:T(4,128)(2,1)S(1)} async-done(((bf16[8,8,4]{1,2,0:T(4,128)(2,1)}), bf16[8,8,4]{1,2,0:T(4,128)(2,1)S(1)}, u32[]{:S(2)}, u32[]{:S(2)}) %all-to-all-start) | async-done | bytes 544 | tf_op jit(solution)/shard_map/all_to_all | solution.py:91
  22.3 0.7 broadcast_in_dim.17
  22.9 3.4 %all-to-all-start.2 = ((bf16[8,8,1024]{2,1,0:T(8,128)(2,1)}), bf16[8,8,1024]{2,1,0:T(8,128)(2,1)S(1)}, u32[]{:S(2)}, u32[]{:S(2)}) async-start(bf16[8,8,1024]{2,1,0:T(8,128)(2,1)} %bitcast.6), calls=%async_computation.2 | async-start | bytes 262144 | tf_op jit(solution)/shard_map/all_to_all | solution.py:89
  26.7 0.1 mul.163
  26.8 6.2 %all-to-all-done.2 = bf16[8,8,1024]{2,1,0:T(8,128)(2,1)S(1)} async-done(((bf16[8,8,1024]{2,1,0:T(8,128)(2,1)}), bf16[8,8,1024]{2,1,0:T(8,128)(2,1)S(1)}, u32[]{:S(2)}, u32[]{:S(2)}) %all-to-all-start.2) | async-done | bytes 131104 | tf_op jit(solution)/shard_map/all_to_all | solution.py:89
  33.0 0.6 broadcast_in_dim.15
  33.7 3.4 %all-to-all-start.1 = ((bf16[8,8,1024]{2,1,0:T(8,128)(2,1)}), bf16[8,8,1024]{2,1,0:T(8,128)(2,1)S(1)}, u32[]{:S(2)}, u32[]{:S(2)}) async-start(bf16[8,8,1024]{2,1,0:T(8,128)(2,1)} %bitcast.2), calls=%async_computation.1 | async-start | bytes 262144 | tf_op jit(solution)/shard_map/all_to_all | solution.py:90
  37.1 1.0 fusion.15
  38.1 1.0 fusion.12
  39.0 4.7 %all-to-all-done.1 = bf16[8,8,1024]{2,1,0:T(8,128)(2,1)S(1)} async-done(((bf16[8,8,1024]{2,1,0:T(8,128)(2,1)}), bf16[8,8,1024]{2,1,0:T(8,128)(2,1)S(1)}, u32[]{:S(2)}, u32[]{:S(2)}) %all-to-all-start.1) | async-done | bytes 131104 | tf_op jit(solution)/shard_map/all_to_all | solution.py:90
  43.8 1.1 fusion.17
  44.9 1.0 broadcast_select_fusion.1
  45.9 0.2 fusion.9
  46.2 16.4 %psum.30 = bf16[64,32]{0,1:T(8,128)(2,1)S(1)} all-reduce(f32[64,32]{0,1:T(8,128)S(1)} %bitcast.136), channel_id=1, replica_groups=mesh['dp'=4,'expert'=8] {'dp'}, use_global_device_ids=true, to_apply=%region_8.9 | all-reduce | flops 2048 | bytes 12288 | tf_op jit(solution)/shard_map/psum | solution.py:119
  62.6 26.3 %all-reduce.3.cloned.1.call-done = (f32[64,512]{1,0:T(8,128)}, f32[64,512]{1,0:T(8,128)}, f32[64,512]{1,0:T(8,128)}) async-done(((f32[64,512]{1,0:T(8,128)}, f32[64,512]{1,0:T(8,128)}, f32[64,512]{1,0:T(8,128)}), (f32[64,512]{1,0:T(8,128)}, f32[64,512]{1,0:T(8,128)}, f32[64,512]{1,0:T(8,128)})) %all-reduce.3.cloned.1.call-update) | async-done | bytes 393232 | tf_op jit(solution)/shard_map/psum | solution.py:119
  88.9 1.2 %multiply_convert_fusion = (bf16[64,512]{1,0:T(8,128)(2,1)S(1)}, f32[64,512]{1,0:T(8,128)S(1)}) fusion(f32[64,512]{1,0:T(8,128)} %get-tuple-element.7, f32[64]{0:T(128)S(1)} %mul.142, f32[64,512]{1,0:T(8,128)} %get-tuple-element.6, bf16[64,512]{1,0:T(8,128)(2,1)S(1)} %bitcast.134, bf16[64,2,64]{0,2,1:T(8,128)(2,1)S(1)} %fusion.30), kind=kOutput, calls=%fused_computation.41 | convolution fusion | flops 4489216 | bytes 541184 | tf_op jit(solution)/shard_map/dot_general | solution.py:124
  90.1 0.2 fusion.6
  90.4 0.4 fusion.10
  90.8 0.5 copy-done.3
  91.3 0.1 convolution_bitcast_fusion.2
  91.4 0.1 convolution_bitcast_fusion.1
  91.6 0.1 convolution_multiply_fusion
  91.7 0.1 convolution_multiply_fusion.1
  91.9 0.4 fusion
  92.4 0.2 copy_select_fusion
  92.6 0.6 collective-permute-start.2
  93.2 0.7 pad_maximum_fusion.1
  93.9 0.1 collective-permute-done.2
  94.0 0.1 copy.83
  94.2 0.2 mul.172
  94.4 0.2 add_convert_fusion
  94.7 0.7 copy.76
  95.3 4.6 %all-to-all-start.3 = ((bf16[8,4,1024]{2,1,0:T(4,128)(2,1)}), bf16[8,4,1024]{2,1,0:T(4,128)(2,1)S(1)}, u32[]{:S(2)}, u32[]{:S(2)}) async-start(bf16[8,4,1024]{2,1,0:T(4,128)(2,1)} %copy.76), calls=%async_computation.3 | async-start | bytes 131072 | tf_op jit(solution)/shard_map/all_to_all | solution.py:182
  99.9 0.9 convolution_bitcast_fusion
  100.8 5.0 %all-to-all-done.3 = bf16[8,4,1024]{2,1,0:T(4,128)(2,1)S(1)} async-done(((bf16[8,4,1024]{2,1,0:T(4,128)(2,1)}), bf16[8,4,1024]{2,1,0:T(4,128)(2,1)S(1)}, u32[]{:S(2)}, u32[]{:S(2)}) %all-to-all-start.3) | async-done | bytes 65568 | tf_op jit(solution)/shard_map/all_to_all | solution.py:182
  105.9 0.7 convolution_convert_fusion.2
  (49 shorter events, 1.1 us)
Async XLA Ops:
  7.2 30.9 %copy-start = (bf16[1,1024,512]{2,1,0:T(8,128)(2,1)S(1)}, bf16[1,1024,512]{2,1,0:T(8,128)(2,1)}, u32[]{:S(2)}) copy-start(bf16[1,1024,512]{2,1,0:T(8,128)(2,1)} %param.15) | copy-start | bytes 3145732
  7.2 0.8 copy-start.5
  7.2 29.9 %copy-start.1 = (bf16[1,1024,512]{2,1,0:T(8,128)(2,1)S(1)}, bf16[1,1024,512]{2,1,0:T(8,128)(2,1)}, u32[]{:S(2)}) copy-start(bf16[1,1024,512]{2,1,0:T(8,128)(2,1)} %param.16) | copy-start | bytes 3145732
  10.3 11.9 %all-to-all-start = ((bf16[8,8,4]{1,2,0:T(4,128)(2,1)}), bf16[8,8,4]{1,2,0:T(4,128)(2,1)S(1)}, u32[]{:S(2)}, u32[]{:S(2)}) async-start(bf16[8,8,4]{1,2,0:T(4,128)(2,1)} %bitcast), calls=%async_computation | async-start | bytes 16384 | tf_op jit(solution)/shard_map/all_to_all | solution.py:91
  16.7 28.2 %collective-permute-start = (bf16[1024,2,4,8]{0,3,2,1:T(8,128)(2,1)}, bf16[1024,2,4,8]{0,3,2,1:T(8,128)(2,1)}, u32[]{:S(2)}, u32[]{:S(2)}) collective-permute-start(bf16[1024,2,4,8]{0,3,2,1:T(8,128)(2,1)} %bitcast.12), channel_id=1, source_target_pairs={{0,1},{1,0},{2,3},{3,2},{4,5},{5,4},{6,7},{7,6},{8,9},{9,8},{10,11... | collective-permute-start | bytes 393224 | tf_op jit(solution)/shard_map/ppermute | solution.py:10
  22.9 10.1 %all-to-all-start.2 = ((bf16[8,8,1024]{2,1,0:T(8,128)(2,1)}), bf16[8,8,1024]{2,1,0:T(8,128)(2,1)S(1)}, u32[]{:S(2)}, u32[]{:S(2)}) async-start(bf16[8,8,1024]{2,1,0:T(8,128)(2,1)} %bitcast.6), calls=%async_computation.2 | async-start | bytes 262144 | tf_op jit(solution)/shard_map/all_to_all | solution.py:89
  33.7 10.1 %all-to-all-start.1 = ((bf16[8,8,1024]{2,1,0:T(8,128)(2,1)}), bf16[8,8,1024]{2,1,0:T(8,128)(2,1)S(1)}, u32[]{:S(2)}, u32[]{:S(2)}) async-start(bf16[8,8,1024]{2,1,0:T(8,128)(2,1)} %bitcast.2), calls=%async_computation.1 | async-start | bytes 262144 | tf_op jit(solution)/shard_map/all_to_all | solution.py:90
  37.1 6.7 %copy-start.2 = (bf16[1,512,1024]{2,1,0:T(8,128)(2,1)S(1)}, bf16[1,512,1024]{2,1,0:T(8,128)(2,1)}, u32[]{:S(2)}) copy-start(bf16[1,512,1024]{2,1,0:T(8,128)(2,1)} %param.17) | copy-start | bytes 3145732
  37.1 51.8 %all-reduce.3.cloned.1.call-start = ((), (), s32[]{:S(2)}) async-start(), calls=%async_computation.4 | async-start | bytes 786432 | tf_op jit(solution)/shard_map/psum | solution.py:119
  46.1 42.7 %copy-start.4 = (bf16[1,1,4,16,512]{4,3,2,1,0:T(8,128)(2,1)S(1)}, bf16[1,1,4,16,512]{4,3,2,1,0:T(8,128)(2,1)}, u32[]{:S(2)}) copy-start(bf16[1,1,4,16,512]{4,3,2,1,0:T(8,128)(2,1)} %get-tuple-element.12) | copy-start | bytes 196612
  88.9 1.2 %copy-start.6 = (f32[64,512]{1,0:T(8,128)S(1)}, f32[64,512]{1,0:T(8,128)}, u32[]{:S(2)}) copy-start(f32[64,512]{1,0:T(8,128)} %get-tuple-element.5) | copy-start | bytes 393220
  88.9 1.2 %copy-start.7 = (f32[64,512]{1,0:T(8,128)S(1)}, f32[64,512]{1,0:T(8,128)}, u32[]{:S(2)}) copy-start(f32[64,512]{1,0:T(8,128)} %get-tuple-element.7) | copy-start | bytes 393220
  90.4 0.9 copy-start.3
  92.5 1.9 %collective-permute-start.1 = (f32[8,4,1024]{2,0,1:T(8,128)S(1)}, f32[8,4,1024]{2,0,1:T(8,128)S(1)}, u32[]{:S(2)}, u32[]{:S(2)}) collective-permute-start(f32[8,4,1024]{2,0,1:T(8,128)S(1)} %copy_select_fusion), channel_id=1, source_target_pairs={{0,1},{1,0},{2,3},{3,2},{4,5},{5,4},{6,7},{7,6},{8,9},{9,8},{10,11... | collective-permute-start | bytes 393224 | tf_op jit(solution)/shard_map/ppermute | solution.py:10
  92.6 1.4 %collective-permute-start.2 = (f32[64,32]{0,1:T(8,128)S(1)}, f32[64,32]{0,1:T(8,128)S(1)}, u32[]{:S(2)}, u32[]{:S(2)}) collective-permute-start(f32[64,32]{0,1:T(8,128)S(1)} %bitcast.132), channel_id=1, source_target_pairs={{0,1},{1,0},{2,3},{3,2},{4,5},{5,4},{6,7},{7,6},{8,9},{9,8},{10,11... | collective-permute-start | bytes 24584 | tf_op jit(solution)/shard_map/ppermute | solution.py:10
  95.3 10.5 %all-to-all-start.3 = ((bf16[8,4,1024]{2,1,0:T(4,128)(2,1)}), bf16[8,4,1024]{2,1,0:T(4,128)(2,1)S(1)}, u32[]{:S(2)}, u32[]{:S(2)}) async-start(bf16[8,4,1024]{2,1,0:T(4,128)(2,1)} %copy.76), calls=%async_computation.3 | async-start | bytes 131072 | tf_op jit(solution)/shard_map/all_to_all | solution.py:182
Sparse Core Ops, SparseCore 0:
  45.0 43.8 all-reduce.2
where the time goes:
time: 114 us; the launch traced here: 113 us
  waiting for transfers between devices  44.1 us (39%)
  starting transfers between devices  18.8 us (16%)
  blocking collectives  16.4 us (14%)
  between operations  14.3 us (13%)
  matrix products  10.7 us (9%)
  local copies, waits for them, and re-layouts  5.89 us (5%)
  other arithmetic  3.16 us (3%)
    psum x1, waiting for transfers between devices, shards(): lax.psum((gate_part, up_part, act_part, proj_part), 'dp')  26.3 us
    psum x1, blocking collectives, shards(): lax.psum((gate_part, up_part, act_part, proj_part), 'dp')  16.4 us
    all_to_all x1, starting transfers between devices, shards(): lax.all_to_all(doubled(send_tag), 'expert', split_axis=0, concat_axis=0,...  6.33 us
    all_to_all x1, waiting for transfers between devices, shards(): lax.all_to_all(doubled(send_rows), 'expert', split_axis=0, concat_axis=0,...  6.2 us
    all_to_all x1, waiting for transfers between devices, shards(): lax.all_to_all(slot_grad, 'expert', split_axis=0, concat_axis=0, tiled=True)  5.05 us
    all_to_all x1, waiting for transfers between devices, shards(): lax.all_to_all(doubled(send_grad), 'expert', split_axis=0, concat_axis=0,...  4.73 us
    all_to_all x1, starting transfers between devices, shards(): lax.all_to_all(slot_grad, 'expert', split_axis=0, concat_axis=0, tiled=True)  4.6 us
    all_to_all x1, starting transfers between devices, shards(): lax.all_to_all(doubled(send_rows), 'expert', split_axis=0, concat_axis=0,...  3.37 us
  transfers between devices with their start and end apart: 8, of which 6 were waited for; matrix products, arithmetic and copies ran while one was open for 10% of the time, Pallas kernels for 0%

commit v1 on v0

--- a/solution.py
+++ b/solution.py
@@ -1,6 +1,10 @@
+import functools
+
 import jax
 import jax.numpy as jnp
 from jax import lax
+from jax.experimental import pallas as pl
+from jax.experimental.pallas import tpu as pltpu
 from jax.sharding import PartitionSpec as P
 
 ADAPTER_SCALE = 2.0
@@ -34,7 +38,7 @@
     return wide.reshape(count, 2, tenant_list * adapter_rank_width).astype(jnp.bfloat16)
 
 
-def shards(
+def routed_shards(
     tokens,
     output_gradient,
     routes,
@@ -185,6 +189,314 @@
     return (input_grad, adapter_a_grad, adapter_b_grad)
 
 
+F32 = jnp.float32
+BF16 = jnp.bfloat16
+VMEM = pl.BlockSpec(memory_space=pltpu.VMEM)
+
+
+def local_call(body, outs, operands, scratch=(), flops=0, moved=0):
+    return pl.pallas_call(
+        body,
+        out_shape=[jax.ShapeDtypeStruct(shape, kind) for shape, kind in outs],
+        in_specs=[VMEM] * len(operands),
+        out_specs=[VMEM] * len(outs),
+        scratch_shapes=list(scratch),
+        cost_estimate=pl.CostEstimate(flops=flops, bytes_accessed=moved, transcendentals=0),
+    )(*operands)
+
+
+def dot_plain(left, right):
+    return lax.dot_general(left, right, (((1,), (0,)), ((), ())), preferred_element_type=F32)
+
+
+def swap(array, axis, offset):
+    return lax.ppermute(array, axis, [(i, i ^ offset) for i in range(lax.axis_size(axis))])
+
+
+def pack_body(x_ref, dy_ref, routes_ref, weight_ref, tenant_ref, out_ref):
+    width = x_ref.shape[1]
+    topk, count = routes_ref.shape
+    out_ref[:, :width] = x_ref[...]
+    out_ref[:, width : 2 * width] = dy_ref[...]
+    tags = [routes_ref[...].astype(F32), weight_ref[...].astype(F32), tenant_ref[...].astype(F32)]
+    rows = 2 * topk + 1
+    tags = jnp.concatenate(tags + [jnp.zeros((count - rows, count), F32)], axis=0)
+    tags = jnp.concatenate([tags, jnp.zeros((count, 128 - count), F32)], axis=1)
+    out_ref[:, 2 * width :] = tags.astype(BF16)
+
+
+def forward_body(topk, *refs):
+    blocks = [ref[...].astype(F32) for ref in refs[:-12]]
+    gate_ref, up_ref, down_ref, mine_ref, other_ref = refs[-12:-7]
+    own_ref, first_ref, second_ref, third_ref, x_ref, tag_ref, total = refs[-7:]
+    width = gate_ref.shape[0]
+    hidden = gate_ref.shape[1]
+    count = blocks[0].shape[0]
+    slots = count * len(blocks)
+    me = lax.axis_index("dp")
+    upper = lax.rem(lax.axis_index("expert"), 2)
+    expert = (lax.axis_index("expert") // 2).astype(F32)
+    x = jnp.concatenate([block[:, :width] for block in blocks], axis=0).astype(BF16)
+    dy = jnp.concatenate([block[:, width : 2 * width] for block in blocks], axis=0).astype(BF16)
+    x_ref[...] = x
+    total[:, :hidden] = dot_plain(x, gate_ref[...])
+    total[:, hidden : 2 * hidden] = dot_plain(x, up_ref[...])
+    total[:, 2 * hidden : 3 * hidden] = product_trailing(dy, down_ref[...])
+    mine = product_trailing(x, mine_ref[...])
+    other = product_trailing(x, other_ref[...])
+    low = jnp.where(upper == 1, other, mine)
+    high = jnp.where(upper == 1, mine, other)
+    total[:, 3 * hidden :] = jnp.concatenate([low, high], axis=1)
+    eye = (
+        lax.broadcasted_iota(jnp.int32, (count, 128), 0)
+        == lax.broadcasted_iota(jnp.int32, (count, 128), 1)
+    ).astype(BF16)
+    tags = jnp.concatenate(
+        [product_leading(block[:, 2 * width :].astype(BF16), eye)[:count] for block in blocks],
+        axis=0,
+    )
+    prob = jnp.zeros((slots, 1), F32)
+    for k in range(topk):
+        prob += jnp.where(tags[:, k : k + 1] == expert, tags[:, topk + k : topk + k + 1], 0.0)
+    lane = lax.broadcasted_iota(jnp.int32, (slots, 128), 1)
+    tenant = tags[:, 2 * topk : 2 * topk + 1]
+    tag_ref[...] = jnp.where(lane == 0, prob, jnp.where(lane == 1, tenant, 0.0))
+    part = slots // 4
+    for k, ref in enumerate((own_ref, first_ref, second_ref, third_ref)):
+        start = pl.multiple_of((me ^ k) * part, part)
+        ref[...] = total[pl.ds(start, part), :].astype(ref.dtype)
+
+
+def lane_masks(tenant, shape, ranks):
+    lane = lax.broadcasted_iota(jnp.int32, shape, 1)
+    half = shape[1] // 2
+    inner = lax.rem(lane, half)
+    is_gate = inner < half // 2
+    tenant_of = lax.rem(inner, half // 2) // ranks
+    return is_gate, tenant_of.astype(F32) == tenant
+
+
+def activation_body(ranks, own_ref, first_ref, second_ref, third_ref, tag_ref, maps_ref, out_ref):
+    hidden = maps_ref.shape[1]
+    part = own_ref.shape[0]
+    me = lax.axis_index("dp")
+    total = (own_ref[...] + first_ref[...].astype(F32)) + (
+        second_ref[...].astype(F32) + third_ref[...].astype(F32)
+    )
+    tags = tag_ref[pl.ds(pl.multiple_of(me * part, part), part), :]
+    prob = tags[:, :1]
+    tenant = tags[:, 1:2]
+    low = total[:, 3 * hidden :]
+    is_gate, keep = lane_masks(tenant, low.shape, ranks)
+    low = jnp.where(keep, low, 0.0).astype(BF16)
+    low_wide = low.astype(F32)
+    maps = maps_ref[...]
+    gate = total[:, :hidden] + ADAPTER_SCALE * dot_plain(
+        jnp.where(is_gate, low_wide, 0.0).astype(BF16), maps
+    )
+    up = total[:, hidden : 2 * hidden] + ADAPTER_SCALE * dot_plain(
+        jnp.where(is_gate, 0.0, low_wide).astype(BF16), maps
+    )
+    act = prob * total[:, 2 * hidden : 3 * hidden]
+    sig = jax.nn.sigmoid(gate)
+    out_ref[:, :hidden] = (act * up * sig * (1.0 + gate * (1.0 - sig))).astype(BF16)
+    out_ref[:, hidden : 2 * hidden] = (act * gate * sig).astype(BF16)
+    out_ref[:, 2 * hidden :] = low
+
+
+def backward_body(
+    ranks,
+    own_ref,
+    first_ref,
+    second_ref,
+    third_ref,
+    gate_ref,
+    up_ref,
+    mine_ref,
+    other_ref,
+    maps_ref,
+    tag_ref,
+    keep_ref,
+    give_ref,
+    back_keep_ref,
+    back_give_ref,
+    rows_ref,
+):
+    part = own_ref.shape[0]
+    slots = 4 * part
+    hidden = gate_ref.shape[1]
+    me = lax.axis_index("dp")
+    upper = lax.rem(lax.axis_index("expert"), 2)
+    for k, ref in enumerate((own_ref, first_ref, second_ref, third_ref)):
+        rows_ref[pl.ds(pl.multiple_of((me ^ k) * part, part), part), :] = ref[...]
+    gate_grad = rows_ref[:, :hidden]
+    up_grad = rows_ref[:, hidden : 2 * hidden]
+    maps = maps_ref[...]
+    back_gate = product_trailing(gate_grad, maps)
+    back_up = product_trailing(up_grad, maps)
+    is_gate, keep = lane_masks(tag_ref[:, 1:2], back_gate.shape, ranks)
+    back = ADAPTER_SCALE * jnp.where(keep, jnp.where(is_gate, back_gate, back_up), 0.0)
+    half = back.shape[1] // 2
+    low, high = back[:, :half], back[:, half:]
+    mine = jnp.where(upper == 1, high, low)
+    other = jnp.where(upper == 1, low, high)
+    back_keep_ref[...] = mine
+    back_give_ref[...] = other
+    total = product_trailing(gate_grad, gate_ref[...])
+    total += product_trailing(up_grad, up_ref[...])
+    total += dot_plain(mine.astype(BF16), mine_ref[...])
+    total += dot_plain(other.astype(BF16), other_ref[...])
+    keep_ref[...] = total[: slots // 2]
+    give_ref[...] = total[slots // 2 :].astype(BF16)
+
+
+def join_body(keep_ref, taken_ref, own_ref, first_ref, second_ref, third_ref):
+    count = own_ref.shape[0]
+    total = keep_ref[...] + taken_ref[...].astype(F32)
+    for k, ref in enumerate((own_ref, first_ref, second_ref, third_ref)):
+        ref[...] = total[k * count : (k + 1) * count].astype(ref.dtype)
+
+
+def finish_body(own_ref, first_ref, second_ref, third_ref, out_ref):
+    total = (own_ref[...] + first_ref[...].astype(F32)) + (
+        second_ref[...].astype(F32) + third_ref[...].astype(F32)
+    )
+    out_ref[...] = total.astype(BF16)
+
+
+def maps_grad_body(rows_ref, out_ref):
+    hidden = out_ref.shape[1]
+    lanes = out_ref.shape[0]
+    half = lanes // 2
+    row = lax.broadcasted_iota(jnp.int32, (lanes, lanes), 0)
+    col = lax.broadcasted_iota(jnp.int32, (lanes, lanes), 1)
+    low = rows_ref[:, 2 * hidden :]
+    source = lax.rem(col // 8, 2) * half + (col // 16) * 8 + lax.rem(col, 8)
+    order = (row == source).astype(BF16)
+    low = dot_plain(low, order).astype(BF16)
+    out_ref[:half] = ADAPTER_SCALE * product_leading(low[:, :half], rows_ref[:, :hidden])
+    out_ref[half:] = ADAPTER_SCALE * product_leading(
+        low[:, half:], rows_ref[:, hidden : 2 * hidden]
+    )
+
+
+def input_maps_grad_body(keep_ref, taken_ref, x_ref, out_ref):
+    half = keep_ref.shape[0] // 2
+    taken = jnp.concatenate([taken_ref[half:], taken_ref[:half]], axis=0)
+    back = (keep_ref[...] + taken).astype(BF16)
+    out_ref[...] = product_leading(back, x_ref[...])
+
+
+def dense_shards(
+    tokens,
+    output_gradient,
+    routes,
+    router_expert_weight,
+    tenant,
+    gate_weight,
+    up_weight,
+    down_weight,
+    adapter_input_maps,
+    adapter_output_maps,
+):
+    devices = lax.axis_size("expert")
+    chips = devices // 2
+    count, width = tokens.shape
+    topk = routes.shape[1]
+    tenants, rank, hidden = adapter_output_maps.shape[2:]
+    ranks = rank // 2
+    lanes = 2 * tenants * rank
+    slots = devices * count
+    part = slots // 4
+    mine_cols = adapter_input_maps[0].transpose(1, 2, 3, 0).reshape(lanes // 2, width)
+    maps = (
+        adapter_output_maps[0]
+        .reshape(2, tenants, 2, ranks, hidden)
+        .transpose(2, 0, 1, 3, 4)
+        .reshape(lanes, hidden)
+    )
+    other_cols = swap(mine_cols, "expert", 1)
+    (packed,) = local_call(
+        pack_body,
+        [((count, 2 * width + 128), BF16)],
+        (tokens, output_gradient, routes.T, router_expert_weight.T, tenant[None, :]),
+    )
+    same_core = [packed] + [swap(packed, "expert", 2 * k) for k in range(1, chips)]
+    other_core = [swap(block, "expert", 1) for block in same_core]
+    gate, up, down = gate_weight[0], up_weight[0], down_weight[0]
+    columns = 3 * hidden + lanes
+    own, first, second, third, x, tags = local_call(
+        functools.partial(forward_body, topk),
+        [
+            ((part, columns), F32),
+            ((part, columns), BF16),
+            ((part, columns), BF16),
+            ((part, columns), BF16),
+            ((slots, width), BF16),
+            ((slots, 128), F32),
+        ],
+        (*same_core, *other_core, gate, up, down, mine_cols, other_cols),
+        scratch=[pltpu.VMEM((slots, columns), F32)],
+        flops=2 * slots * width * columns,
+        moved=4 * width * columns,
+    )
+    sums = [own] + [swap(block, "dp", k + 1) for k, block in enumerate((first, second, third))]
+    (gradients,) = local_call(
+        functools.partial(activation_body, ranks),
+        [((part, 2 * hidden + lanes), BF16)],
+        (*sums, tags, maps),
+    )
+    gathered = [gradients] + [swap(gradients, "dp", k) for k in (1, 2, 3)]
+    keep, give, back_keep, back_give, rows = local_call(
+        functools.partial(backward_body, ranks),
+        [
+            ((slots // 2, width), F32),
+            ((slots // 2, width), BF16),
+            ((slots, lanes // 2), F32),
+            ((slots, lanes // 2), F32),
+            ((slots, 2 * hidden + lanes), BF16),
+        ],
+        (*gathered, gate, up, mine_cols, other_cols, maps, tags),
+        flops=4 * slots * width * hidden,
+        moved=4 * width * hidden,
+    )
+    taken = swap(give, "expert", 1)
+    back_taken = swap(back_give, "expert", 1)
+    own, first, second, third = local_call(
+        join_body,
+        [((count, width), F32)] + [((count, width), BF16)] * 3,
+        (keep, taken),
+    )
+    returned = [own] + [
+        swap(block, "expert", 2 * (k + 1)) for k, block in enumerate((first, second, third))
+    ]
+    (maps_grad,) = local_call(maps_grad_body, [((lanes, hidden), F32)], (rows,))
+    (input_maps_grad,) = local_call(
+        input_maps_grad_body, [((lanes // 2, width), F32)], (back_keep, back_taken, x)
+    )
+    (input_grad,) = local_call(finish_body, [((count, width), BF16)], returned)
+    adapter_a_grad = (
+        input_maps_grad.reshape(2, tenants, ranks, width).transpose(3, 0, 1, 2)[None]
+    )
+    adapter_b_grad = maps_grad.reshape(1, 2, tenants, rank, hidden)
+    return input_grad, adapter_a_grad, adapter_b_grad
+
+
+def shards(*arrays):
+    tokens, routes, maps = arrays[0], arrays[2], arrays[9]
+    devices = lax.axis_size("expert")
+    capacity = 4 * tokens.shape[0] * routes.shape[1] // devices
+    if (
+        capacity >= tokens.shape[0]
+        and devices == 8
+        and lax.axis_size("dp") == 4
+        and tokens.shape[0] == 8
+        and maps.shape[2] * maps.shape[3] == 64
+    ):
+        return dense_shards(*arrays)
+    return routed_shards(*arrays)
+
+
 def solution(mesh):
     placed = (
         P("expert", "dp"),

time: 114 us -> 53.9 us (0.47)
  waiting for transfers between devices: 44.1 us -> 13.1 us
  Pallas kernels: 0 us -> 17.2 us
  blocking collectives: 16.4 us -> 0 us
  between operations: 14.3 us -> 0.76 us
  matrix products: 10.7 us -> 0 us
  other arithmetic: 3.16 us -> 0 us
  local copies, waits for them, and re-layouts: 5.89 us -> 4.35 us
    psum x1 -> x0, waiting for transfers between devices: 26.3 us -> none  [shards(): lax.psum((gate_part, up_part, act_part, proj_part), 'dp')]
    all_to_all x4 -> x0, waiting for transfers between devices: 17.7 us -> none  [the longest x1 6.2 us: shards(): lax.all_to_all(doubled(send_rows), 'expert', split_axis=0, concat_axis=0,...]
    all_to_all x4 -> x0, starting transfers between devices: 17.7 us -> none  [the longest x1 6.33 us: shards(): lax.all_to_all(doubled(send_tag), 'expert', split_axis=0, concat_axis=0,...]
    pallas_call x0 -> x8, Pallas kernels: none -> 17.2 us  [local_call(): pl.pallas_call(body, out_shape=[jax.ShapeDtypeStruct(shape, kind) for sha...]
    ppermute x3 -> x19, starting transfers between devices: 1.13 us -> 18.1 us  [swap(): lax.ppermute(array, axis, [(i, i ^ offset) for i in range(lax.axis_size(a...]
    psum x1 -> x0, blocking collectives: 16.4 us -> none  [shards(): lax.psum((gate_part, up_part, act_part, proj_part), 'dp')]
    ppermute x3 -> x19, waiting for transfers between devices: 0.12 us -> 13.1 us  [swap(): lax.ppermute(array, axis, [(i, i ^ offset) for i in range(lax.axis_size(a...]
    dot_general x18 -> x0, matrix products: 10.7 us -> none  [the longest x6 2.45 us: product_trailing(): lax.dot_general(left, right, (((1,), (1,)), ((), ())), preferred_element_...]
  transfers between devices with their start and end apart: 8 -> 19, of which waited for: 6 -> 10; matrix products, arithmetic and copies ran while one was open for 10% -> 1% of each run, Pallas kernels for 0% -> 13%
where the time goes in v1:
time: 53.9 us; the launch traced here: 53.5 us
  starting transfers between devices  18.1 us (34%)
  Pallas kernels  17.2 us (32%)
  waiting for transfers between devices  13.1 us (24%)
  local copies, waits for them, and re-layouts  4.35 us (8%)
  between operations  0.76 us (1%)
    ppermute x19, starting transfers between devices, swap(): lax.ppermute(array, axis, [(i, i ^ offset) for i in range(lax.axis_size(a...  18.1 us
    pallas_call x8, Pallas kernels, local_call(): pl.pallas_call(body, out_shape=[jax.ShapeDtypeStruct(shape, kind) for sha...  17.2 us
    ppermute x19, waiting for transfers between devices, swap(): lax.ppermute(array, axis, [(i, i ^ offset) for i in range(lax.axis_size(a...  13.1 us
    unnamed x40, local copies, waits for them, and re-layouts  3.7 us
  transfers between devices with their start and end apart: 19, of which 10 were waited for; matrix products, arithmetic and copies ran while one was open for 1% of the time, Pallas kernels for 13%

profile of v1, /device:TPU:0, one launch (start us, length us, event | category | flops | bytes accessed | tf_op | source)
XLA Modules:
  0.0 53.5 jit_solution(14500758570124427669)
XLA Ops:
  0.6 0.5 collective-permute-start.7
  1.1 1.4 %shard_map.121.refs_0_ = bf16[8,2176]{1,0:T(8,128)(2,1)} custom-call(bf16[8,1024]{1,0:T(8,128)(2,1)} %x_ref.1, bf16[8,1024]{1,0:T(8,128)(2,1)} %dy_ref.1, s32[2,8]{1,0:T(2,128)} %bitcast.34, bf16[2,8]{1,0:T(2,128)(2,1)} %bitcast.35, s32[1,8]{1,0:T(1,128)} %bitcast.36), custom_call_target="tpu_custom_call" | custom-call | tf_op jit(solution)/shard_map/pallas_call | solution.py:198
  2.5 4.6 %collective-permute-start.2 = (bf16[8,2176]{1,0:T(8,128)(2,1)}, bf16[8,2176]{1,0:T(8,128)(2,1)S(1)}, u32[]{:S(2)}, u32[]{:S(2)}) collective-permute-start(bf16[8,2176]{1,0:T(8,128)(2,1)} %shard_map.121.refs_0_), channel_id=1, source_target_pairs={{0,6},{1,7},{2,4},{3,5},{4,2},{5,3},{6,0},{7,1},{8,14},{9,15},{10,... | collective-permute-start | bytes 104456 | tf_op jit(solution)/shard_map/ppermute | solution.py:213
  7.1 0.0 collective-permute-start.1
  7.1 0.6 %collective-permute-start = (bf16[8,2176]{1,0:T(8,128)(2,1)}, bf16[8,2176]{1,0:T(8,128)(2,1)S(1)}, u32[]{:S(2)}, u32[]{:S(2)}) collective-permute-start(bf16[8,2176]{1,0:T(8,128)(2,1)} %shard_map.121.refs_0_), channel_id=1, source_target_pairs={{0,2},{1,3},{2,0},{3,1},{4,6},{5,7},{6,4},{7,5},{8,10},{9,11},{10,... | collective-permute-start | bytes 104456 | tf_op jit(solution)/shard_map/ppermute | solution.py:213
  7.7 1.7 %collective-permute-done.2.refs_3_ = bf16[8,2176]{1,0:T(8,128)(2,1)S(1)} collective-permute-done((bf16[8,2176]{1,0:T(8,128)(2,1)}, bf16[8,2176]{1,0:T(8,128)(2,1)S(1)}, u32[]{:S(2)}, u32[]{:S(2)}) %collective-permute-start.2) | collective-permute-done | bytes 34848 | tf_op jit(solution)/shard_map/ppermute | solution.py:213
  9.4 0.0 collective-permute-start.6
  9.5 2.7 %collective-permute-done.1.refs_2_ = bf16[8,2176]{1,0:T(8,128)(2,1)S(1)} collective-permute-done((bf16[8,2176]{1,0:T(8,128)(2,1)}, bf16[8,2176]{1,0:T(8,128)(2,1)S(1)}, u32[]{:S(2)}, u32[]{:S(2)}) %collective-permute-start.1) | collective-permute-done | bytes 34848 | tf_op jit(solution)/shard_map/ppermute | solution.py:213
  12.2 0.0 collective-permute-start.5
  12.2 0.0 collective-permute-done.refs_1_
  12.2 0.5 collective-permute-start.4
  12.7 0.7 %collective-permute-done.5.refs_6_ = bf16[8,2176]{1,0:T(8,128)(2,1)S(1)} collective-permute-done((bf16[8,2176]{1,0:T(8,128)(2,1)S(1)}, bf16[8,2176]{1,0:T(8,128)(2,1)S(1)}, u32[]{:S(2)}, u32[]{:S(2)}) %collective-permute-start.5) | collective-permute-done | bytes 34848 | tf_op jit(solution)/shard_map/ppermute | solution.py:213
  13.4 0.2 collective-permute-done.4.refs_5_
  13.6 0.4 copy-done.14
  14.0 0.2 copy-done.15
  14.2 0.1 copy-done
  14.2 3.9 %shard_map.122 = (f32[16,1664]{1,0:T(8,128)}, bf16[16,1664]{1,0:T(8,128)(2,1)}, bf16[16,1664]{1,0:T(8,128)(2,1)}, bf16[16,1664]{1,0:T(8,128)(2,1)}, bf16[64,1024]{1,0:T(8,128)(2,1)}, /*index=5*/f32[64,128]{1,0:T(8,128)}) custom-call(bf16[8,2176]{1,0:T(8,128)(2,1)} %shard_map.121.refs_0_, bf16[8,2176]{1,0:T(8,128)(2,1)} %copy-done.11, ...), custom_call_target="tpu_custom_call" | custom-call | flops 218103808 | bytes 6815744 | tf_op jit(solution)/shard_map/pallas_call | solution.py:198
  18.1 1.5 %collective-permute-start.8 = (bf16[16,1664]{1,0:T(8,128)(2,1)}, bf16[16,1664]{1,0:T(8,128)(2,1)S(1)}, u32[]{:S(2)}, u32[]{:S(2)}) collective-permute-start(bf16[16,1664]{1,0:T(8,128)(2,1)} %get-tuple-element.19), channel_id=1, source_target_pairs={{0,8},{8,0},{16,24},{24,16},{1,9},{9,1},{17,25},{25,17},{2,10},{10... | collective-permute-start | bytes 159752 | tf_op jit(solution)/shard_map/ppermute | solution.py:213
  19.7 1.5 %collective-permute-start.9 = (bf16[16,1664]{1,0:T(8,128)(2,1)}, bf16[16,1664]{1,0:T(8,128)(2,1)S(1)}, u32[]{:S(2)}, u32[]{:S(2)}) collective-permute-start(bf16[16,1664]{1,0:T(8,128)(2,1)} %get-tuple-element.20), channel_id=1, source_target_pairs={{0,16},{8,24},{16,0},{24,8},{1,17},{9,25},{17,1},{25,9},{2,18},{10... | collective-permute-start | bytes 159752 | tf_op jit(solution)/shard_map/ppermute | solution.py:213
  21.2 0.5 collective-permute-start.10
  21.7 0.7 %copy.13 = bf16[2,4,2,8,512]{4,3,1,0,2:T(8,128)(2,1)} copy(bf16[2,4,2,8,512]{4,3,2,1,0:T(8,128)(2,1)S(1)} %bitcast.33) | data formatting | bytes 262144 | tf_op jit(solution)/shard_map/reshape;squeeze | solution.py:414
  22.3 0.2 collective-permute-done.8.first_ref
  22.5 1.5 %collective-permute-done.9.second_ref = bf16[16,1664]{1,0:T(8,128)(2,1)S(1)} collective-permute-done((bf16[16,1664]{1,0:T(8,128)(2,1)}, bf16[16,1664]{1,0:T(8,128)(2,1)S(1)}, u32[]{:S(2)}, u32[]{:S(2)}) %collective-permute-start.9) | collective-permute-done | bytes 53280 | tf_op jit(solution)/shard_map/ppermute | solution.py:213
  24.0 2.4 %collective-permute-done.10.third_ref = bf16[16,1664]{1,0:T(8,128)(2,1)S(1)} collective-permute-done((bf16[16,1664]{1,0:T(8,128)(2,1)}, bf16[16,1664]{1,0:T(8,128)(2,1)S(1)}, u32[]{:S(2)}, u32[]{:S(2)}) %collective-permute-start.10) | collective-permute-done | bytes 53280 | tf_op jit(solution)/shard_map/ppermute | solution.py:213
  26.4 0.6 %copy-done.5 = bf16[16,1664]{1,0:T(8,128)(2,1)} copy-done((bf16[16,1664]{1,0:T(8,128)(2,1)}, bf16[16,1664]{1,0:T(8,128)(2,1)S(1)}, u32[]{:S(2)}) %copy-start.5) | copy-done | bytes 53272
  27.1 1.9 %shard_map.123.own_ref = bf16[16,1152]{1,0:T(8,128)(2,1)} custom-call(f32[16,1664]{1,0:T(8,128)} %get-tuple-element.18.own_ref, bf16[16,1664]{1,0:T(8,128)(2,1)} %copy-done.3, bf16[16,1664]{1,0:T(8,128)(2,1)} %copy-done.4, bf16[16,1664]{1,0:T(8,128)(2,1)} %copy-done.5, f32[64,128]{1,0:T(8,128)} %get-tuple-element.22.tag_ref, bf16[128,512]{1,0:T(8,128)(2,1)} %bitcast.25), custom_call_target="tpu_custom_call" | custom-call | tf_op jit(solution)/shard_map/pallas_call | solution.py:198
  28.9 0.5 collective-permute-start.13
  29.4 1.5 %collective-permute-start.12 = (bf16[16,1152]{1,0:T(8,128)(2,1)}, bf16[16,1152]{1,0:T(8,128)(2,1)S(1)}, u32[]{:S(2)}, u32[]{:S(2)}) collective-permute-start(bf16[16,1152]{1,0:T(8,128)(2,1)} %shard_map.123.own_ref), channel_id=1, source_target_pairs={{0,16},{8,24},{16,0},{24,8},{1,17},{9,25},{17,1},{25,9},{2,18},{10... | collective-permute-start | bytes 110600 | tf_op jit(solution)/shard_map/ppermute | solution.py:213
  30.9 1.5 %collective-permute-start.11 = (bf16[16,1152]{1,0:T(8,128)(2,1)}, bf16[16,1152]{1,0:T(8,128)(2,1)S(1)}, u32[]{:S(2)}, u32[]{:S(2)}) collective-permute-start(bf16[16,1152]{1,0:T(8,128)(2,1)} %shard_map.123.own_ref), channel_id=1, source_target_pairs={{0,8},{8,0},{16,24},{24,16},{1,9},{9,1},{17,25},{25,17},{2,10},{10... | collective-permute-start | bytes 110600 | tf_op jit(solution)/shard_map/ppermute | solution.py:213
  32.4 1.6 %collective-permute-done.13.third_ref = bf16[16,1152]{1,0:T(8,128)(2,1)S(1)} collective-permute-done((bf16[16,1152]{1,0:T(8,128)(2,1)}, bf16[16,1152]{1,0:T(8,128)(2,1)S(1)}, u32[]{:S(2)}, u32[]{:S(2)}) %collective-permute-start.13) | collective-permute-done | bytes 36896 | tf_op jit(solution)/shard_map/ppermute | solution.py:213
  34.0 1.1 %collective-permute-done.11.first_ref = bf16[16,1152]{1,0:T(8,128)(2,1)S(1)} collective-permute-done((bf16[16,1152]{1,0:T(8,128)(2,1)}, bf16[16,1152]{1,0:T(8,128)(2,1)S(1)}, u32[]{:S(2)}, u32[]{:S(2)}) %collective-permute-start.11) | collective-permute-done | bytes 36896 | tf_op jit(solution)/shard_map/ppermute | solution.py:213
  35.1 0.6 %copy-done.8 = bf16[16,1152]{1,0:T(8,128)(2,1)} copy-done((bf16[16,1152]{1,0:T(8,128)(2,1)}, bf16[16,1152]{1,0:T(8,128)(2,1)S(1)}, u32[]{:S(2)}) %copy-start.8) | copy-done | bytes 36888
  35.7 3.3 %shard_map.124 = (f32[32,1024]{1,0:T(8,128)}, bf16[32,1024]{1,0:T(8,128)(2,1)}, f32[64,64]{1,0:T(8,128)}, f32[64,64]{1,0:T(8,128)}, bf16[64,1152]{1,0:T(8,128)(2,1)}) custom-call(bf16[16,1152]{1,0:T(8,128)(2,1)} %shard_map.123.own_ref, bf16[16,1152]{1,0:T(8,128)(2,1)} %copy-done.8, bf16[16,1152]{1,0:T(8,128)(2,1)} %copy-done.7, bf16[16,1152]{1,0:T(8,128)(2,1)} %copy-done.6, ...), custom_call_target="tpu_custom_call" | custom-call | flops 134217728 | bytes 2097152 | tf_op jit(solution)/shard_map/pallas_call | solution.py:198
  39.0 0.0 collective-permute-start.14
  39.0 0.5 collective-permute-start.18
  39.5 1.0 %collective-permute-done.14.taken_ref = bf16[32,1024]{1,0:T(8,128)(2,1)S(1)} collective-permute-done((bf16[32,1024]{1,0:T(8,128)(2,1)}, bf16[32,1024]{1,0:T(8,128)(2,1)S(1)}, u32[]{:S(2)}, u32[]{:S(2)}) %collective-permute-start.14) | collective-permute-done | bytes 65568 | tf_op jit(solution)/shard_map/ppermute | solution.py:213
  40.5 0.6 %copy-done.2 = bf16[32,1024]{1,0:T(8,128)(2,1)} copy-done((bf16[32,1024]{1,0:T(8,128)(2,1)}, bf16[32,1024]{1,0:T(8,128)(2,1)S(1)}, u32[]{:S(2)}) %copy-start.2) | copy-done | bytes 65560
  41.1 1.5 %shard_map.125 = (f32[8,1024]{1,0:T(8,128)}, bf16[8,1024]{1,0:T(8,128)(2,1)}, bf16[8,1024]{1,0:T(8,128)(2,1)}, bf16[8,1024]{1,0:T(8,128)(2,1)}) custom-call(f32[32,1024]{1,0:T(8,128)} %get-tuple-element.23.keep_ref, bf16[32,1024]{1,0:T(8,128)(2,1)} %copy-done.2), custom_call_target="tpu_custom_call" | custom-call | tf_op jit(solution)/shard_map/pallas_call | solution.py:198
  42.6 0.4 collective-permute-start.15
  43.0 1.8 %collective-permute-start.16 = (bf16[8,1024]{1,0:T(8,128)(2,1)}, bf16[8,1024]{1,0:T(8,128)(2,1)S(1)}, u32[]{:S(2)}, u32[]{:S(2)}) collective-permute-start(bf16[8,1024]{1,0:T(8,128)(2,1)} %get-tuple-element.27), channel_id=1, source_target_pairs={{0,4},{1,5},{2,6},{3,7},{4,0},{5,1},{6,2},{7,3},{8,12},{9,13},{10,... | collective-permute-start | bytes 49160 | tf_op jit(solution)/shard_map/ppermute | solution.py:213
  44.8 2.2 %collective-permute-start.17 = (bf16[8,1024]{1,0:T(8,128)(2,1)}, bf16[8,1024]{1,0:T(8,128)(2,1)S(1)}, u32[]{:S(2)}, u32[]{:S(2)}) collective-permute-start(bf16[8,1024]{1,0:T(8,128)(2,1)} %get-tuple-element.28), channel_id=1, source_target_pairs={{0,6},{1,7},{2,4},{3,5},{4,2},{5,3},{6,0},{7,1},{8,14},{9,15},{10,... | collective-permute-start | bytes 49160 | tf_op jit(solution)/shard_map/ppermute | solution.py:213
  47.0 2.0 %shard_map.128 = f32[128,512]{1,0:T(8,128)} custom-call(bf16[64,1152]{1,0:T(8,128)(2,1)} %get-tuple-element.32.rows_ref), custom_call_target="tpu_custom_call" | custom-call | tf_op jit(solution)/shard_map/pallas_call | solution.py:198
  49.0 0.6 %copy-done.16 = f32[64,64]{1,0:T(8,128)} copy-done((f32[64,64]{1,0:T(8,128)}, f32[64,64]{1,0:T(8,128)S(1)}, u32[]{:S(2)}) %copy-start.16) | copy-done | bytes 16408
  49.6 1.9 %shard_map.127 = f32[64,1024]{1,0:T(8,128)} custom-call(f32[64,64]{1,0:T(8,128)} %get-tuple-element.29.keep_ref, f32[64,64]{1,0:T(8,128)} %copy-done.16, bf16[64,1024]{1,0:T(8,128)(2,1)} %get-tuple-element.31.x_ref), custom_call_target="tpu_custom_call" | custom-call | tf_op jit(solution)/shard_map/pallas_call | solution.py:198
  51.5 0.6 %copy-done.17 = bf16[8,1024]{1,0:T(8,128)(2,1)} copy-done((bf16[8,1024]{1,0:T(8,128)(2,1)}, bf16[8,1024]{1,0:T(8,128)(2,1)S(1)}, u32[]{:S(2)}) %copy-start.17) | copy-done | bytes 16408
  52.1 0.0 copy-done.18
  52.1 0.0 copy-done.19
  52.1 1.4 %shard_map.126 = bf16[8,1024]{1,0:T(8,128)(2,1)} custom-call(f32[8,1024]{1,0:T(8,128)} %get-tuple-element.25.own_ref, bf16[8,1024]{1,0:T(8,128)(2,1)} %copy-done.17, bf16[8,1024]{1,0:T(8,128)(2,1)} %copy-done.18, bf16[8,1024]{1,0:T(8,128)(2,1)} %copy-done.19), custom_call_target="tpu_custom_call" | custom-call | tf_op jit(solution)/shard_map/pallas_call | solution.py:198
  (39 shorter events, 0.1 us)
Async XLA Ops:
  0.6 12.9 %collective-permute-start.7 = (bf16[64,1024]{1,0:T(8,128)(2,1)}, bf16[64,1024]{1,0:T(8,128)(2,1)S(1)}, u32[]{:S(2)}, u32[]{:S(2)}) collective-permute-start(bf16[64,1024]{1,0:T(8,128)(2,1)} %bitcast.28), channel_id=1, source_target_pairs={{0,1},{1,0},{2,3},{3,2},{4,5},{5,4},{6,7},{7,6},{8,9},{9,8},{10,11... | collective-permute-start | bytes 393224 | tf_op jit(solution)/shard_map/ppermute | solution.py:213
  2.5 6.9 %collective-permute-start.2 = (bf16[8,2176]{1,0:T(8,128)(2,1)}, bf16[8,2176]{1,0:T(8,128)(2,1)S(1)}, u32[]{:S(2)}, u32[]{:S(2)}) collective-permute-start(bf16[8,2176]{1,0:T(8,128)(2,1)} %shard_map.121.refs_0_), channel_id=1, source_target_pairs={{0,6},{1,7},{2,4},{3,5},{4,2},{5,3},{6,0},{7,1},{8,14},{9,15},{10,... | collective-permute-start | bytes 104456 | tf_op jit(solution)/shard_map/ppermute | solution.py:213
  7.1 5.0 %collective-permute-start.1 = (bf16[8,2176]{1,0:T(8,128)(2,1)}, bf16[8,2176]{1,0:T(8,128)(2,1)S(1)}, u32[]{:S(2)}, u32[]{:S(2)}) collective-permute-start(bf16[8,2176]{1,0:T(8,128)(2,1)} %shard_map.121.refs_0_), channel_id=1, source_target_pairs={{0,4},{1,5},{2,6},{3,7},{4,0},{5,1},{6,2},{7,3},{8,12},{9,13},{10,... | collective-permute-start | bytes 104456 | tf_op jit(solution)/shard_map/ppermute | solution.py:213
  7.1 5.1 %collective-permute-start = (bf16[8,2176]{1,0:T(8,128)(2,1)}, bf16[8,2176]{1,0:T(8,128)(2,1)S(1)}, u32[]{:S(2)}, u32[]{:S(2)}) collective-permute-start(bf16[8,2176]{1,0:T(8,128)(2,1)} %shard_map.121.refs_0_), channel_id=1, source_target_pairs={{0,2},{1,3},{2,0},{3,1},{4,6},{5,7},{6,4},{7,5},{8,10},{9,11},{10,... | collective-permute-start | bytes 104456 | tf_op jit(solution)/shard_map/ppermute | solution.py:213
  7.7 5.0 %collective-permute-start.3 = (bf16[8,2176]{1,0:T(8,128)(2,1)}, bf16[8,2176]{1,0:T(8,128)(2,1)S(1)}, u32[]{:S(2)}, u32[]{:S(2)}) collective-permute-start(bf16[8,2176]{1,0:T(8,128)(2,1)} %shard_map.121.refs_0_), channel_id=1, source_target_pairs={{0,1},{1,0},{2,3},{3,2},{4,5},{5,4},{6,7},{7,6},{8,9},{9,8},{10,11... | collective-permute-start | bytes 104456 | tf_op jit(solution)/shard_map/ppermute | solution.py:213
  9.4 4.1 %copy-start.9 = (bf16[8,2176]{1,0:T(8,128)(2,1)}, bf16[8,2176]{1,0:T(8,128)(2,1)S(1)}, u32[]{:S(2)}) copy-start(bf16[8,2176]{1,0:T(8,128)(2,1)S(1)} %collective-permute-done.2.refs_3_) | copy-start | bytes 104452
  9.4 3.3 %collective-permute-start.6 = (bf16[8,2176]{1,0:T(8,128)(2,1)S(1)}, bf16[8,2176]{1,0:T(8,128)(2,1)S(1)}, u32[]{:S(2)}, u32[]{:S(2)}) collective-permute-start(bf16[8,2176]{1,0:T(8,128)(2,1)S(1)} %collective-permute-done.2.refs_3_), channel_id=1, source_target_pairs={{0,1},{1,0},{2,3},{3,2},{4,5},{5,4},{6,7},{7,6},{8,9},{9,8},{10,11... | collective-permute-start | bytes 104456 | tf_op jit(solution)/shard_map/ppermute | solution.py:213
  12.2 1.4 %copy-start.10 = (bf16[8,2176]{1,0:T(8,128)(2,1)}, bf16[8,2176]{1,0:T(8,128)(2,1)S(1)}, u32[]{:S(2)}) copy-start(bf16[8,2176]{1,0:T(8,128)(2,1)S(1)} %collective-permute-done.1.refs_2_) | copy-start | bytes 104452
  12.2 1.2 %collective-permute-start.5 = (bf16[8,2176]{1,0:T(8,128)(2,1)S(1)}, bf16[8,2176]{1,0:T(8,128)(2,1)S(1)}, u32[]{:S(2)}, u32[]{:S(2)}) collective-permute-start(bf16[8,2176]{1,0:T(8,128)(2,1)S(1)} %collective-permute-done.1.refs_2_), channel_id=1, source_target_pairs={{0,1},{1,0},{2,3},{3,2},{4,5},{5,4},{6,7},{7,6},{8,9},{9,8},{10,11... | collective-permute-start | bytes 104456 | tf_op jit(solution)/shard_map/ppermute | solution.py:213
  12.2 1.4 %copy-start.11 = (bf16[8,2176]{1,0:T(8,128)(2,1)}, bf16[8,2176]{1,0:T(8,128)(2,1)S(1)}, u32[]{:S(2)}) copy-start(bf16[8,2176]{1,0:T(8,128)(2,1)S(1)} %collective-permute-done.refs_1_) | copy-start | bytes 104452
  12.2 1.4 %collective-permute-start.4 = (bf16[8,2176]{1,0:T(8,128)(2,1)S(1)}, bf16[8,2176]{1,0:T(8,128)(2,1)S(1)}, u32[]{:S(2)}, u32[]{:S(2)}) collective-permute-start(bf16[8,2176]{1,0:T(8,128)(2,1)S(1)} %collective-permute-done.refs_1_), channel_id=1, source_target_pairs={{0,1},{1,0},{2,3},{3,2},{4,5},{5,4},{6,7},{7,6},{8,9},{9,8},{10,11... | collective-permute-start | bytes 104456 | tf_op jit(solution)/shard_map/ppermute | solution.py:213
  12.7 0.9 %copy-start.12 = (bf16[8,2176]{1,0:T(8,128)(2,1)}, bf16[8,2176]{1,0:T(8,128)(2,1)S(1)}, u32[]{:S(2)}) copy-start(bf16[8,2176]{1,0:T(8,128)(2,1)S(1)} %collective-permute-done.3.refs_4_) | copy-start | bytes 104452
  12.7 0.9 %copy-start.13 = (bf16[8,2176]{1,0:T(8,128)(2,1)}, bf16[8,2176]{1,0:T(8,128)(2,1)S(1)}, u32[]{:S(2)}) copy-start(bf16[8,2176]{1,0:T(8,128)(2,1)S(1)} %collective-permute-done.6.refs_7_) | copy-start | bytes 104452
  13.4 0.6 %copy-start.14 = (bf16[8,2176]{1,0:T(8,128)(2,1)}, bf16[8,2176]{1,0:T(8,128)(2,1)S(1)}, u32[]{:S(2)}) copy-start(bf16[8,2176]{1,0:T(8,128)(2,1)S(1)} %collective-permute-done.5.refs_6_) | copy-start | bytes 104452
  13.6 0.6 %copy-start.15 = (bf16[8,2176]{1,0:T(8,128)(2,1)}, bf16[8,2176]{1,0:T(8,128)(2,1)S(1)}, u32[]{:S(2)}) copy-start(bf16[8,2176]{1,0:T(8,128)(2,1)S(1)} %collective-permute-done.4.refs_5_) | copy-start | bytes 104452
  13.6 0.7 %copy-start = (bf16[64,1024]{1,0:T(8,128)(2,1)}, bf16[64,1024]{1,0:T(8,128)(2,1)S(1)}, u32[]{:S(2)}) copy-start(bf16[64,1024]{1,0:T(8,128)(2,1)S(1)} %collective-permute-done.7.refs_12_.other_ref) | copy-start | bytes 393220
  14.2 7.4 %copy-start.1 = (bf16[1,2,4,16,512]{4,3,2,1,0:T(8,128)(2,1)S(1)}, bf16[1,2,4,16,512]{4,3,2,1,0:T(8,128)(2,1)}, u32[]{:S(2)}) copy-start(bf16[1,2,4,16,512]{4,3,2,1,0:T(8,128)(2,1)} %param.19) | copy-start | bytes 393220
  18.1 4.4 %collective-permute-start.8 = (bf16[16,1664]{1,0:T(8,128)(2,1)}, bf16[16,1664]{1,0:T(8,128)(2,1)S(1)}, u32[]{:S(2)}, u32[]{:S(2)}) collective-permute-start(bf16[16,1664]{1,0:T(8,128)(2,1)} %get-tuple-element.19), channel_id=1, source_target_pairs={{0,8},{8,0},{16,24},{24,16},{1,9},{9,1},{17,25},{25,17},{2,10},{10... | collective-permute-start | bytes 159752 | tf_op jit(solution)/shard_map/ppermute | solution.py:213
  19.7 4.3 %collective-permute-start.9 = (bf16[16,1664]{1,0:T(8,128)(2,1)}, bf16[16,1664]{1,0:T(8,128)(2,1)S(1)}, u32[]{:S(2)}, u32[]{:S(2)}) collective-permute-start(bf16[16,1664]{1,0:T(8,128)(2,1)} %get-tuple-element.20), channel_id=1, source_target_pairs={{0,16},{8,24},{16,0},{24,8},{1,17},{9,25},{17,1},{25,9},{2,18},{10... | collective-permute-start | bytes 159752 | tf_op jit(solution)/shard_map/ppermute | solution.py:213
  21.2 5.2 %collective-permute-start.10 = (bf16[16,1664]{1,0:T(8,128)(2,1)}, bf16[16,1664]{1,0:T(8,128)(2,1)S(1)}, u32[]{:S(2)}, u32[]{:S(2)}) collective-permute-start(bf16[16,1664]{1,0:T(8,128)(2,1)} %get-tuple-element.21), channel_id=1, source_target_pairs={{0,24},{8,16},{16,8},{24,0},{1,25},{9,17},{17,9},{25,1},{2,26},{10... | collective-permute-start | bytes 159752 | tf_op jit(solution)/shard_map/ppermute | solution.py:213
  22.5 3.9 %copy-start.3 = (bf16[16,1664]{1,0:T(8,128)(2,1)}, bf16[16,1664]{1,0:T(8,128)(2,1)S(1)}, u32[]{:S(2)}) copy-start(bf16[16,1664]{1,0:T(8,128)(2,1)S(1)} %collective-permute-done.8.first_ref) | copy-start | bytes 159748
  24.0 2.4 %copy-start.4 = (bf16[16,1664]{1,0:T(8,128)(2,1)}, bf16[16,1664]{1,0:T(8,128)(2,1)S(1)}, u32[]{:S(2)}) copy-start(bf16[16,1664]{1,0:T(8,128)(2,1)S(1)} %collective-permute-done.9.second_ref) | copy-start | bytes 159748
  26.4 0.6 %copy-start.5 = (bf16[16,1664]{1,0:T(8,128)(2,1)}, bf16[16,1664]{1,0:T(8,128)(2,1)S(1)}, u32[]{:S(2)}) copy-start(bf16[16,1664]{1,0:T(8,128)(2,1)S(1)} %collective-permute-done.10.third_ref) | copy-start | bytes 159748
  28.9 5.1 %collective-permute-start.13 = (bf16[16,1152]{1,0:T(8,128)(2,1)}, bf16[16,1152]{1,0:T(8,128)(2,1)S(1)}, u32[]{:S(2)}, u32[]{:S(2)}) collective-permute-start(bf16[16,1152]{1,0:T(8,128)(2,1)} %shard_map.123.own_ref), channel_id=1, source_target_pairs={{0,24},{8,16},{16,8},{24,0},{1,25},{9,17},{17,9},{25,1},{2,26},{10... | collective-permute-start | bytes 110600 | tf_op jit(solution)/shard_map/ppermute | solution.py:213
  29.4 4.6 %collective-permute-start.12 = (bf16[16,1152]{1,0:T(8,128)(2,1)}, bf16[16,1152]{1,0:T(8,128)(2,1)S(1)}, u32[]{:S(2)}, u32[]{:S(2)}) collective-permute-start(bf16[16,1152]{1,0:T(8,128)(2,1)} %shard_map.123.own_ref), channel_id=1, source_target_pairs={{0,16},{8,24},{16,0},{24,8},{1,17},{9,25},{17,1},{25,9},{2,18},{10... | collective-permute-start | bytes 110600 | tf_op jit(solution)/shard_map/ppermute | solution.py:213
  30.9 4.2 %collective-permute-start.11 = (bf16[16,1152]{1,0:T(8,128)(2,1)}, bf16[16,1152]{1,0:T(8,128)(2,1)S(1)}, u32[]{:S(2)}, u32[]{:S(2)}) collective-permute-start(bf16[16,1152]{1,0:T(8,128)(2,1)} %shard_map.123.own_ref), channel_id=1, source_target_pairs={{0,8},{8,0},{16,24},{24,16},{1,9},{9,1},{17,25},{25,17},{2,10},{10... | collective-permute-start | bytes 110600 | tf_op jit(solution)/shard_map/ppermute | solution.py:213
  34.0 1.1 %copy-start.6 = (bf16[16,1152]{1,0:T(8,128)(2,1)}, bf16[16,1152]{1,0:T(8,128)(2,1)S(1)}, u32[]{:S(2)}) copy-start(bf16[16,1152]{1,0:T(8,128)(2,1)S(1)} %collective-permute-done.13.third_ref) | copy-start | bytes 110596
  34.0 1.1 %copy-start.7 = (bf16[16,1152]{1,0:T(8,128)(2,1)}, bf16[16,1152]{1,0:T(8,128)(2,1)S(1)}, u32[]{:S(2)}) copy-start(bf16[16,1152]{1,0:T(8,128)(2,1)S(1)} %collective-permute-done.12.second_ref) | copy-start | bytes 110596
  35.1 0.6 %copy-start.8 = (bf16[16,1152]{1,0:T(8,128)(2,1)}, bf16[16,1152]{1,0:T(8,128)(2,1)S(1)}, u32[]{:S(2)}) copy-start(bf16[16,1152]{1,0:T(8,128)(2,1)S(1)} %collective-permute-done.11.first_ref) | copy-start | bytes 110596
  39.0 1.5 %collective-permute-start.14 = (bf16[32,1024]{1,0:T(8,128)(2,1)}, bf16[32,1024]{1,0:T(8,128)(2,1)S(1)}, u32[]{:S(2)}, u32[]{:S(2)}) collective-permute-start(bf16[32,1024]{1,0:T(8,128)(2,1)} %get-tuple-element.24), channel_id=1, source_target_pairs={{0,1},{1,0},{2,3},{3,2},{4,5},{5,4},{6,7},{7,6},{8,9},{9,8},{10,11... | collective-permute-start | bytes 196616 | tf_op jit(solution)/shard_map/ppermute | solution.py:213
  39.0 10.0 %collective-permute-start.18 = (f32[64,64]{1,0:T(8,128)}, f32[64,64]{1,0:T(8,128)S(1)}, u32[]{:S(2)}, u32[]{:S(2)}) collective-permute-start(f32[64,64]{1,0:T(8,128)} %get-tuple-element.30), channel_id=1, source_target_pairs={{0,1},{1,0},{2,3},{3,2},{4,5},{5,4},{6,7},{7,6},{8,9},{9,8},{10,11... | collective-permute-start | bytes 49160 | tf_op jit(solution)/shard_map/ppermute | solution.py:213
  40.5 0.6 %copy-start.2 = (bf16[32,1024]{1,0:T(8,128)(2,1)}, bf16[32,1024]{1,0:T(8,128)(2,1)S(1)}, u32[]{:S(2)}) copy-start(bf16[32,1024]{1,0:T(8,128)(2,1)S(1)} %collective-permute-done.14.taken_ref) | copy-start | bytes 196612
  42.6 8.9 %collective-permute-start.15 = (bf16[8,1024]{1,0:T(8,128)(2,1)}, bf16[8,1024]{1,0:T(8,128)(2,1)S(1)}, u32[]{:S(2)}, u32[]{:S(2)}) collective-permute-start(bf16[8,1024]{1,0:T(8,128)(2,1)} %get-tuple-element.26), channel_id=1, source_target_pairs={{0,2},{1,3},{2,0},{3,1},{4,6},{5,7},{6,4},{7,5},{8,10},{9,11},{10,... | collective-permute-start | bytes 49160 | tf_op jit(solution)/shard_map/ppermute | solution.py:213
  43.0 8.5 %collective-permute-start.16 = (bf16[8,1024]{1,0:T(8,128)(2,1)}, bf16[8,1024]{1,0:T(8,128)(2,1)S(1)}, u32[]{:S(2)}, u32[]{:S(2)}) collective-permute-start(bf16[8,1024]{1,0:T(8,128)(2,1)} %get-tuple-element.27), channel_id=1, source_target_pairs={{0,4},{1,5},{2,6},{3,7},{4,0},{5,1},{6,2},{7,3},{8,12},{9,13},{10,... | collective-permute-start | bytes 49160 | tf_op jit(solution)/shard_map/ppermute | solution.py:213
  44.8 6.7 %collective-permute-start.17 = (bf16[8,1024]{1,0:T(8,128)(2,1)}, bf16[8,1024]{1,0:T(8,128)(2,1)S(1)}, u32[]{:S(2)}, u32[]{:S(2)}) collective-permute-start(bf16[8,1024]{1,0:T(8,128)(2,1)} %get-tuple-element.28), channel_id=1, source_target_pairs={{0,6},{1,7},{2,4},{3,5},{4,2},{5,3},{6,0},{7,1},{8,14},{9,15},{10,... | collective-permute-start | bytes 49160 | tf_op jit(solution)/shard_map/ppermute | solution.py:213
  49.0 0.6 %copy-start.16 = (f32[64,64]{1,0:T(8,128)}, f32[64,64]{1,0:T(8,128)S(1)}, u32[]{:S(2)}) copy-start(f32[64,64]{1,0:T(8,128)S(1)} %collective-permute-done.18.taken_ref) | copy-start | bytes 49156
  51.5 0.6 %copy-start.17 = (bf16[8,1024]{1,0:T(8,128)(2,1)}, bf16[8,1024]{1,0:T(8,128)(2,1)S(1)}, u32[]{:S(2)}) copy-start(bf16[8,1024]{1,0:T(8,128)(2,1)S(1)} %collective-permute-done.15.first_ref) | copy-start | bytes 49156
  51.5 0.6 %copy-start.18 = (bf16[8,1024]{1,0:T(8,128)(2,1)}, bf16[8,1024]{1,0:T(8,128)(2,1)S(1)}, u32[]{:S(2)}) copy-start(bf16[8,1024]{1,0:T(8,128)(2,1)S(1)} %collective-permute-done.16.second_ref) | copy-start | bytes 49156
  51.5 0.6 %copy-start.19 = (bf16[8,1024]{1,0:T(8,128)(2,1)}, bf16[8,1024]{1,0:T(8,128)(2,1)S(1)}, u32[]{:S(2)}) copy-start(bf16[8,1024]{1,0:T(8,128)(2,1)S(1)} %collective-permute-done.17.third_ref) | copy-start | bytes 49156

commit v2 on v1

--- a/solution.py
+++ b/solution.py
@@ -192,16 +192,22 @@
 F32 = jnp.float32
 BF16 = jnp.bfloat16
 VMEM = pl.BlockSpec(memory_space=pltpu.VMEM)
-
-
-def local_call(body, outs, operands, scratch=(), flops=0, moved=0):
+HBM = pl.BlockSpec(memory_space=pltpu.HBM)
+
+
+def local_call(body, outs, operands, scratch=(), flops=0, moved=0, far=0):
+    operands = [
+        pltpu.with_memory_space_constraint(array, pltpu.HBM) if k < far else array
+        for k, array in enumerate(operands)
+    ]
     return pl.pallas_call(
         body,
         out_shape=[jax.ShapeDtypeStruct(shape, kind) for shape, kind in outs],
-        in_specs=[VMEM] * len(operands),
+        in_specs=[HBM] * far + [VMEM] * (len(operands) - far),
         out_specs=[VMEM] * len(outs),
         scratch_shapes=list(scratch),
         cost_estimate=pl.CostEstimate(flops=flops, bytes_accessed=moved, transcendentals=0),
+        compiler_params=pltpu.CompilerParams(vmem_limit_bytes=16 << 20),
     )(*operands)
 
 
@@ -213,16 +219,58 @@
     return lax.ppermute(array, axis, [(i, i ^ offset) for i in range(lax.axis_size(axis))])
 
 
-def pack_body(x_ref, dy_ref, routes_ref, weight_ref, tenant_ref, out_ref):
+def pack_body(
+    x_ref, dy_ref, routes_ref, weight_ref, tenant_ref, out_ref, routes, weight, tenant, arrived
+):
     width = x_ref.shape[1]
     topk, count = routes_ref.shape
-    out_ref[:, :width] = x_ref[...]
-    out_ref[:, width : 2 * width] = dy_ref[...]
-    tags = [routes_ref[...].astype(F32), weight_ref[...].astype(F32), tenant_ref[...].astype(F32)]
+    copies = [
+        pltpu.make_async_copy(source, target, arrived.at[k])
+        for k, (source, target) in enumerate(
+            (
+                (routes_ref, routes),
+                (weight_ref, weight),
+                (tenant_ref, tenant),
+                (x_ref, out_ref.at[:, :width]),
+                (dy_ref, out_ref.at[:, width : 2 * width]),
+            )
+        )
+    ]
+    for copy in copies:
+        copy.start()
+    for copy in copies[:3]:
+        copy.wait()
+    tags = [routes[...].astype(F32), weight[...].astype(F32), tenant[...].astype(F32)]
     rows = 2 * topk + 1
     tags = jnp.concatenate(tags + [jnp.zeros((count - rows, count), F32)], axis=0)
     tags = jnp.concatenate([tags, jnp.zeros((count, 128 - count), F32)], axis=1)
     out_ref[:, 2 * width :] = tags.astype(BF16)
+    for copy in copies[3:]:
+        copy.wait()
+
+
+def stage_body(*refs):
+    count = (len(refs) - 2) // 2
+    sources, targets, maps, arrived = refs[:count], refs[count : 2 * count], refs[-2], refs[-1]
+    copies = [
+        pltpu.make_async_copy(source, target, arrived.at[k])
+        for k, (source, target) in enumerate(zip(sources, targets[:-1] + (maps,)))
+    ]
+    for copy in copies:
+        copy.start()
+    copies[-1].wait()
+    targets[-1][...] = dot_plain(rank_order(maps.shape[0], False), maps[...]).astype(BF16)
+    for copy in copies[:-1]:
+        copy.wait()
+
+
+def rank_order(lanes, columns):
+    at = lax.broadcasted_iota(jnp.int32, (lanes, lanes), 0 if columns else 1)
+    place = lax.broadcasted_iota(jnp.int32, (lanes, lanes), 1 if columns else 0)
+    if not columns:
+        at, place = place, at
+    source = lax.rem(place // 8, 2) * (lanes // 2) + (place // 16) * 8 + lax.rem(place, 8)
+    return (at == source).astype(BF16)
 
 
 def forward_body(topk, *refs):
@@ -276,7 +324,7 @@
     return is_gate, tenant_of.astype(F32) == tenant
 
 
-def activation_body(ranks, own_ref, first_ref, second_ref, third_ref, tag_ref, maps_ref, out_ref):
+def activation_body(ranks, own_ref, third_ref, second_ref, first_ref, tag_ref, maps_ref, out_ref):
     hidden = maps_ref.shape[1]
     part = own_ref.shape[0]
     me = lax.axis_index("dp")
@@ -357,7 +405,7 @@
         ref[...] = total[k * count : (k + 1) * count].astype(ref.dtype)
 
 
-def finish_body(own_ref, first_ref, second_ref, third_ref, out_ref):
+def finish_body(own_ref, third_ref, second_ref, first_ref, out_ref):
     total = (own_ref[...] + first_ref[...].astype(F32)) + (
         second_ref[...].astype(F32) + third_ref[...].astype(F32)
     )
@@ -368,12 +416,7 @@
     hidden = out_ref.shape[1]
     lanes = out_ref.shape[0]
     half = lanes // 2
-    row = lax.broadcasted_iota(jnp.int32, (lanes, lanes), 0)
-    col = lax.broadcasted_iota(jnp.int32, (lanes, lanes), 1)
-    low = rows_ref[:, 2 * hidden :]
-    source = lax.rem(col // 8, 2) * half + (col // 16) * 8 + lax.rem(col, 8)
-    order = (row == source).astype(BF16)
-    low = dot_plain(low, order).astype(BF16)
+    low = dot_plain(rows_ref[:, 2 * hidden :], rank_order(lanes, True)).astype(BF16)
     out_ref[:half] = ADAPTER_SCALE * product_leading(low[:, :half], rows_ref[:, :hidden])
     out_ref[half:] = ADAPTER_SCALE * product_leading(
         low[:, half:], rows_ref[:, hidden : 2 * hidden]
@@ -409,21 +452,39 @@
     slots = devices * count
     part = slots // 4
     mine_cols = adapter_input_maps[0].transpose(1, 2, 3, 0).reshape(lanes // 2, width)
-    maps = (
-        adapter_output_maps[0]
-        .reshape(2, tenants, 2, ranks, hidden)
-        .transpose(2, 0, 1, 3, 4)
-        .reshape(lanes, hidden)
-    )
     other_cols = swap(mine_cols, "expert", 1)
     (packed,) = local_call(
         pack_body,
         [((count, 2 * width + 128), BF16)],
         (tokens, output_gradient, routes.T, router_expert_weight.T, tenant[None, :]),
+        scratch=[
+            pltpu.VMEM((topk, count), jnp.int32),
+            pltpu.VMEM((topk, count), BF16),
+            pltpu.VMEM((1, count), jnp.int32),
+            pltpu.SemaphoreType.DMA((5,)),
+        ],
+        far=5,
+    )
+    stored = (
+        gate_weight[0],
+        up_weight[0],
+        down_weight[0],
+        mine_cols,
+        adapter_output_maps.reshape(lanes, hidden),
+    )
+    gate, up, down, mine_cols, maps = local_call(
+        stage_body,
+        [(array.shape, BF16) for array in stored],
+        stored,
+        scratch=[pltpu.VMEM((lanes, hidden), BF16), pltpu.SemaphoreType.DMA((len(stored),))],
+        moved=sum(2 * array.size for array in stored),
+        far=len(stored),
     )
     same_core = [packed] + [swap(packed, "expert", 2 * k) for k in range(1, chips)]
+    same_core[-1], (gate, up, down, mine_cols, maps) = lax.optimization_barrier(
+        (same_core[-1], (gate, up, down, mine_cols, maps))
+    )
     other_core = [swap(block, "expert", 1) for block in same_core]
-    gate, up, down = gate_weight[0], up_weight[0], down_weight[0]
     columns = 3 * hidden + lanes
     own, first, second, third, x, tags = local_call(
         functools.partial(forward_body, topk),
@@ -440,7 +501,8 @@
         flops=2 * slots * width * columns,
         moved=4 * width * columns,
     )
-    sums = [own] + [swap(block, "dp", k + 1) for k, block in enumerate((first, second, third))]
+    third, second, first = swap(third, "dp", 3), swap(second, "dp", 2), swap(first, "dp", 1)
+    sums = [own, third, second, first]
     (gradients,) = local_call(
         functools.partial(activation_body, ranks),
         [((part, 2 * hidden + lanes), BF16)],
@@ -467,9 +529,8 @@
         [((count, width), F32)] + [((count, width), BF16)] * 3,
         (keep, taken),
     )
-    returned = [own] + [
-        swap(block, "expert", 2 * (k + 1)) for k, block in enumerate((first, second, third))
-    ]
+    third, second = swap(third, "expert", 6), swap(second, "expert", 4)
+    returned = [own, third, second, swap(first, "expert", 2)]
     (maps_grad,) = local_call(maps_grad_body, [((lanes, hidden), F32)], (rows,))
     (input_maps_grad,) = local_call(
         input_maps_grad_body, [((lanes // 2, width), F32)], (back_keep, back_taken, x)

time: 53.9 us -> 37.5 us (0.70)
  Pallas kernels: 17.2 us -> 7.86 us
  local copies, waits for them, and re-layouts: 4.35 us -> 0 us
  waiting for transfers between devices: 13.1 us -> 10.3 us
    pallas_call x8 -> x9, Pallas kernels: 17.2 us -> 7.86 us  [local_call(): pl.pallas_call(body, out_shape=[jax.ShapeDtypeStruct(shape, kind) for sha...]
    unnamed x40 -> x0, local copies, waits for them, and re-layouts: 3.7 us -> none
    ppermute x19, waiting for transfers between devices: 13.1 us -> 10.3 us  [swap(): lax.ppermute(array, axis, [(i, i ^ offset) for i in range(lax.axis_size(a...]
    another operation x1 -> x0, local copies, waits for them, and re-layouts: 0.65 us -> none  [dense_shards(): maps = adapter_output_maps[0].reshape(2, tenants, 2, ranks, hidden).trans...]
  transfers between devices with their start and end apart: 19 -> 19, of which waited for: 10 -> 12; matrix products, arithmetic and copies ran while one was open for 1% -> 0% of each run, Pallas kernels for 13% -> 13%
where the time goes in v2:
time: 37.5 us; the launch traced here: 37.3 us
  starting transfers between devices  18.5 us (49%)
  waiting for transfers between devices  10.3 us (27%)
  Pallas kernels  7.86 us (21%)
  between operations  0.7 us (2%)
    ppermute x19, starting transfers between devices, swap(): lax.ppermute(array, axis, [(i, i ^ offset) for i in range(lax.axis_size(a...  18.5 us
    ppermute x19, waiting for transfers between devices, swap(): lax.ppermute(array, axis, [(i, i ^ offset) for i in range(lax.axis_size(a...  10.3 us
    pallas_call x9, Pallas kernels, local_call(): pl.pallas_call(body, out_shape=[jax.ShapeDtypeStruct(shape, kind) for sha...  7.86 us
  transfers between devices with their start and end apart: 19, of which 12 were waited for; matrix products, arithmetic and copies ran while one was open for 0% of the time, Pallas kernels for 13%

profile of v2, /device:TPU:0, one launch (start us, length us, event | category | flops | bytes accessed | tf_op | source)
XLA Modules:
  0.0 37.3 jit_solution(17292061351962975943)
XLA Ops:
  0.6 0.5 %collective-permute-start.7 = (bf16[64,1024]{1,0:T(8,128)(2,1)}, bf16[64,1024]{1,0:T(8,128)(2,1)S(1)}, u32[]{:S(2)}, u32[]{:S(2)}) collective-permute-start(bf16[64,1024]{1,0:T(8,128)(2,1)} %bitcast.24), channel_id=1, source_target_pairs={{0,1},{1,0},{2,3},{3,2},{4,5},{5,4},{6,7},{7,6},{8,9},{9,8},{10,11... | collective-permute-start | bytes 393224 | tf_op jit(solution)/shard_map/ppermute | solution.py:219
  1.1 0.8 %shard_map.121.refs_0_ = bf16[8,2176]{1,0:T(8,128)(2,1)S(1)} custom-call(bf16[8,1024]{1,0:T(8,128)(2,1)} %x_ref.1, bf16[8,1024]{1,0:T(8,128)(2,1)} %dy_ref.1, s32[2,8]{1,0:T(2,128)} %bitcast.26, bf16[2,8]{1,0:T(2,128)(2,1)} %bitcast.27, s32[1,8]{1,0:T(1,128)} %bitcast.28), custom_call_target="tpu_custom_call" | custom-call | tf_op jit(solution)/shard_map/pallas_call | solution.py:203
  2.0 4.7 %collective-permute-start.2 = (bf16[8,2176]{1,0:T(8,128)(2,1)S(1)}, bf16[8,2176]{1,0:T(8,128)(2,1)S(1)}, u32[]{:S(2)}, u32[]{:S(2)}) collective-permute-start(bf16[8,2176]{1,0:T(8,128)(2,1)S(1)} %shard_map.121.refs_0_), channel_id=1, source_target_pairs={{0,6},{1,7},{2,4},{3,5},{4,2},{5,3},{6,0},{7,1},{8,14},{9,15},{10,... | collective-permute-start | bytes 104456 | tf_op jit(solution)/shard_map/ppermute | solution.py:219
  6.7 0.0 collective-permute-start.1
  6.7 0.6 %collective-permute-start = (bf16[8,2176]{1,0:T(8,128)(2,1)S(1)}, bf16[8,2176]{1,0:T(8,128)(2,1)S(1)}, u32[]{:S(2)}, u32[]{:S(2)}) collective-permute-start(bf16[8,2176]{1,0:T(8,128)(2,1)S(1)} %shard_map.121.refs_0_), channel_id=1, source_target_pairs={{0,2},{1,3},{2,0},{3,1},{4,6},{5,7},{6,4},{7,5},{8,10},{9,11},{10,... | collective-permute-start | bytes 104456 | tf_op jit(solution)/shard_map/ppermute | solution.py:219
  7.3 0.0 collective-permute-start.3
  7.3 2.1 %shard_map.122 = (bf16[1024,512]{1,0:T(8,128)(2,1)S(1)}, bf16[1024,512]{1,0:T(8,128)(2,1)S(1)}, bf16[512,1024]{1,0:T(8,128)(2,1)S(1)}, bf16[64,1024]{1,0:T(8,128)(2,1)S(1)}, bf16[128,512]{1,0:T(8,128)(2,1)S(1)}) custom-call(bf16[1024,512]{1,0:T(8,128)(2,1)} %bitcast.18, bf16[1024,512]{1,0:T(8,128)(2,1)} %bitcast.19, bf16[512,1024]{1,0:T(8,128)(2,1)} %bitcast.20, ...), custom_call_target="tpu_custom_call" | custom-call | bytes 3407872 | tf_op jit(solution)/shard_map/pallas_call | solution.py:203
  9.4 0.0 collective-permute-done.2.refs_3_
  9.4 2.1 %collective-permute-done.1.refs_2_ = bf16[8,2176]{1,0:T(8,128)(2,1)S(1)} collective-permute-done((bf16[8,2176]{1,0:T(8,128)(2,1)S(1)}, bf16[8,2176]{1,0:T(8,128)(2,1)S(1)}, u32[]{:S(2)}, u32[]{:S(2)}) %collective-permute-start.1) | collective-permute-done | bytes 34848 | tf_op jit(solution)/shard_map/ppermute | solution.py:219
  11.5 0.0 collective-permute-start.5
  11.5 0.0 collective-permute-done.refs_1_
  11.5 0.5 %collective-permute-start.4 = (bf16[8,2176]{1,0:T(8,128)(2,1)S(1)}, bf16[8,2176]{1,0:T(8,128)(2,1)S(1)}, u32[]{:S(2)}, u32[]{:S(2)}) collective-permute-start(bf16[8,2176]{1,0:T(8,128)(2,1)S(1)} %collective-permute-done.refs_1_), channel_id=1, source_target_pairs={{0,1},{1,0},{2,3},{3,2},{4,5},{5,4},{6,7},{7,6},{8,9},{9,8},{10,11... | collective-permute-start | bytes 104456 | tf_op jit(solution)/shard_map/ppermute | solution.py:219
  12.0 0.0 collective-permute-start.6
  12.0 0.0 collective-permute-done.3.refs_4_
  12.0 0.7 %collective-permute-done.5.refs_6_ = bf16[8,2176]{1,0:T(8,128)(2,1)S(1)} collective-permute-done((bf16[8,2176]{1,0:T(8,128)(2,1)S(1)}, bf16[8,2176]{1,0:T(8,128)(2,1)S(1)}, u32[]{:S(2)}, u32[]{:S(2)}) %collective-permute-start.5) | collective-permute-done | bytes 34848 | tf_op jit(solution)/shard_map/ppermute | solution.py:219
  12.7 0.2 collective-permute-done.4.refs_5_
  12.9 0.3 collective-permute-done.6.refs_7_
  13.2 0.0 collective-permute-done.7.refs_12_.other_ref
  13.2 1.1 %shard_map.123 = (f32[16,1664]{1,0:T(8,128)S(1)}, bf16[16,1664]{1,0:T(8,128)(2,1)S(1)}, bf16[16,1664]{1,0:T(8,128)(2,1)S(1)}, bf16[16,1664]{1,0:T(8,128)(2,1)S(1...) custom-call(bf16[8,2176]{1,0:T(8,128)(2,1)S(1)} %shard_map.121.refs_0_, ...), custom_call_target="tpu_custom_call" | custom-call | flops 218103808 | bytes 6815744 | tf_op jit(solution)/shard_map/pallas_call | solution.py:203
  14.4 2.5 %collective-permute-start.8 = (bf16[16,1664]{1,0:T(8,128)(2,1)S(1)}, bf16[16,1664]{1,0:T(8,128)(2,1)S(1)}, u32[]{:S(2)}, u32[]{:S(2)}) collective-permute-start(bf16[16,1664]{1,0:T(8,128)(2,1)S(1)} %get-tuple-element.40), channel_id=1, source_target_pairs={{0,24},{8,16},{16,8},{24,0},{1,25},{9,17},{17,9},{25,1},{2,26},{10... | collective-permute-start | bytes 159752 | tf_op jit(solution)/shard_map/ppermute | solution.py:219
  16.9 0.5 %collective-permute-start.9 = (bf16[16,1664]{1,0:T(8,128)(2,1)S(1)}, bf16[16,1664]{1,0:T(8,128)(2,1)S(1)}, u32[]{:S(2)}, u32[]{:S(2)}) collective-permute-start(bf16[16,1664]{1,0:T(8,128)(2,1)S(1)} %get-tuple-element.41), channel_id=1, source_target_pairs={{0,16},{8,24},{16,0},{24,8},{1,17},{9,25},{17,1},{25,9},{2,18},{10... | collective-permute-start | bytes 159752 | tf_op jit(solution)/shard_map/ppermute | solution.py:219
  17.4 0.5 %collective-permute-start.10 = (bf16[16,1664]{1,0:T(8,128)(2,1)S(1)}, bf16[16,1664]{1,0:T(8,128)(2,1)S(1)}, u32[]{:S(2)}, u32[]{:S(2)}) collective-permute-start(bf16[16,1664]{1,0:T(8,128)(2,1)S(1)} %get-tuple-element.42), channel_id=1, source_target_pairs={{0,8},{8,0},{16,24},{24,16},{1,9},{9,1},{17,25},{25,17},{2,10},{10... | collective-permute-start | bytes 159752 | tf_op jit(solution)/shard_map/ppermute | solution.py:219
  17.9 1.5 %collective-permute-done.8.third_ref = bf16[16,1664]{1,0:T(8,128)(2,1)S(1)} collective-permute-done((bf16[16,1664]{1,0:T(8,128)(2,1)S(1)}, bf16[16,1664]{1,0:T(8,128)(2,1)S(1)}, u32[]{:S(2)}, u32[]{:S(2)}) %collective-permute-start.8) | collective-permute-done | bytes 53280 | tf_op jit(solution)/shard_map/ppermute | solution.py:219
  19.4 1.5 %collective-permute-done.9.second_ref = bf16[16,1664]{1,0:T(8,128)(2,1)S(1)} collective-permute-done((bf16[16,1664]{1,0:T(8,128)(2,1)S(1)}, bf16[16,1664]{1,0:T(8,128)(2,1)S(1)}, u32[]{:S(2)}, u32[]{:S(2)}) %collective-permute-start.9) | collective-permute-done | bytes 53280 | tf_op jit(solution)/shard_map/ppermute | solution.py:219
  21.0 0.5 %collective-permute-done.10.first_ref = bf16[16,1664]{1,0:T(8,128)(2,1)S(1)} collective-permute-done((bf16[16,1664]{1,0:T(8,128)(2,1)S(1)}, bf16[16,1664]{1,0:T(8,128)(2,1)S(1)}, u32[]{:S(2)}, u32[]{:S(2)}) %collective-permute-start.10) | collective-permute-done | bytes 53280 | tf_op jit(solution)/shard_map/ppermute | solution.py:219
  21.5 0.2 shard_map.124.own_ref
  21.7 1.6 %collective-permute-start.13 = (bf16[16,1152]{1,0:T(8,128)(2,1)S(1)}, bf16[16,1152]{1,0:T(8,128)(2,1)S(1)}, u32[]{:S(2)}, u32[]{:S(2)}) collective-permute-start(bf16[16,1152]{1,0:T(8,128)(2,1)S(1)} %shard_map.124.own_ref), channel_id=1, source_target_pairs={{0,24},{8,16},{16,8},{24,0},{1,25},{9,17},{17,9},{25,1},{2,26},{10... | collective-permute-start | bytes 110600 | tf_op jit(solution)/shard_map/ppermute | solution.py:219
  23.3 0.5 %collective-permute-start.12 = (bf16[16,1152]{1,0:T(8,128)(2,1)S(1)}, bf16[16,1152]{1,0:T(8,128)(2,1)S(1)}, u32[]{:S(2)}, u32[]{:S(2)}) collective-permute-start(bf16[16,1152]{1,0:T(8,128)(2,1)S(1)} %shard_map.124.own_ref), channel_id=1, source_target_pairs={{0,16},{8,24},{16,0},{24,8},{1,17},{9,25},{17,1},{25,9},{2,18},{10... | collective-permute-start | bytes 110600 | tf_op jit(solution)/shard_map/ppermute | solution.py:219
  23.8 1.5 %collective-permute-start.11 = (bf16[16,1152]{1,0:T(8,128)(2,1)S(1)}, bf16[16,1152]{1,0:T(8,128)(2,1)S(1)}, u32[]{:S(2)}, u32[]{:S(2)}) collective-permute-start(bf16[16,1152]{1,0:T(8,128)(2,1)S(1)} %shard_map.124.own_ref), channel_id=1, source_target_pairs={{0,8},{8,0},{16,24},{24,16},{1,9},{9,1},{17,25},{25,17},{2,10},{10... | collective-permute-start | bytes 110600 | tf_op jit(solution)/shard_map/ppermute | solution.py:219
  25.3 1.4 %collective-permute-done.13.third_ref = bf16[16,1152]{1,0:T(8,128)(2,1)S(1)} collective-permute-done((bf16[16,1152]{1,0:T(8,128)(2,1)S(1)}, bf16[16,1152]{1,0:T(8,128)(2,1)S(1)}, u32[]{:S(2)}, u32[]{:S(2)}) %collective-permute-start.13) | collective-permute-done | bytes 36896 | tf_op jit(solution)/shard_map/ppermute | solution.py:219
  26.6 0.6 %collective-permute-done.12.second_ref = bf16[16,1152]{1,0:T(8,128)(2,1)S(1)} collective-permute-done((bf16[16,1152]{1,0:T(8,128)(2,1)S(1)}, bf16[16,1152]{1,0:T(8,128)(2,1)S(1)}, u32[]{:S(2)}, u32[]{:S(2)}) %collective-permute-start.12) | collective-permute-done | bytes 36896 | tf_op jit(solution)/shard_map/ppermute | solution.py:219
  27.2 0.5 %collective-permute-done.11.first_ref = bf16[16,1152]{1,0:T(8,128)(2,1)S(1)} collective-permute-done((bf16[16,1152]{1,0:T(8,128)(2,1)S(1)}, bf16[16,1152]{1,0:T(8,128)(2,1)S(1)}, u32[]{:S(2)}, u32[]{:S(2)}) %collective-permute-start.11) | collective-permute-done | bytes 36896 | tf_op jit(solution)/shard_map/ppermute | solution.py:219
  27.7 0.9 %shard_map.125 = (f32[32,1024]{1,0:T(8,128)S(1)}, bf16[32,1024]{1,0:T(8,128)(2,1)S(1)}, f32[64,64]{1,0:T(8,128)S(1)}, f32[64,64]{1,0:T(8,128)S(1)}, bf16[64,1152]{1,0:T(8,128)(2,1)S(1)}) custom-call(bf16[16,1152]{1,0:T(8,128)(2,1)S(1)} %shard_map.124.own_ref, bf16[16,1152]{1,0:T(8,128)(2,1)S(1)} %collective-permute-done.11.first_ref, ...), custom_call_target="tpu_custom_call" | custom-call | flops 134217728 | bytes 2097152 | tf_op jit(solution)/shard_map/pallas_call | solution.py:203
  28.7 0.1 collective-permute-start.14
  28.8 0.5 %collective-permute-start.18 = (f32[64,64]{1,0:T(8,128)S(1)}, f32[64,64]{1,0:T(8,128)S(1)}, u32[]{:S(2)}, u32[]{:S(2)}) collective-permute-start(f32[64,64]{1,0:T(8,128)S(1)} %get-tuple-element.52), channel_id=1, source_target_pairs={{0,1},{1,0},{2,3},{3,2},{4,5},{5,4},{6,7},{7,6},{8,9},{9,8},{10,11... | collective-permute-start | bytes 49160 | tf_op jit(solution)/shard_map/ppermute | solution.py:219
  29.3 0.7 %collective-permute-done.14.taken_ref = bf16[32,1024]{1,0:T(8,128)(2,1)S(1)} collective-permute-done((bf16[32,1024]{1,0:T(8,128)(2,1)S(1)}, bf16[32,1024]{1,0:T(8,128)(2,1)S(1)}, u32[]{:S(2)}, u32[]{:S(2)}) %collective-permute-start.14) | collective-permute-done | bytes 65568 | tf_op jit(solution)/shard_map/ppermute | solution.py:219
  30.0 2.0 %collective-permute-start.15 = (bf16[8,1024]{1,0:T(8,128)(2,1)S(1)}, bf16[8,1024]{1,0:T(8,128)(2,1)S(1)}, u32[]{:S(2)}, u32[]{:S(2)}) collective-permute-start(bf16[8,1024]{1,0:T(8,128)(2,1)S(1)} %get-tuple-element.48), channel_id=1, source_target_pairs={{0,6},{1,7},{2,4},{3,5},{4,2},{5,3},{6,0},{7,1},{8,14},{9,15},{10,... | collective-permute-start | bytes 49160 | tf_op jit(solution)/shard_map/ppermute | solution.py:219
  32.1 0.0 collective-permute-start.16
  32.1 2.4 %collective-permute-start.17 = (bf16[8,1024]{1,0:T(8,128)(2,1)S(1)}, bf16[8,1024]{1,0:T(8,128)(2,1)S(1)}, u32[]{:S(2)}, u32[]{:S(2)}) collective-permute-start(bf16[8,1024]{1,0:T(8,128)(2,1)S(1)} %get-tuple-element.50), channel_id=1, source_target_pairs={{0,2},{1,3},{2,0},{3,1},{4,6},{5,7},{6,4},{7,5},{8,10},{9,11},{10,... | collective-permute-start | bytes 49160 | tf_op jit(solution)/shard_map/ppermute | solution.py:219
  34.5 1.1 %shard_map.129 = f32[128,512]{1,0:T(8,128)} custom-call(bf16[64,1152]{1,0:T(8,128)(2,1)S(1)} %get-tuple-element.54.rows_ref), custom_call_target="tpu_custom_call" | custom-call | tf_op jit(solution)/shard_map/pallas_call | solution.py:203
  35.6 0.0 collective-permute-done.18.taken_ref
  35.6 0.9 %shard_map.128 = f32[64,1024]{1,0:T(8,128)} custom-call(f32[64,64]{1,0:T(8,128)S(1)} %get-tuple-element.51.keep_ref, f32[64,64]{1,0:T(8,128)S(1)} %collective-permute-done.18.taken_ref, bf16[64,1024]{1,0:T(8,128)(2,1)S(1)} %get-tuple-element.53.x_ref), custom_call_target="tpu_custom_call" | custom-call | tf_op jit(solution)/shard_map/pallas_call | solution.py:203
  36.5 0.0 collective-permute-done.15.third_ref
  36.5 0.2 collective-permute-done.16.second_ref
  36.7 0.0 collective-permute-done.17.first_ref
  36.7 0.6 %shard_map.127 = bf16[8,1024]{1,0:T(8,128)(2,1)} custom-call(f32[8,1024]{1,0:T(8,128)S(1)} %get-tuple-element.47.own_ref, bf16[8,1024]{1,0:T(8,128)(2,1)S(1)} %collective-permute-done.15.third_ref, bf16[8,1024]{1,0:T(8,128)(2,1)S(1)} %collective-permute-done.16.second_ref, bf16[8,1024]{1,0:T(8,128)(2,1)S(1)} %collective-permute-done.17.first_ref), custom_call_target="tpu_custom_call" | custom-call | tf_op jit(solution)/shard_map/pallas_call | solution.py:203
  (1 shorter events, 0.0 us)
Async XLA Ops:
  0.6 12.6 %collective-permute-start.7 = (bf16[64,1024]{1,0:T(8,128)(2,1)}, bf16[64,1024]{1,0:T(8,128)(2,1)S(1)}, u32[]{:S(2)}, u32[]{:S(2)}) collective-permute-start(bf16[64,1024]{1,0:T(8,128)(2,1)} %bitcast.24), channel_id=1, source_target_pairs={{0,1},{1,0},{2,3},{3,2},{4,5},{5,4},{6,7},{7,6},{8,9},{9,8},{10,11... | collective-permute-start | bytes 393224 | tf_op jit(solution)/shard_map/ppermute | solution.py:219
  2.0 7.4 %collective-permute-start.2 = (bf16[8,2176]{1,0:T(8,128)(2,1)S(1)}, bf16[8,2176]{1,0:T(8,128)(2,1)S(1)}, u32[]{:S(2)}, u32[]{:S(2)}) collective-permute-start(bf16[8,2176]{1,0:T(8,128)(2,1)S(1)} %shard_map.121.refs_0_), channel_id=1, source_target_pairs={{0,6},{1,7},{2,4},{3,5},{4,2},{5,3},{6,0},{7,1},{8,14},{9,15},{10,... | collective-permute-start | bytes 104456 | tf_op jit(solution)/shard_map/ppermute | solution.py:219
  6.7 4.8 %collective-permute-start.1 = (bf16[8,2176]{1,0:T(8,128)(2,1)S(1)}, bf16[8,2176]{1,0:T(8,128)(2,1)S(1)}, u32[]{:S(2)}, u32[]{:S(2)}) collective-permute-start(bf16[8,2176]{1,0:T(8,128)(2,1)S(1)} %shard_map.121.refs_0_), channel_id=1, source_target_pairs={{0,4},{1,5},{2,6},{3,7},{4,0},{5,1},{6,2},{7,3},{8,12},{9,13},{10,... | collective-permute-start | bytes 104456 | tf_op jit(solution)/shard_map/ppermute | solution.py:219
  6.7 4.8 %collective-permute-start = (bf16[8,2176]{1,0:T(8,128)(2,1)S(1)}, bf16[8,2176]{1,0:T(8,128)(2,1)S(1)}, u32[]{:S(2)}, u32[]{:S(2)}) collective-permute-start(bf16[8,2176]{1,0:T(8,128)(2,1)S(1)} %shard_map.121.refs_0_), channel_id=1, source_target_pairs={{0,2},{1,3},{2,0},{3,1},{4,6},{5,7},{6,4},{7,5},{8,10},{9,11},{10,... | collective-permute-start | bytes 104456 | tf_op jit(solution)/shard_map/ppermute | solution.py:219
  7.3 4.7 %collective-permute-start.3 = (bf16[8,2176]{1,0:T(8,128)(2,1)S(1)}, bf16[8,2176]{1,0:T(8,128)(2,1)S(1)}, u32[]{:S(2)}, u32[]{:S(2)}) collective-permute-start(bf16[8,2176]{1,0:T(8,128)(2,1)S(1)} %shard_map.121.refs_0_), channel_id=1, source_target_pairs={{0,1},{1,0},{2,3},{3,2},{4,5},{5,4},{6,7},{7,6},{8,9},{9,8},{10,11... | collective-permute-start | bytes 104456 | tf_op jit(solution)/shard_map/ppermute | solution.py:219
  11.5 1.2 %collective-permute-start.5 = (bf16[8,2176]{1,0:T(8,128)(2,1)S(1)}, bf16[8,2176]{1,0:T(8,128)(2,1)S(1)}, u32[]{:S(2)}, u32[]{:S(2)}) collective-permute-start(bf16[8,2176]{1,0:T(8,128)(2,1)S(1)} %collective-permute-done.1.refs_2_), channel_id=1, source_target_pairs={{0,1},{1,0},{2,3},{3,2},{4,5},{5,4},{6,7},{7,6},{8,9},{9,8},{10,11... | collective-permute-start | bytes 104456 | tf_op jit(solution)/shard_map/ppermute | solution.py:219
  11.5 1.4 %collective-permute-start.4 = (bf16[8,2176]{1,0:T(8,128)(2,1)S(1)}, bf16[8,2176]{1,0:T(8,128)(2,1)S(1)}, u32[]{:S(2)}, u32[]{:S(2)}) collective-permute-start(bf16[8,2176]{1,0:T(8,128)(2,1)S(1)} %collective-permute-done.refs_1_), channel_id=1, source_target_pairs={{0,1},{1,0},{2,3},{3,2},{4,5},{5,4},{6,7},{7,6},{8,9},{9,8},{10,11... | collective-permute-start | bytes 104456 | tf_op jit(solution)/shard_map/ppermute | solution.py:219
  12.0 1.2 %collective-permute-start.6 = (bf16[8,2176]{1,0:T(8,128)(2,1)S(1)}, bf16[8,2176]{1,0:T(8,128)(2,1)S(1)}, u32[]{:S(2)}, u32[]{:S(2)}) collective-permute-start(bf16[8,2176]{1,0:T(8,128)(2,1)S(1)} %collective-permute-done.2.refs_3_), channel_id=1, source_target_pairs={{0,1},{1,0},{2,3},{3,2},{4,5},{5,4},{6,7},{7,6},{8,9},{9,8},{10,11... | collective-permute-start | bytes 104456 | tf_op jit(solution)/shard_map/ppermute | solution.py:219
  14.4 5.1 %collective-permute-start.8 = (bf16[16,1664]{1,0:T(8,128)(2,1)S(1)}, bf16[16,1664]{1,0:T(8,128)(2,1)S(1)}, u32[]{:S(2)}, u32[]{:S(2)}) collective-permute-start(bf16[16,1664]{1,0:T(8,128)(2,1)S(1)} %get-tuple-element.40), channel_id=1, source_target_pairs={{0,24},{8,16},{16,8},{24,0},{1,25},{9,17},{17,9},{25,1},{2,26},{10... | collective-permute-start | bytes 159752 | tf_op jit(solution)/shard_map/ppermute | solution.py:219
  16.9 4.1 %collective-permute-start.9 = (bf16[16,1664]{1,0:T(8,128)(2,1)S(1)}, bf16[16,1664]{1,0:T(8,128)(2,1)S(1)}, u32[]{:S(2)}, u32[]{:S(2)}) collective-permute-start(bf16[16,1664]{1,0:T(8,128)(2,1)S(1)} %get-tuple-element.41), channel_id=1, source_target_pairs={{0,16},{8,24},{16,0},{24,8},{1,17},{9,25},{17,1},{25,9},{2,18},{10... | collective-permute-start | bytes 159752 | tf_op jit(solution)/shard_map/ppermute | solution.py:219
  17.4 4.1 %collective-permute-start.10 = (bf16[16,1664]{1,0:T(8,128)(2,1)S(1)}, bf16[16,1664]{1,0:T(8,128)(2,1)S(1)}, u32[]{:S(2)}, u32[]{:S(2)}) collective-permute-start(bf16[16,1664]{1,0:T(8,128)(2,1)S(1)} %get-tuple-element.42), channel_id=1, source_target_pairs={{0,8},{8,0},{16,24},{24,16},{1,9},{9,1},{17,25},{25,17},{2,10},{10... | collective-permute-start | bytes 159752 | tf_op jit(solution)/shard_map/ppermute | solution.py:219
  21.7 4.9 %collective-permute-start.13 = (bf16[16,1152]{1,0:T(8,128)(2,1)S(1)}, bf16[16,1152]{1,0:T(8,128)(2,1)S(1)}, u32[]{:S(2)}, u32[]{:S(2)}) collective-permute-start(bf16[16,1152]{1,0:T(8,128)(2,1)S(1)} %shard_map.124.own_ref), channel_id=1, source_target_pairs={{0,24},{8,16},{16,8},{24,0},{1,25},{9,17},{17,9},{25,1},{2,26},{10... | collective-permute-start | bytes 110600 | tf_op jit(solution)/shard_map/ppermute | solution.py:219
  23.3 4.0 %collective-permute-start.12 = (bf16[16,1152]{1,0:T(8,128)(2,1)S(1)}, bf16[16,1152]{1,0:T(8,128)(2,1)S(1)}, u32[]{:S(2)}, u32[]{:S(2)}) collective-permute-start(bf16[16,1152]{1,0:T(8,128)(2,1)S(1)} %shard_map.124.own_ref), channel_id=1, source_target_pairs={{0,16},{8,24},{16,0},{24,8},{1,17},{9,25},{17,1},{25,9},{2,18},{10... | collective-permute-start | bytes 110600 | tf_op jit(solution)/shard_map/ppermute | solution.py:219
  23.8 4.0 %collective-permute-start.11 = (bf16[16,1152]{1,0:T(8,128)(2,1)S(1)}, bf16[16,1152]{1,0:T(8,128)(2,1)S(1)}, u32[]{:S(2)}, u32[]{:S(2)}) collective-permute-start(bf16[16,1152]{1,0:T(8,128)(2,1)S(1)} %shard_map.124.own_ref), channel_id=1, source_target_pairs={{0,8},{8,0},{16,24},{24,16},{1,9},{9,1},{17,25},{25,17},{2,10},{10... | collective-permute-start | bytes 110600 | tf_op jit(solution)/shard_map/ppermute | solution.py:219
  28.7 1.3 %collective-permute-start.14 = (bf16[32,1024]{1,0:T(8,128)(2,1)S(1)}, bf16[32,1024]{1,0:T(8,128)(2,1)S(1)}, u32[]{:S(2)}, u32[]{:S(2)}) collective-permute-start(bf16[32,1024]{1,0:T(8,128)(2,1)S(1)} %get-tuple-element.46), channel_id=1, source_target_pairs={{0,1},{1,0},{2,3},{3,2},{4,5},{5,4},{6,7},{7,6},{8,9},{9,8},{10,11... | collective-permute-start | bytes 196616 | tf_op jit(solution)/shard_map/ppermute | solution.py:219
  28.8 6.8 %collective-permute-start.18 = (f32[64,64]{1,0:T(8,128)S(1)}, f32[64,64]{1,0:T(8,128)S(1)}, u32[]{:S(2)}, u32[]{:S(2)}) collective-permute-start(f32[64,64]{1,0:T(8,128)S(1)} %get-tuple-element.52), channel_id=1, source_target_pairs={{0,1},{1,0},{2,3},{3,2},{4,5},{5,4},{6,7},{7,6},{8,9},{9,8},{10,11... | collective-permute-start | bytes 49160 | tf_op jit(solution)/shard_map/ppermute | solution.py:219
  30.0 6.5 %collective-permute-start.15 = (bf16[8,1024]{1,0:T(8,128)(2,1)S(1)}, bf16[8,1024]{1,0:T(8,128)(2,1)S(1)}, u32[]{:S(2)}, u32[]{:S(2)}) collective-permute-start(bf16[8,1024]{1,0:T(8,128)(2,1)S(1)} %get-tuple-element.48), channel_id=1, source_target_pairs={{0,6},{1,7},{2,4},{3,5},{4,2},{5,3},{6,0},{7,1},{8,14},{9,15},{10,... | collective-permute-start | bytes 49160 | tf_op jit(solution)/shard_map/ppermute | solution.py:219
  32.1 4.6 %collective-permute-start.16 = (bf16[8,1024]{1,0:T(8,128)(2,1)S(1)}, bf16[8,1024]{1,0:T(8,128)(2,1)S(1)}, u32[]{:S(2)}, u32[]{:S(2)}) collective-permute-start(bf16[8,1024]{1,0:T(8,128)(2,1)S(1)} %get-tuple-element.49), channel_id=1, source_target_pairs={{0,4},{1,5},{2,6},{3,7},{4,0},{5,1},{6,2},{7,3},{8,12},{9,13},{10,... | collective-permute-start | bytes 49160 | tf_op jit(solution)/shard_map/ppermute | solution.py:219
  32.1 4.6 %collective-permute-start.17 = (bf16[8,1024]{1,0:T(8,128)(2,1)S(1)}, bf16[8,1024]{1,0:T(8,128)(2,1)S(1)}, u32[]{:S(2)}, u32[]{:S(2)}) collective-permute-start(bf16[8,1024]{1,0:T(8,128)(2,1)S(1)} %get-tuple-element.50), channel_id=1, source_target_pairs={{0,2},{1,3},{2,0},{3,1},{4,6},{5,7},{6,4},{7,5},{8,10},{9,11},{10,... | collective-permute-start | bytes 49160 | tf_op jit(solution)/shard_map/ppermute | solution.py:219

commit v3 on v2

--- a/solution.py
+++ b/solution.py
@@ -193,9 +193,10 @@
 BF16 = jnp.bfloat16
 VMEM = pl.BlockSpec(memory_space=pltpu.VMEM)
 HBM = pl.BlockSpec(memory_space=pltpu.HBM)
-
-
-def local_call(body, outs, operands, scratch=(), flops=0, moved=0, far=0):
+LONG = 20_000_000_000
+
+
+def local_call(body, outs, operands, scratch=(), flops=0, moved=0, far=0, far_outs=0):
     operands = [
         pltpu.with_memory_space_constraint(array, pltpu.HBM) if k < far else array
         for k, array in enumerate(operands)
@@ -204,7 +205,7 @@
         body,
         out_shape=[jax.ShapeDtypeStruct(shape, kind) for shape, kind in outs],
         in_specs=[HBM] * far + [VMEM] * (len(operands) - far),
-        out_specs=[VMEM] * len(outs),
+        out_specs=[HBM] * far_outs + [VMEM] * (len(outs) - far_outs),
         scratch_shapes=list(scratch),
         cost_estimate=pl.CostEstimate(flops=flops, bytes_accessed=moved, transcendentals=0),
         compiler_params=pltpu.CompilerParams(vmem_limit_bytes=16 << 20),
@@ -273,28 +274,46 @@
     return (at == source).astype(BF16)
 
 
-def forward_body(topk, *refs):
-    blocks = [ref[...].astype(F32) for ref in refs[:-12]]
-    gate_ref, up_ref, down_ref, mine_ref, other_ref = refs[-12:-7]
-    own_ref, first_ref, second_ref, third_ref, x_ref, tag_ref, total = refs[-7:]
-    width = gate_ref.shape[0]
-    hidden = gate_ref.shape[1]
-    count = blocks[0].shape[0]
-    slots = count * len(blocks)
-    me = lax.axis_index("dp")
+def forward_body(*refs):
+    gate_ref, up_ref, down_ref, mine_ref, other_ref, total_ref = refs[-6:]
+    width, hidden = gate_ref.shape
+    blocks = [ref[...].astype(F32) for ref in refs[:-6]]
     upper = lax.rem(lax.axis_index("expert"), 2)
-    expert = (lax.axis_index("expert") // 2).astype(F32)
     x = jnp.concatenate([block[:, :width] for block in blocks], axis=0).astype(BF16)
     dy = jnp.concatenate([block[:, width : 2 * width] for block in blocks], axis=0).astype(BF16)
-    x_ref[...] = x
-    total[:, :hidden] = dot_plain(x, gate_ref[...])
-    total[:, hidden : 2 * hidden] = dot_plain(x, up_ref[...])
-    total[:, 2 * hidden : 3 * hidden] = product_trailing(dy, down_ref[...])
+    total_ref[:, :hidden] = dot_plain(x, gate_ref[...]).astype(BF16)
+    total_ref[:, hidden : 2 * hidden] = dot_plain(x, up_ref[...]).astype(BF16)
+    total_ref[:, 2 * hidden : 3 * hidden] = product_trailing(dy, down_ref[...]).astype(BF16)
     mine = product_trailing(x, mine_ref[...])
     other = product_trailing(x, other_ref[...])
     low = jnp.where(upper == 1, other, mine)
     high = jnp.where(upper == 1, mine, other)
-    total[:, 3 * hidden :] = jnp.concatenate([low, high], axis=1)
+    total_ref[:, 3 * hidden :] = jnp.concatenate([low, high], axis=1).astype(BF16)
+
+
+def forward_rest_body(*refs):
+    before_ref, total_ref, low_ref, high_ref = refs[-4:]
+    half = low_ref.shape[0]
+    forward_body(*refs[:-4], total_ref)
+    low_ref[...] = before_ref[:half]
+    high_ref[...] = before_ref[half:]
+
+
+def pair_body(high_ref, high_taken_ref, low_ref, low_taken_ref, low_out_ref, high_out_ref):
+    low = low_ref[...].astype(F32) + low_taken_ref[...].astype(F32)
+    high = high_ref[...].astype(F32) + high_taken_ref[...].astype(F32)
+    low_out_ref[...] = low.astype(BF16)
+    high_out_ref[...] = high.astype(BF16)
+
+
+def tags_body(topk, *refs):
+    x_ref, tag_ref = refs[-2:]
+    width = x_ref.shape[1]
+    blocks = [ref[...].astype(F32) for ref in refs[:-2]]
+    count = blocks[0].shape[0]
+    slots = count * len(blocks)
+    expert = (lax.axis_index("expert") // 2).astype(F32)
+    x_ref[...] = jnp.concatenate([block[:, :width] for block in blocks], axis=0).astype(BF16)
     eye = (
         lax.broadcasted_iota(jnp.int32, (count, 128), 0)
         == lax.broadcasted_iota(jnp.int32, (count, 128), 1)
@@ -309,10 +328,6 @@
     lane = lax.broadcasted_iota(jnp.int32, (slots, 128), 1)
     tenant = tags[:, 2 * topk : 2 * topk + 1]
     tag_ref[...] = jnp.where(lane == 0, prob, jnp.where(lane == 1, tenant, 0.0))
-    part = slots // 4
-    for k, ref in enumerate((own_ref, first_ref, second_ref, third_ref)):
-        start = pl.multiple_of((me ^ k) * part, part)
-        ref[...] = total[pl.ds(start, part), :].astype(ref.dtype)
 
 
 def lane_masks(tenant, shape, ranks):
@@ -324,18 +339,25 @@
     return is_gate, tenant_of.astype(F32) == tenant
 
 
-def activation_body(ranks, own_ref, third_ref, second_ref, first_ref, tag_ref, maps_ref, out_ref):
-    hidden = maps_ref.shape[1]
-    part = own_ref.shape[0]
-    me = lax.axis_index("dp")
-    total = (own_ref[...] + first_ref[...].astype(F32)) + (
-        second_ref[...].astype(F32) + third_ref[...].astype(F32)
-    )
-    tags = tag_ref[pl.ds(pl.multiple_of(me * part, part), part), :]
-    prob = tags[:, :1]
-    tenant = tags[:, 1:2]
+def backward_rows(
+    ranks,
+    rows,
+    total,
+    tag_ref,
+    gate_ref,
+    up_ref,
+    mine_ref,
+    other_ref,
+    maps_ref,
+    rows_ref,
+    back_ref,
+):
+    hidden = gate_ref.shape[1]
+    half = mine_ref.shape[0]
+    upper = lax.rem(lax.axis_index("expert"), 2)
+    tags = tag_ref[rows, :]
     low = total[:, 3 * hidden :]
-    is_gate, keep = lane_masks(tenant, low.shape, ranks)
+    is_gate, keep = lane_masks(tags[:, 1:2], low.shape, ranks)
     low = jnp.where(keep, low, 0.0).astype(BF16)
     low_wide = low.astype(F32)
     maps = maps_ref[...]
@@ -345,62 +367,53 @@
     up = total[:, hidden : 2 * hidden] + ADAPTER_SCALE * dot_plain(
         jnp.where(is_gate, 0.0, low_wide).astype(BF16), maps
     )
-    act = prob * total[:, 2 * hidden : 3 * hidden]
+    act = tags[:, :1] * total[:, 2 * hidden : 3 * hidden]
     sig = jax.nn.sigmoid(gate)
-    out_ref[:, :hidden] = (act * up * sig * (1.0 + gate * (1.0 - sig))).astype(BF16)
-    out_ref[:, hidden : 2 * hidden] = (act * gate * sig).astype(BF16)
-    out_ref[:, 2 * hidden :] = low
-
-
-def backward_body(
-    ranks,
-    own_ref,
-    first_ref,
-    second_ref,
-    third_ref,
-    gate_ref,
-    up_ref,
-    mine_ref,
-    other_ref,
-    maps_ref,
-    tag_ref,
-    keep_ref,
-    give_ref,
-    back_keep_ref,
-    back_give_ref,
-    rows_ref,
-):
-    part = own_ref.shape[0]
-    slots = 4 * part
-    hidden = gate_ref.shape[1]
-    me = lax.axis_index("dp")
-    upper = lax.rem(lax.axis_index("expert"), 2)
-    for k, ref in enumerate((own_ref, first_ref, second_ref, third_ref)):
-        rows_ref[pl.ds(pl.multiple_of((me ^ k) * part, part), part), :] = ref[...]
-    gate_grad = rows_ref[:, :hidden]
-    up_grad = rows_ref[:, hidden : 2 * hidden]
-    maps = maps_ref[...]
+    gate_grad = (act * up * sig * (1.0 + gate * (1.0 - sig))).astype(BF16)
+    up_grad = (act * gate * sig).astype(BF16)
+    rows_ref[:, :hidden] = gate_grad
+    rows_ref[:, hidden : 2 * hidden] = up_grad
+    rows_ref[:, 2 * hidden :] = low
     back_gate = product_trailing(gate_grad, maps)
     back_up = product_trailing(up_grad, maps)
-    is_gate, keep = lane_masks(tag_ref[:, 1:2], back_gate.shape, ranks)
     back = ADAPTER_SCALE * jnp.where(keep, jnp.where(is_gate, back_gate, back_up), 0.0)
-    half = back.shape[1] // 2
     low, high = back[:, :half], back[:, half:]
     mine = jnp.where(upper == 1, high, low)
     other = jnp.where(upper == 1, low, high)
-    back_keep_ref[...] = mine
-    back_give_ref[...] = other
+    back_ref[...] = jnp.concatenate([mine, other], axis=1)
     total = product_trailing(gate_grad, gate_ref[...])
     total += product_trailing(up_grad, up_ref[...])
     total += dot_plain(mine.astype(BF16), mine_ref[...])
-    total += dot_plain(other.astype(BF16), other_ref[...])
-    keep_ref[...] = total[: slots // 2]
-    give_ref[...] = total[slots // 2 :].astype(BF16)
+    return total + dot_plain(other.astype(BF16), other_ref[...])
+
+
+def backward_body(ranks, own_ref, first_ref, second_ref, third_ref, *refs):
+    give_ref, rows_ref, back_ref = refs[-3:]
+    count, lanes = back_ref.shape
+    width = give_ref.shape[1] - lanes // 2
+    total = (own_ref[...].astype(F32) + first_ref[...].astype(F32)) + (
+        second_ref[...].astype(F32) + third_ref[...].astype(F32)
+    )
+    total = backward_rows(ranks, slice(0, count), total, *refs[:-3], rows_ref, back_ref)
+    give_ref[:, :width] = total.astype(BF16)
+    give_ref[:, width:] = back_ref[:, lanes // 2 :].astype(BF16)
+
+
+def backward_rest_body(ranks, low_ref, low_taken_ref, high_ref, high_taken_ref, *refs):
+    keep_ref, back_give_ref, rows_ref, back_ref = refs[-4:]
+    count, lanes = back_ref.shape
+    low = low_ref[...].astype(F32) + low_taken_ref[...].astype(F32)
+    high = high_ref[...].astype(F32) + high_taken_ref[...].astype(F32)
+    total = jnp.concatenate([low, high], axis=0)
+    keep_ref[...] = backward_rows(
+        ranks, slice(count, 2 * count), total, *refs[:-4], rows_ref, back_ref
+    )
+    back_give_ref[...] = back_ref[:, lanes // 2 :]
 
 
 def join_body(keep_ref, taken_ref, own_ref, first_ref, second_ref, third_ref):
     count = own_ref.shape[0]
-    total = keep_ref[...] + taken_ref[...].astype(F32)
+    total = keep_ref[...] + taken_ref[:, : own_ref.shape[1]].astype(F32)
     for k, ref in enumerate((own_ref, first_ref, second_ref, third_ref)):
         ref[...] = total[k * count : (k + 1) * count].astype(ref.dtype)
 
@@ -412,22 +425,38 @@
     out_ref[...] = total.astype(BF16)
 
 
-def maps_grad_body(rows_ref, out_ref):
-    hidden = out_ref.shape[1]
-    lanes = out_ref.shape[0]
+def maps_grad_body(
+    rows_ref,
+    rest_rows_ref,
+    back_ref,
+    rest_back_ref,
+    taken_ref,
+    rest_taken_ref,
+    x_ref,
+    maps_out_ref,
+    inputs_out_ref,
+    maps,
+    inputs,
+    arrived,
+):
+    lanes, hidden = maps.shape
     half = lanes // 2
-    low = dot_plain(rows_ref[:, 2 * hidden :], rank_order(lanes, True)).astype(BF16)
-    out_ref[:half] = ADAPTER_SCALE * product_leading(low[:, :half], rows_ref[:, :hidden])
-    out_ref[half:] = ADAPTER_SCALE * product_leading(
-        low[:, half:], rows_ref[:, hidden : 2 * hidden]
-    )
-
-
-def input_maps_grad_body(keep_ref, taken_ref, x_ref, out_ref):
-    half = keep_ref.shape[0] // 2
-    taken = jnp.concatenate([taken_ref[half:], taken_ref[:half]], axis=0)
-    back = (keep_ref[...] + taken).astype(BF16)
-    out_ref[...] = product_leading(back, x_ref[...])
+    width = x_ref.shape[1]
+    copies = [
+        pltpu.make_async_copy(maps, maps_out_ref, arrived.at[0]),
+        pltpu.make_async_copy(inputs, inputs_out_ref, arrived.at[1]),
+    ]
+    taken = jnp.concatenate([rest_taken_ref[...], taken_ref[:, width:].astype(F32)], axis=0)
+    back = jnp.concatenate([back_ref[:, :half], rest_back_ref[:, :half]], axis=0)
+    inputs[...] = product_leading((back + taken).astype(BF16), x_ref[...])
+    copies[1].start()
+    rows = jnp.concatenate([rows_ref[...], rest_rows_ref[...]], axis=0)
+    low = dot_plain(rows[:, 2 * hidden :], rank_order(lanes, True)).astype(BF16)
+    maps[:half] = ADAPTER_SCALE * product_leading(low[:, :half], rows[:, :hidden])
+    maps[half:] = ADAPTER_SCALE * product_leading(low[:, half:], rows[:, hidden : 2 * hidden])
+    copies[0].start()
+    for copy in copies:
+        copy.wait()
 
 
 def dense_shards(
@@ -450,7 +479,6 @@
     ranks = rank // 2
     lanes = 2 * tenants * rank
     slots = devices * count
-    part = slots // 4
     mine_cols = adapter_input_maps[0].transpose(1, 2, 3, 0).reshape(lanes // 2, width)
     other_cols = swap(mine_cols, "expert", 1)
     (packed,) = local_call(
@@ -486,43 +514,49 @@
     )
     other_core = [swap(block, "expert", 1) for block in same_core]
     columns = 3 * hidden + lanes
-    own, first, second, third, x, tags = local_call(
-        functools.partial(forward_body, topk),
-        [
-            ((part, columns), F32),
-            ((part, columns), BF16),
-            ((part, columns), BF16),
-            ((part, columns), BF16),
-            ((slots, width), BF16),
-            ((slots, 128), F32),
-        ],
-        (*same_core, *other_core, gate, up, down, mine_cols, other_cols),
-        scratch=[pltpu.VMEM((slots, columns), F32)],
-        flops=2 * slots * width * columns,
-        moved=4 * width * columns,
-    )
-    third, second, first = swap(third, "dp", 3), swap(second, "dp", 2), swap(first, "dp", 1)
-    sums = [own, third, second, first]
-    (gradients,) = local_call(
-        functools.partial(activation_body, ranks),
-        [((part, 2 * hidden + lanes), BF16)],
-        (*sums, tags, maps),
-    )
-    gathered = [gradients] + [swap(gradients, "dp", k) for k in (1, 2, 3)]
-    keep, give, back_keep, back_give, rows = local_call(
+    weights = (gate, up, down, mine_cols, other_cols)
+    (before,) = local_call(
+        forward_body,
+        [((slots // 2, columns), BF16)],
+        (*same_core, *weights),
+        flops=slots * width * columns,
+    )
+    part = slots // 4
+    own, low, high = local_call(
+        forward_rest_body,
+        [((slots // 2, columns), BF16), ((part, columns), BF16), ((part, columns), BF16)],
+        (*other_core, *weights, before),
+        flops=slots * width * columns,
+    )
+    low_taken, high_taken = swap(low, "dp", 1), swap(high, "dp", 2)
+    sums = [own] + [swap(own, "dp", k) for k in (1, 2, 3)]
+    low, high = local_call(
+        pair_body,
+        [((part, columns), BF16)] * 2,
+        (high, high_taken, low, low_taken),
+        flops=LONG,
+    )
+    rest_sums = [low, swap(low, "dp", 2), high, swap(high, "dp", 1)]
+    x, tags = local_call(
+        functools.partial(tags_body, topk),
+        [((slots, width), BF16), ((slots, 128), F32)],
+        (*other_core, *same_core),
+    )
+    shared = (tags, gate, up, mine_cols, other_cols, maps)
+    outs = [((slots // 2, 2 * hidden + lanes), BF16), ((slots // 2, lanes), F32)]
+    give, rows, back = local_call(
         functools.partial(backward_body, ranks),
-        [
-            ((slots // 2, width), F32),
-            ((slots // 2, width), BF16),
-            ((slots, lanes // 2), F32),
-            ((slots, lanes // 2), F32),
-            ((slots, 2 * hidden + lanes), BF16),
-        ],
-        (*gathered, gate, up, mine_cols, other_cols, maps, tags),
-        flops=4 * slots * width * hidden,
-        moved=4 * width * hidden,
+        [((slots // 2, width + lanes // 2), BF16)] + outs,
+        (*sums, *shared),
+        flops=LONG,
     )
     taken = swap(give, "expert", 1)
+    keep, back_give, rest_rows, rest_back = local_call(
+        functools.partial(backward_rest_body, ranks),
+        [((slots // 2, width), F32), ((slots // 2, lanes // 2), F32)] + outs,
+        (*rest_sums, *shared),
+        flops=LONG,
+    )
     back_taken = swap(back_give, "expert", 1)
     own, first, second, third = local_call(
         join_body,
@@ -531,9 +565,17 @@
     )
     third, second = swap(third, "expert", 6), swap(second, "expert", 4)
     returned = [own, third, second, swap(first, "expert", 2)]
-    (maps_grad,) = local_call(maps_grad_body, [((lanes, hidden), F32)], (rows,))
-    (input_maps_grad,) = local_call(
-        input_maps_grad_body, [((lanes // 2, width), F32)], (back_keep, back_taken, x)
+    maps_grad, input_maps_grad = local_call(
+        maps_grad_body,
+        [((lanes, hidden), F32), ((lanes // 2, width), F32)],
+        (rows, rest_rows, back, rest_back, taken, back_taken, x),
+        scratch=[
+            pltpu.VMEM((lanes, hidden), F32),
+            pltpu.VMEM((lanes // 2, width), F32),
+            pltpu.SemaphoreType.DMA((2,)),
+        ],
+        far_outs=2,
+        flops=LONG,
     )
     (input_grad,) = local_call(finish_body, [((count, width), BF16)], returned)
     adapter_a_grad = (

time: 37.5 us -> 35.5 us (0.947)
  waiting for transfers between devices: 10.3 us -> 6.39 us
  Pallas kernels: 7.86 us -> 8.99 us
  starting transfers between devices: 18.5 us -> 19.1 us
    ppermute x19 -> x20, waiting for transfers between devices: 10.3 us -> 6.39 us  [swap(): lax.ppermute(array, axis, [(i, i ^ offset) for i in range(lax.axis_size(a...]
    pallas_call x9 -> x11, Pallas kernels: 7.86 us -> 8.99 us  [local_call(): pl.pallas_call(body, out_shape=[jax.ShapeDtypeStruct(shape, kind) for sha...]
    ppermute x19 -> x20, starting transfers between devices: 18.5 us -> 19.1 us  [swap(): lax.ppermute(array, axis, [(i, i ^ offset) for i in range(lax.axis_size(a...]
  transfers between devices with their start and end apart: 19 -> 20, of which waited for: 12 -> 5; matrix products, arithmetic and copies ran while one was open for 0% -> 0% of each run, Pallas kernels for 13% -> 21%
where the time goes in v3:
time: 35.5 us; the launch traced here: 35.2 us
  starting transfers between devices  19.1 us (54%)
  Pallas kernels  8.99 us (25%)
  waiting for transfers between devices  6.39 us (18%)
  between operations  0.75 us (2%)
    ppermute x20, starting transfers between devices, swap(): lax.ppermute(array, axis, [(i, i ^ offset) for i in range(lax.axis_size(a...  19.1 us
    pallas_call x11, Pallas kernels, local_call(): pl.pallas_call(body, out_shape=[jax.ShapeDtypeStruct(shape, kind) for sha...  8.99 us
    ppermute x20, waiting for transfers between devices, swap(): lax.ppermute(array, axis, [(i, i ^ offset) for i in range(lax.axis_size(a...  6.39 us
  transfers between devices with their start and end apart: 20, of which 5 were waited for; matrix products, arithmetic and copies ran while one was open for 0% of the time, Pallas kernels for 21%

profile of v3, /device:TPU:0, one launch (start us, length us, event | category | flops | bytes accessed | tf_op | source)
XLA Modules:
  0.0 35.2 jit_solution(1880149543961605611)
XLA Ops:
  0.6 0.5 %collective-permute-start.7 = (bf16[64,1024]{1,0:T(8,128)(2,1)}, bf16[64,1024]{1,0:T(8,128)(2,1)S(1)}, u32[]{:S(2)}, u32[]{:S(2)}) collective-permute-start(bf16[64,1024]{1,0:T(8,128)(2,1)} %bitcast.22), channel_id=1, source_target_pairs={{0,1},{1,0},{2,3},{3,2},{4,5},{5,4},{6,7},{7,6},{8,9},{9,8},{10,11... | collective-permute-start | bytes 393224 | tf_op jit(solution)/shard_map/ppermute | solution.py:220
  1.1 0.8 %shard_map.121.refs_0_.refs_4_ = bf16[8,2176]{1,0:T(8,128)(2,1)S(1)} custom-call(bf16[8,1024]{1,0:T(8,128)(2,1)} %x_ref.1, bf16[8,1024]{1,0:T(8,128)(2,1)} %dy_ref.1, s32[2,8]{1,0:T(2,128)} %bitcast.24, bf16[2,8]{1,0:T(2,128)(2,1)} %bitcast.25, s32[1,8]{1,0:T(1,128)} %bitcast.26), custom_call_target="tpu_custom_call" | custom-call | tf_op jit(solution)/shard_map/pallas_call | solution.py:204
  2.0 4.7 %collective-permute-start.5 = (bf16[8,2176]{1,0:T(8,128)(2,1)S(1)}, bf16[8,2176]{1,0:T(8,128)(2,1)S(1)}, u32[]{:S(2)}, u32[]{:S(2)}) collective-permute-start(bf16[8,2176]{1,0:T(8,128)(2,1)S(1)} %shard_map.121.refs_0_.refs_4_), channel_id=1, source_target_pairs={{0,6},{1,7},{2,4},{3,5},{4,2},{5,3},{6,0},{7,1},{8,14},{9,15},{10,... | collective-permute-start | bytes 104456 | tf_op jit(solution)/shard_map/ppermute | solution.py:220
  6.7 0.0 collective-permute-start.3
  6.7 0.6 %collective-permute-start.1 = (bf16[8,2176]{1,0:T(8,128)(2,1)S(1)}, bf16[8,2176]{1,0:T(8,128)(2,1)S(1)}, u32[]{:S(2)}, u32[]{:S(2)}) collective-permute-start(bf16[8,2176]{1,0:T(8,128)(2,1)S(1)} %shard_map.121.refs_0_.refs_4_), channel_id=1, source_target_pairs={{0,2},{1,3},{2,0},{3,1},{4,6},{5,7},{6,4},{7,5},{8,10},{9,11},{10,... | collective-permute-start | bytes 104456 | tf_op jit(solution)/shard_map/ppermute | solution.py:220
  7.3 0.0 collective-permute-start
  7.3 2.1 %shard_map.122 = (bf16[1024,512]{1,0:T(8,128)(2,1)S(1)}, bf16[1024,512]{1,0:T(8,128)(2,1)S(1)}, bf16[512,1024]{1,0:T(8,128)(2,1)S(1)}, bf16[64,1024]{1,0:T(8,128)(2,1)S(1)}, bf16[128,512]{1,0:T(8,128)(2,1)S(1)}) custom-call(bf16[1024,512]{1,0:T(8,128)(2,1)} %bitcast.18, bf16[1024,512]{1,0:T(8,128)(2,1)} %bitcast.19, bf16[512,1024]{1,0:T(8,128)(2,1)} %bitcast.20, ...), custom_call_target="tpu_custom_call" | custom-call | bytes 3407872 | tf_op jit(solution)/shard_map/pallas_call | solution.py:204
  9.4 0.0 collective-permute-done.5.refs_3_.refs_7_
  9.4 2.1 %collective-permute-done.3.refs_2_.refs_6_ = bf16[8,2176]{1,0:T(8,128)(2,1)S(1)} collective-permute-done((bf16[8,2176]{1,0:T(8,128)(2,1)S(1)}, bf16[8,2176]{1,0:T(8,128)(2,1)S(1)}, u32[]{:S(2)}, u32[]{:S(2)}) %collective-permute-start.3) | collective-permute-done | bytes 34848 | tf_op jit(solution)/shard_map/ppermute | solution.py:220
  11.5 0.0 collective-permute-start.4
  11.5 0.0 collective-permute-done.1.refs_1_.refs_5_
  11.5 0.5 %collective-permute-start.2 = (bf16[8,2176]{1,0:T(8,128)(2,1)S(1)}, bf16[8,2176]{1,0:T(8,128)(2,1)S(1)}, u32[]{:S(2)}, u32[]{:S(2)}) collective-permute-start(bf16[8,2176]{1,0:T(8,128)(2,1)S(1)} %collective-permute-done.1.refs_1_.refs_5_), channel_id=1, source_target_pairs={{0,1},{1,0},{2,3},{3,2},{4,5},{5,4},{6,7},{7,6},{8,9},{9,8},{10,11... | collective-permute-start | bytes 104456 | tf_op jit(solution)/shard_map/ppermute | solution.py:220
  12.0 0.0 collective-permute-start.6
  12.0 0.0 collective-permute-done.7.refs_8_.refs_4_
  12.0 0.9 %shard_map.123.refs_9_ = bf16[32,1664]{1,0:T(8,128)(2,1)S(1)} custom-call(bf16[8,2176]{1,0:T(8,128)(2,1)S(1)} %shard_map.121.refs_0_.refs_4_, bf16[8,2176]{1,0:T(8,128)(2,1)S(1)} %collective-permute-done.1.refs_1_.refs_5_, bf16[8,2176]{1,0:T(8,128)(2,1)S(1)} %collective-permute-done.3.refs_2_.refs_6_, ...), custom_call_target="tpu_custom_call" | custom-call | flops 109051904 | tf_op jit(solution)/shard_map/pallas_call | solution.py:204
  12.9 0.0 collective-permute-done.refs_0_
  12.9 0.0 collective-permute-done.4.refs_2_
  12.9 0.0 collective-permute-done.2.refs_1_
  13.0 0.3 collective-permute-done.6.refs_3_
  13.2 0.9 %shard_map.124 = (bf16[32,1664]{1,0:T(8,128)(2,1)S(1)}, bf16[16,1664]{1,0:T(8,128)(2,1)S(1)}, bf16[16,1664]{1,0:T(8,128)(2,1)S(1)}) custom-call(bf16[8,2176]{1,0:T(8,128)(2,1)S(1)} %collective-permute-done.refs_0_, bf16[8,2176]{1,0:T(8,128)(2,1)S(1)} %collective-permute-done.2.refs_1_, bf16[8,2176]{1,0:T(8,128)(2,1)S(1)} %collective-permute-done.4.refs_2_, ...), custom_call_target="tpu_custom_call" | custom-call | flops 109051904 | tf_op jit(solution)/shard_map/pallas_call | solution.py:204
  14.1 1.5 %collective-permute-start.8 = (bf16[16,1664]{1,0:T(8,128)(2,1)S(1)}, bf16[16,1664]{1,0:T(8,128)(2,1)S(1)}, u32[]{:S(2)}, u32[]{:S(2)}) collective-permute-start(bf16[16,1664]{1,0:T(8,128)(2,1)S(1)} %get-tuple-element.44.high_ref), channel_id=1, source_target_pairs={{0,16},{8,24},{16,0},{24,8},{1,17},{9,25},{17,1},{25,9},{2,18},{10... | collective-permute-start | bytes 159752 | tf_op jit(solution)/shard_map/ppermute | solution.py:220
  15.7 1.5 %collective-permute-start.9 = (bf16[16,1664]{1,0:T(8,128)(2,1)S(1)}, bf16[16,1664]{1,0:T(8,128)(2,1)S(1)}, u32[]{:S(2)}, u32[]{:S(2)}) collective-permute-start(bf16[16,1664]{1,0:T(8,128)(2,1)S(1)} %get-tuple-element.45.low_ref), channel_id=1, source_target_pairs={{0,8},{8,0},{16,24},{24,16},{1,9},{9,1},{17,25},{25,17},{2,10},{10... | collective-permute-start | bytes 159752 | tf_op jit(solution)/shard_map/ppermute | solution.py:220
  17.2 0.4 %shard_map.126 = (bf16[64,1024]{1,0:T(8,128)(2,1)S(1)}, f32[64,128]{1,0:T(8,128)S(1)}) custom-call(bf16[8,2176]{1,0:T(8,128)(2,1)S(1)} %collective-permute-done.refs_0_, bf16[8,2176]{1,0:T(8,128)(2,1)S(1)} %collective-permute-done.2.refs_1_, bf16[8,2176]{1,0:T(8,128)(2,1)S(1)} %collective-permute-done.4.refs_2_, ...), custom_call_target="tpu_custom_call" | custom-call | tf_op jit(solution)/shard_map/pallas_call | solution.py:204
  17.6 0.5 %collective-permute-start.14 = (bf16[32,1664]{1,0:T(8,128)(2,1)S(1)}, bf16[32,1664]{1,0:T(8,128)(2,1)S(1)}, u32[]{:S(2)}, u32[]{:S(2)}) collective-permute-start(bf16[32,1664]{1,0:T(8,128)(2,1)S(1)} %get-tuple-element.51.own_ref), channel_id=1, source_target_pairs={{0,24},{8,16},{16,8},{24,0},{1,25},{9,17},{17,9},{25,1},{2,26},{10... | collective-permute-start | bytes 319496 | tf_op jit(solution)/shard_map/ppermute | solution.py:220
  18.1 1.5 %collective-permute-start.13 = (bf16[32,1664]{1,0:T(8,128)(2,1)S(1)}, bf16[32,1664]{1,0:T(8,128)(2,1)S(1)}, u32[]{:S(2)}, u32[]{:S(2)}) collective-permute-start(bf16[32,1664]{1,0:T(8,128)(2,1)S(1)} %get-tuple-element.51.own_ref), channel_id=1, source_target_pairs={{0,16},{8,24},{16,0},{24,8},{1,17},{9,25},{17,1},{25,9},{2,18},{10... | collective-permute-start | bytes 319496 | tf_op jit(solution)/shard_map/ppermute | solution.py:220
  19.6 1.5 %collective-permute-start.12 = (bf16[32,1664]{1,0:T(8,128)(2,1)S(1)}, bf16[32,1664]{1,0:T(8,128)(2,1)S(1)}, u32[]{:S(2)}, u32[]{:S(2)}) collective-permute-start(bf16[32,1664]{1,0:T(8,128)(2,1)S(1)} %get-tuple-element.51.own_ref), channel_id=1, source_target_pairs={{0,8},{8,0},{16,24},{24,16},{1,9},{9,1},{17,25},{25,17},{2,10},{10... | collective-permute-start | bytes 319496 | tf_op jit(solution)/shard_map/ppermute | solution.py:220
  21.1 0.0 collective-permute-done.8.high_taken_ref
  21.1 0.0 collective-permute-done.9.low_taken_ref
  21.2 0.6 %collective-permute-start.10 = (bf16[16,1664]{1,0:T(8,128)(2,1)S(1)}, bf16[16,1664]{1,0:T(8,128)(2,1)S(1)}, u32[]{:S(2)}, u32[]{:S(2)}) collective-permute-start(bf16[16,1664]{1,0:T(8,128)(2,1)S(1)} %get-tuple-element.46.low_ref), channel_id=1, source_target_pairs={{0,16},{8,24},{16,0},{24,8},{1,17},{9,25},{17,1},{25,9},{2,18},{10... | collective-permute-start | bytes 159752 | tf_op jit(solution)/shard_map/ppermute | solution.py:220
  21.7 0.5 %collective-permute-start.11 = (bf16[16,1664]{1,0:T(8,128)(2,1)S(1)}, bf16[16,1664]{1,0:T(8,128)(2,1)S(1)}, u32[]{:S(2)}, u32[]{:S(2)}) collective-permute-start(bf16[16,1664]{1,0:T(8,128)(2,1)S(1)} %get-tuple-element.47.high_ref), channel_id=1, source_target_pairs={{0,8},{8,0},{16,24},{24,16},{1,9},{9,1},{17,25},{25,17},{2,10},{10... | collective-permute-start | bytes 159752 | tf_op jit(solution)/shard_map/ppermute | solution.py:220
  22.3 2.1 %collective-permute-done.14.third_ref = bf16[32,1664]{1,0:T(8,128)(2,1)S(1)} collective-permute-done((bf16[32,1664]{1,0:T(8,128)(2,1)S(1)}, bf16[32,1664]{1,0:T(8,128)(2,1)S(1)}, u32[]{:S(2)}, u32[]{:S(2)}) %collective-permute-start.14) | collective-permute-done | bytes 106528 | tf_op jit(solution)/shard_map/ppermute | solution.py:220
  24.4 0.8 %collective-permute-done.13.second_ref = bf16[32,1664]{1,0:T(8,128)(2,1)S(1)} collective-permute-done((bf16[32,1664]{1,0:T(8,128)(2,1)S(1)}, bf16[32,1664]{1,0:T(8,128)(2,1)S(1)}, u32[]{:S(2)}, u32[]{:S(2)}) %collective-permute-start.13) | collective-permute-done | bytes 106528 | tf_op jit(solution)/shard_map/ppermute | solution.py:220
  25.3 0.0 collective-permute-done.12.first_ref
  25.3 1.0 %shard_map.128 = (bf16[32,1088]{1,0:T(8,128)(2,1)S(1)}, bf16[32,1152]{1,0:T(8,128)(2,1)S(1)}, f32[32,128]{1,0:T(8,128)S(1)}) custom-call(bf16[32,1664]{1,0:T(8,128)(2,1)S(1)} %get-tuple-element.51.own_ref, bf16[32,1664]{1,0:T(8,128)(2,1)S(1)} %collective-permute-done.12.first_ref, bf16[32,1664]{1,0:T(8,128)(2,1)S(1)} %collective-permute-done.13.second_ref, ...), custom_call_target="tpu_custom_call" | custom-call | flops 20000000000 | tf_op jit(solution)/shard_map/pallas_call | solution.py:204
  26.2 0.1 collective-permute-start.15
  26.3 0.0 collective-permute-done.10.low_taken_ref
  26.3 0.0 collective-permute-done.11.high_taken_ref
  26.3 1.0 %shard_map.127 = (f32[32,1024]{1,0:T(8,128)S(1)}, f32[32,64]{1,0:T(8,128)S(1)}, bf16[32,1152]{1,0:T(8,128)(2,1)S(1)}, f32[32,128]{1,0:T(8,128)S(1)}) custom-call(bf16[16,1664]{1,0:T(8,128)(2,1)S(1)} %get-tuple-element.46.low_ref, bf16[16,1664]{1,0:T(8,128)(2,1)S(1)} %collective-permute-done.10.low_taken_ref, ...), custom_call_target="tpu_custom_call" | custom-call | flops 20000000000 | tf_op jit(solution)/shard_map/pallas_call | solution.py:204
  27.3 0.5 %collective-permute-start.19 = (f32[32,64]{1,0:T(8,128)S(1)}, f32[32,64]{1,0:T(8,128)S(1)}, u32[]{:S(2)}, u32[]{:S(2)}) collective-permute-start(f32[32,64]{1,0:T(8,128)S(1)} %get-tuple-element.61), channel_id=1, source_target_pairs={{0,1},{1,0},{2,3},{3,2},{4,5},{5,4},{6,7},{7,6},{8,9},{9,8},{10,11... | collective-permute-start | bytes 24584 | tf_op jit(solution)/shard_map/ppermute | solution.py:220
  27.9 0.0 collective-permute-done.15.taken_ref
  27.9 2.1 %collective-permute-start.16 = (bf16[8,1024]{1,0:T(8,128)(2,1)S(1)}, bf16[8,1024]{1,0:T(8,128)(2,1)S(1)}, u32[]{:S(2)}, u32[]{:S(2)}) collective-permute-start(bf16[8,1024]{1,0:T(8,128)(2,1)S(1)} %get-tuple-element.54), channel_id=1, source_target_pairs={{0,6},{1,7},{2,4},{3,5},{4,2},{5,3},{6,0},{7,1},{8,14},{9,15},{10,... | collective-permute-start | bytes 49160 | tf_op jit(solution)/shard_map/ppermute | solution.py:220
  30.0 0.0 collective-permute-start.17
  30.0 2.4 %collective-permute-start.18 = (bf16[8,1024]{1,0:T(8,128)(2,1)S(1)}, bf16[8,1024]{1,0:T(8,128)(2,1)S(1)}, u32[]{:S(2)}, u32[]{:S(2)}) collective-permute-start(bf16[8,1024]{1,0:T(8,128)(2,1)S(1)} %get-tuple-element.56), channel_id=1, source_target_pairs={{0,2},{1,3},{2,0},{3,1},{4,6},{5,7},{6,4},{7,5},{8,10},{9,11},{10,... | collective-permute-start | bytes 49160 | tf_op jit(solution)/shard_map/ppermute | solution.py:220
  32.3 0.0 collective-permute-done.19.rest_taken_ref
  32.3 1.2 %shard_map.131 = (f32[128,512]{1,0:T(8,128)}, f32[64,1024]{1,0:T(8,128)}) custom-call(bf16[32,1152]{1,0:T(8,128)(2,1)S(1)} %get-tuple-element.57.rows_ref, bf16[32,1152]{1,0:T(8,128)(2,1)S(1)} %get-tuple-element.58.rest_rows_ref, f32[32,128]{1,0:T(8,128)S(1)} %get-tuple-element.59.back_ref, f32[32,128]{1,0:T(8,128)S(1)} %get-tuple-element.60.rest_back_ref, ...), custom_call_target="tpu_custom_call" | custom-call | flops 20000000000 | tf_op jit(solution)/shard_map/pallas_call | solution.py:204
  33.6 0.0 collective-permute-done.16.third_ref
  33.6 1.0 %collective-permute-done.17.second_ref = bf16[8,1024]{1,0:T(8,128)(2,1)S(1)} collective-permute-done((bf16[8,1024]{1,0:T(8,128)(2,1)S(1)}, bf16[8,1024]{1,0:T(8,128)(2,1)S(1)}, u32[]{:S(2)}, u32[]{:S(2)}) %collective-permute-start.17) | collective-permute-done | bytes 16416 | tf_op jit(solution)/shard_map/ppermute | solution.py:220
  34.6 0.6 %shard_map.130 = bf16[8,1024]{1,0:T(8,128)(2,1)} custom-call(f32[8,1024]{1,0:T(8,128)S(1)} %get-tuple-element.53.own_ref, bf16[8,1024]{1,0:T(8,128)(2,1)S(1)} %collective-permute-done.16.third_ref, bf16[8,1024]{1,0:T(8,128)(2,1)S(1)} %collective-permute-done.17.second_ref, bf16[8,1024]{1,0:T(8,128)(2,1)S(1)} %collective-permute-done.18.first_ref), custom_call_target="tpu_custom_call" | custom-call | tf_op jit(solution)/shard_map/pallas_call | solution.py:204
  (3 shorter events, 0.0 us)
Async XLA Ops:
  0.6 11.4 %collective-permute-start.7 = (bf16[64,1024]{1,0:T(8,128)(2,1)}, bf16[64,1024]{1,0:T(8,128)(2,1)S(1)}, u32[]{:S(2)}, u32[]{:S(2)}) collective-permute-start(bf16[64,1024]{1,0:T(8,128)(2,1)} %bitcast.22), channel_id=1, source_target_pairs={{0,1},{1,0},{2,3},{3,2},{4,5},{5,4},{6,7},{7,6},{8,9},{9,8},{10,11... | collective-permute-start | bytes 393224 | tf_op jit(solution)/shard_map/ppermute | solution.py:220
  2.0 7.4 %collective-permute-start.5 = (bf16[8,2176]{1,0:T(8,128)(2,1)S(1)}, bf16[8,2176]{1,0:T(8,128)(2,1)S(1)}, u32[]{:S(2)}, u32[]{:S(2)}) collective-permute-start(bf16[8,2176]{1,0:T(8,128)(2,1)S(1)} %shard_map.121.refs_0_.refs_4_), channel_id=1, source_target_pairs={{0,6},{1,7},{2,4},{3,5},{4,2},{5,3},{6,0},{7,1},{8,14},{9,15},{10,... | collective-permute-start | bytes 104456 | tf_op jit(solution)/shard_map/ppermute | solution.py:220
  6.7 4.8 %collective-permute-start.3 = (bf16[8,2176]{1,0:T(8,128)(2,1)S(1)}, bf16[8,2176]{1,0:T(8,128)(2,1)S(1)}, u32[]{:S(2)}, u32[]{:S(2)}) collective-permute-start(bf16[8,2176]{1,0:T(8,128)(2,1)S(1)} %shard_map.121.refs_0_.refs_4_), channel_id=1, source_target_pairs={{0,4},{1,5},{2,6},{3,7},{4,0},{5,1},{6,2},{7,3},{8,12},{9,13},{10,... | collective-permute-start | bytes 104456 | tf_op jit(solution)/shard_map/ppermute | solution.py:220
  6.7 4.8 %collective-permute-start.1 = (bf16[8,2176]{1,0:T(8,128)(2,1)S(1)}, bf16[8,2176]{1,0:T(8,128)(2,1)S(1)}, u32[]{:S(2)}, u32[]{:S(2)}) collective-permute-start(bf16[8,2176]{1,0:T(8,128)(2,1)S(1)} %shard_map.121.refs_0_.refs_4_), channel_id=1, source_target_pairs={{0,2},{1,3},{2,0},{3,1},{4,6},{5,7},{6,4},{7,5},{8,10},{9,11},{10,... | collective-permute-start | bytes 104456 | tf_op jit(solution)/shard_map/ppermute | solution.py:220
  7.3 5.6 %collective-permute-start = (bf16[8,2176]{1,0:T(8,128)(2,1)S(1)}, bf16[8,2176]{1,0:T(8,128)(2,1)S(1)}, u32[]{:S(2)}, u32[]{:S(2)}) collective-permute-start(bf16[8,2176]{1,0:T(8,128)(2,1)S(1)} %shard_map.121.refs_0_.refs_4_), channel_id=1, source_target_pairs={{0,1},{1,0},{2,3},{3,2},{4,5},{5,4},{6,7},{7,6},{8,9},{9,8},{10,11... | collective-permute-start | bytes 104456 | tf_op jit(solution)/shard_map/ppermute | solution.py:220
  11.5 1.4 %collective-permute-start.4 = (bf16[8,2176]{1,0:T(8,128)(2,1)S(1)}, bf16[8,2176]{1,0:T(8,128)(2,1)S(1)}, u32[]{:S(2)}, u32[]{:S(2)}) collective-permute-start(bf16[8,2176]{1,0:T(8,128)(2,1)S(1)} %collective-permute-done.3.refs_2_.refs_6_), channel_id=1, source_target_pairs={{0,1},{1,0},{2,3},{3,2},{4,5},{5,4},{6,7},{7,6},{8,9},{9,8},{10,11... | collective-permute-start | bytes 104456 | tf_op jit(solution)/shard_map/ppermute | solution.py:220
  11.5 1.4 %collective-permute-start.2 = (bf16[8,2176]{1,0:T(8,128)(2,1)S(1)}, bf16[8,2176]{1,0:T(8,128)(2,1)S(1)}, u32[]{:S(2)}, u32[]{:S(2)}) collective-permute-start(bf16[8,2176]{1,0:T(8,128)(2,1)S(1)} %collective-permute-done.1.refs_1_.refs_5_), channel_id=1, source_target_pairs={{0,1},{1,0},{2,3},{3,2},{4,5},{5,4},{6,7},{7,6},{8,9},{9,8},{10,11... | collective-permute-start | bytes 104456 | tf_op jit(solution)/shard_map/ppermute | solution.py:220
  12.0 1.2 %collective-permute-start.6 = (bf16[8,2176]{1,0:T(8,128)(2,1)S(1)}, bf16[8,2176]{1,0:T(8,128)(2,1)S(1)}, u32[]{:S(2)}, u32[]{:S(2)}) collective-permute-start(bf16[8,2176]{1,0:T(8,128)(2,1)S(1)} %collective-permute-done.5.refs_3_.refs_7_), channel_id=1, source_target_pairs={{0,1},{1,0},{2,3},{3,2},{4,5},{5,4},{6,7},{7,6},{8,9},{9,8},{10,11... | collective-permute-start | bytes 104456 | tf_op jit(solution)/shard_map/ppermute | solution.py:220
  14.1 7.0 %collective-permute-start.8 = (bf16[16,1664]{1,0:T(8,128)(2,1)S(1)}, bf16[16,1664]{1,0:T(8,128)(2,1)S(1)}, u32[]{:S(2)}, u32[]{:S(2)}) collective-permute-start(bf16[16,1664]{1,0:T(8,128)(2,1)S(1)} %get-tuple-element.44.high_ref), channel_id=1, source_target_pairs={{0,16},{8,24},{16,0},{24,8},{1,17},{9,25},{17,1},{25,9},{2,18},{10... | collective-permute-start | bytes 159752 | tf_op jit(solution)/shard_map/ppermute | solution.py:220
  15.7 5.5 %collective-permute-start.9 = (bf16[16,1664]{1,0:T(8,128)(2,1)S(1)}, bf16[16,1664]{1,0:T(8,128)(2,1)S(1)}, u32[]{:S(2)}, u32[]{:S(2)}) collective-permute-start(bf16[16,1664]{1,0:T(8,128)(2,1)S(1)} %get-tuple-element.45.low_ref), channel_id=1, source_target_pairs={{0,8},{8,0},{16,24},{24,16},{1,9},{9,1},{17,25},{25,17},{2,10},{10... | collective-permute-start | bytes 159752 | tf_op jit(solution)/shard_map/ppermute | solution.py:220
  17.6 6.8 %collective-permute-start.14 = (bf16[32,1664]{1,0:T(8,128)(2,1)S(1)}, bf16[32,1664]{1,0:T(8,128)(2,1)S(1)}, u32[]{:S(2)}, u32[]{:S(2)}) collective-permute-start(bf16[32,1664]{1,0:T(8,128)(2,1)S(1)} %get-tuple-element.51.own_ref), channel_id=1, source_target_pairs={{0,24},{8,16},{16,8},{24,0},{1,25},{9,17},{17,9},{25,1},{2,26},{10... | collective-permute-start | bytes 319496 | tf_op jit(solution)/shard_map/ppermute | solution.py:220
  18.1 7.1 %collective-permute-start.13 = (bf16[32,1664]{1,0:T(8,128)(2,1)S(1)}, bf16[32,1664]{1,0:T(8,128)(2,1)S(1)}, u32[]{:S(2)}, u32[]{:S(2)}) collective-permute-start(bf16[32,1664]{1,0:T(8,128)(2,1)S(1)} %get-tuple-element.51.own_ref), channel_id=1, source_target_pairs={{0,16},{8,24},{16,0},{24,8},{1,17},{9,25},{17,1},{25,9},{2,18},{10... | collective-permute-start | bytes 319496 | tf_op jit(solution)/shard_map/ppermute | solution.py:220
  19.6 5.6 %collective-permute-start.12 = (bf16[32,1664]{1,0:T(8,128)(2,1)S(1)}, bf16[32,1664]{1,0:T(8,128)(2,1)S(1)}, u32[]{:S(2)}, u32[]{:S(2)}) collective-permute-start(bf16[32,1664]{1,0:T(8,128)(2,1)S(1)} %get-tuple-element.51.own_ref), channel_id=1, source_target_pairs={{0,8},{8,0},{16,24},{24,16},{1,9},{9,1},{17,25},{25,17},{2,10},{10... | collective-permute-start | bytes 319496 | tf_op jit(solution)/shard_map/ppermute | solution.py:220
  21.2 5.2 %collective-permute-start.10 = (bf16[16,1664]{1,0:T(8,128)(2,1)S(1)}, bf16[16,1664]{1,0:T(8,128)(2,1)S(1)}, u32[]{:S(2)}, u32[]{:S(2)}) collective-permute-start(bf16[16,1664]{1,0:T(8,128)(2,1)S(1)} %get-tuple-element.46.low_ref), channel_id=1, source_target_pairs={{0,16},{8,24},{16,0},{24,8},{1,17},{9,25},{17,1},{25,9},{2,18},{10... | collective-permute-start | bytes 159752 | tf_op jit(solution)/shard_map/ppermute | solution.py:220
  21.7 4.6 %collective-permute-start.11 = (bf16[16,1664]{1,0:T(8,128)(2,1)S(1)}, bf16[16,1664]{1,0:T(8,128)(2,1)S(1)}, u32[]{:S(2)}, u32[]{:S(2)}) collective-permute-start(bf16[16,1664]{1,0:T(8,128)(2,1)S(1)} %get-tuple-element.47.high_ref), channel_id=1, source_target_pairs={{0,8},{8,0},{16,24},{24,16},{1,9},{9,1},{17,25},{25,17},{2,10},{10... | collective-permute-start | bytes 159752 | tf_op jit(solution)/shard_map/ppermute | solution.py:220
  26.2 1.6 %collective-permute-start.15 = (bf16[32,1088]{1,0:T(8,128)(2,1)S(1)}, bf16[32,1088]{1,0:T(8,128)(2,1)S(1)}, u32[]{:S(2)}, u32[]{:S(2)}) collective-permute-start(bf16[32,1088]{1,0:T(8,128)(2,1)S(1)} %get-tuple-element.52), channel_id=1, source_target_pairs={{0,1},{1,0},{2,3},{3,2},{4,5},{5,4},{6,7},{7,6},{8,9},{9,8},{10,11... | collective-permute-start | bytes 208904 | tf_op jit(solution)/shard_map/ppermute | solution.py:220
  27.3 5.0 %collective-permute-start.19 = (f32[32,64]{1,0:T(8,128)S(1)}, f32[32,64]{1,0:T(8,128)S(1)}, u32[]{:S(2)}, u32[]{:S(2)}) collective-permute-start(f32[32,64]{1,0:T(8,128)S(1)} %get-tuple-element.61), channel_id=1, source_target_pairs={{0,1},{1,0},{2,3},{3,2},{4,5},{5,4},{6,7},{7,6},{8,9},{9,8},{10,11... | collective-permute-start | bytes 24584 | tf_op jit(solution)/shard_map/ppermute | solution.py:220
  27.9 5.7 %collective-permute-start.16 = (bf16[8,1024]{1,0:T(8,128)(2,1)S(1)}, bf16[8,1024]{1,0:T(8,128)(2,1)S(1)}, u32[]{:S(2)}, u32[]{:S(2)}) collective-permute-start(bf16[8,1024]{1,0:T(8,128)(2,1)S(1)} %get-tuple-element.54), channel_id=1, source_target_pairs={{0,6},{1,7},{2,4},{3,5},{4,2},{5,3},{6,0},{7,1},{8,14},{9,15},{10,... | collective-permute-start | bytes 49160 | tf_op jit(solution)/shard_map/ppermute | solution.py:220
  30.0 4.6 %collective-permute-start.17 = (bf16[8,1024]{1,0:T(8,128)(2,1)S(1)}, bf16[8,1024]{1,0:T(8,128)(2,1)S(1)}, u32[]{:S(2)}, u32[]{:S(2)}) collective-permute-start(bf16[8,1024]{1,0:T(8,128)(2,1)S(1)} %get-tuple-element.55), channel_id=1, source_target_pairs={{0,4},{1,5},{2,6},{3,7},{4,0},{5,1},{6,2},{7,3},{8,12},{9,13},{10,... | collective-permute-start | bytes 49160 | tf_op jit(solution)/shard_map/ppermute | solution.py:220
  30.0 4.6 %collective-permute-start.18 = (bf16[8,1024]{1,0:T(8,128)(2,1)S(1)}, bf16[8,1024]{1,0:T(8,128)(2,1)S(1)}, u32[]{:S(2)}, u32[]{:S(2)}) collective-permute-start(bf16[8,1024]{1,0:T(8,128)(2,1)S(1)} %get-tuple-element.56), channel_id=1, source_target_pairs={{0,2},{1,3},{2,0},{3,1},{4,6},{5,7},{6,4},{7,5},{8,10},{9,11},{10,... | collective-permute-start | bytes 49160 | tf_op jit(solution)/shard_map/ppermute | solution.py:220

commit v4 on v3

--- a/solution.py
+++ b/solution.py
@@ -292,18 +292,13 @@
 
 
 def forward_rest_body(*refs):
-    before_ref, total_ref, low_ref, high_ref = refs[-4:]
-    half = low_ref.shape[0]
-    forward_body(*refs[:-4], total_ref)
-    low_ref[...] = before_ref[:half]
-    high_ref[...] = before_ref[half:]
-
-
-def pair_body(high_ref, high_taken_ref, low_ref, low_taken_ref, low_out_ref, high_out_ref):
-    low = low_ref[...].astype(F32) + low_taken_ref[...].astype(F32)
-    high = high_ref[...].astype(F32) + high_taken_ref[...].astype(F32)
-    low_out_ref[...] = low.astype(BF16)
-    high_out_ref[...] = high.astype(BF16)
+    before_ref, total_ref, mine_total_ref = refs[-3:]
+    forward_body(*refs[:-3], total_ref)
+    mine_total_ref[...] = before_ref[...]
+
+
+def pair_body(own_ref, taken_ref, out_ref):
+    out_ref[...] = (own_ref[...].astype(F32) + taken_ref[...].astype(F32)).astype(BF16)
 
 
 def tags_body(topk, *refs):
@@ -387,7 +382,7 @@
     return total + dot_plain(other.astype(BF16), other_ref[...])
 
 
-def backward_body(ranks, own_ref, first_ref, second_ref, third_ref, *refs):
+def backward_body(ranks, own_ref, second_ref, first_ref, third_ref, *refs):
     give_ref, rows_ref, back_ref = refs[-3:]
     count, lanes = back_ref.shape
     width = give_ref.shape[1] - lanes // 2
@@ -399,12 +394,10 @@
     give_ref[:, width:] = back_ref[:, lanes // 2 :].astype(BF16)
 
 
-def backward_rest_body(ranks, low_ref, low_taken_ref, high_ref, high_taken_ref, *refs):
+def backward_rest_body(ranks, own_ref, pair_ref, *refs):
     keep_ref, back_give_ref, rows_ref, back_ref = refs[-4:]
     count, lanes = back_ref.shape
-    low = low_ref[...].astype(F32) + low_taken_ref[...].astype(F32)
-    high = high_ref[...].astype(F32) + high_taken_ref[...].astype(F32)
-    total = jnp.concatenate([low, high], axis=0)
+    total = own_ref[...].astype(F32) + pair_ref[...].astype(F32)
     keep_ref[...] = backward_rows(
         ranks, slice(count, 2 * count), total, *refs[:-4], rows_ref, back_ref
     )
@@ -521,22 +514,20 @@
         (*same_core, *weights),
         flops=slots * width * columns,
     )
-    part = slots // 4
-    own, low, high = local_call(
+    own, mine = local_call(
         forward_rest_body,
-        [((slots // 2, columns), BF16), ((part, columns), BF16), ((part, columns), BF16)],
+        [((slots // 2, columns), BF16)] * 2,
         (*other_core, *weights, before),
         flops=slots * width * columns,
     )
-    low_taken, high_taken = swap(low, "dp", 1), swap(high, "dp", 2)
-    sums = [own] + [swap(own, "dp", k) for k in (1, 2, 3)]
-    low, high = local_call(
+    sums = [own] + [swap(own, "dp", k) for k in (2, 1, 3)]
+    (pair,) = local_call(
         pair_body,
-        [((part, columns), BF16)] * 2,
-        (high, high_taken, low, low_taken),
+        [((slots // 2, columns), BF16)],
+        (mine, swap(mine, "dp", 2)),
         flops=LONG,
     )
-    rest_sums = [low, swap(low, "dp", 2), high, swap(high, "dp", 1)]
+    rest_sums = [pair, swap(pair, "dp", 1)]
     x, tags = local_call(
         functools.partial(tags_body, topk),
         [((slots, width), BF16), ((slots, 128), F32)],

time: 35.5 us -> 34.4 us (0.969)
  starting transfers between devices: 19.1 us -> 17.8 us
    ppermute x20 -> x18, starting transfers between devices: 19.1 us -> 17.8 us  [swap(): lax.ppermute(array, axis, [(i, i ^ offset) for i in range(lax.axis_size(a...]
    ppermute x20 -> x18, waiting for transfers between devices: 6.39 us -> 6.7 us  [swap(): lax.ppermute(array, axis, [(i, i ^ offset) for i in range(lax.axis_size(a...]
  transfers between devices with their start and end apart: 20 -> 18, of which waited for: 5 -> 7; matrix products, arithmetic and copies ran while one was open for 0% -> 0% of each run, Pallas kernels for 21% -> 22%
where the time goes in v4:
time: 34.4 us; the launch traced here: 34.2 us
  starting transfers between devices  17.8 us (52%)
  Pallas kernels  8.99 us (26%)
  waiting for transfers between devices  6.7 us (19%)
  between operations  0.73 us (2%)
    ppermute x18, starting transfers between devices, swap(): lax.ppermute(array, axis, [(i, i ^ offset) for i in range(lax.axis_size(a...  17.8 us
    pallas_call x11, Pallas kernels, local_call(): pl.pallas_call(body, out_shape=[jax.ShapeDtypeStruct(shape, kind) for sha...  8.99 us
    ppermute x18, waiting for transfers between devices, swap(): lax.ppermute(array, axis, [(i, i ^ offset) for i in range(lax.axis_size(a...  6.7 us
  transfers between devices with their start and end apart: 18, of which 7 were waited for; matrix products, arithmetic and copies ran while one was open for 0% of the time, Pallas kernels for 22%

profile of v4, /device:TPU:0, one launch (start us, length us, event | category | flops | bytes accessed | tf_op | source)
XLA Modules:
  0.0 34.2 jit_solution(5301290194518740443)
XLA Ops:
  0.6 0.5 %collective-permute-start.7 = (bf16[64,1024]{1,0:T(8,128)(2,1)}, bf16[64,1024]{1,0:T(8,128)(2,1)S(1)}, u32[]{:S(2)}, u32[]{:S(2)}) collective-permute-start(bf16[64,1024]{1,0:T(8,128)(2,1)} %bitcast.22), channel_id=1, source_target_pairs={{0,1},{1,0},{2,3},{3,2},{4,5},{5,4},{6,7},{7,6},{8,9},{9,8},{10,11... | collective-permute-start | bytes 393224 | tf_op jit(solution)/shard_map/ppermute | solution.py:220
  1.1 0.8 %shard_map.121.refs_0_.refs_4_ = bf16[8,2176]{1,0:T(8,128)(2,1)S(1)} custom-call(bf16[8,1024]{1,0:T(8,128)(2,1)} %x_ref.1, bf16[8,1024]{1,0:T(8,128)(2,1)} %dy_ref.1, s32[2,8]{1,0:T(2,128)} %bitcast.24, bf16[2,8]{1,0:T(2,128)(2,1)} %bitcast.25, s32[1,8]{1,0:T(1,128)} %bitcast.26), custom_call_target="tpu_custom_call" | custom-call | tf_op jit(solution)/shard_map/pallas_call | solution.py:204
  2.0 4.7 %collective-permute-start.5 = (bf16[8,2176]{1,0:T(8,128)(2,1)S(1)}, bf16[8,2176]{1,0:T(8,128)(2,1)S(1)}, u32[]{:S(2)}, u32[]{:S(2)}) collective-permute-start(bf16[8,2176]{1,0:T(8,128)(2,1)S(1)} %shard_map.121.refs_0_.refs_4_), channel_id=1, source_target_pairs={{0,6},{1,7},{2,4},{3,5},{4,2},{5,3},{6,0},{7,1},{8,14},{9,15},{10,... | collective-permute-start | bytes 104456 | tf_op jit(solution)/shard_map/ppermute | solution.py:220
  6.7 0.0 collective-permute-start.3
  6.7 0.6 %collective-permute-start.1 = (bf16[8,2176]{1,0:T(8,128)(2,1)S(1)}, bf16[8,2176]{1,0:T(8,128)(2,1)S(1)}, u32[]{:S(2)}, u32[]{:S(2)}) collective-permute-start(bf16[8,2176]{1,0:T(8,128)(2,1)S(1)} %shard_map.121.refs_0_.refs_4_), channel_id=1, source_target_pairs={{0,2},{1,3},{2,0},{3,1},{4,6},{5,7},{6,4},{7,5},{8,10},{9,11},{10,... | collective-permute-start | bytes 104456 | tf_op jit(solution)/shard_map/ppermute | solution.py:220
  7.3 0.0 collective-permute-start
  7.3 2.1 %shard_map.122 = (bf16[1024,512]{1,0:T(8,128)(2,1)S(1)}, bf16[1024,512]{1,0:T(8,128)(2,1)S(1)}, bf16[512,1024]{1,0:T(8,128)(2,1)S(1)}, bf16[64,1024]{1,0:T(8,128)(2,1)S(1)}, bf16[128,512]{1,0:T(8,128)(2,1)S(1)}) custom-call(bf16[1024,512]{1,0:T(8,128)(2,1)} %bitcast.18, bf16[1024,512]{1,0:T(8,128)(2,1)} %bitcast.19, bf16[512,1024]{1,0:T(8,128)(2,1)} %bitcast.20, ...), custom_call_target="tpu_custom_call" | custom-call | bytes 3407872 | tf_op jit(solution)/shard_map/pallas_call | solution.py:204
  9.4 0.0 collective-permute-done.5.refs_3_.refs_7_
  9.4 2.1 %collective-permute-done.3.refs_2_.refs_6_ = bf16[8,2176]{1,0:T(8,128)(2,1)S(1)} collective-permute-done((bf16[8,2176]{1,0:T(8,128)(2,1)S(1)}, bf16[8,2176]{1,0:T(8,128)(2,1)S(1)}, u32[]{:S(2)}, u32[]{:S(2)}) %collective-permute-start.3) | collective-permute-done | bytes 34848 | tf_op jit(solution)/shard_map/ppermute | solution.py:220
  11.5 0.0 collective-permute-start.4
  11.5 0.0 collective-permute-done.1.refs_1_.refs_5_
  11.5 0.5 %collective-permute-start.2 = (bf16[8,2176]{1,0:T(8,128)(2,1)S(1)}, bf16[8,2176]{1,0:T(8,128)(2,1)S(1)}, u32[]{:S(2)}, u32[]{:S(2)}) collective-permute-start(bf16[8,2176]{1,0:T(8,128)(2,1)S(1)} %collective-permute-done.1.refs_1_.refs_5_), channel_id=1, source_target_pairs={{0,1},{1,0},{2,3},{3,2},{4,5},{5,4},{6,7},{7,6},{8,9},{9,8},{10,11... | collective-permute-start | bytes 104456 | tf_op jit(solution)/shard_map/ppermute | solution.py:220
  12.0 0.0 collective-permute-start.6
  12.0 0.0 collective-permute-done.7.refs_8_.refs_4_
  12.0 0.9 %shard_map.123.refs_9_ = bf16[32,1664]{1,0:T(8,128)(2,1)S(1)} custom-call(bf16[8,2176]{1,0:T(8,128)(2,1)S(1)} %shard_map.121.refs_0_.refs_4_, bf16[8,2176]{1,0:T(8,128)(2,1)S(1)} %collective-permute-done.1.refs_1_.refs_5_, bf16[8,2176]{1,0:T(8,128)(2,1)S(1)} %collective-permute-done.3.refs_2_.refs_6_, ...), custom_call_target="tpu_custom_call" | custom-call | flops 109051904 | tf_op jit(solution)/shard_map/pallas_call | solution.py:204
  12.9 0.0 collective-permute-done.refs_0_
  12.9 0.0 collective-permute-done.4.refs_2_
  12.9 0.0 collective-permute-done.2.refs_1_
  13.0 0.3 collective-permute-done.6.refs_3_
  13.2 0.9 %shard_map.124 = (bf16[32,1664]{1,0:T(8,128)(2,1)S(1)}, bf16[32,1664]{1,0:T(8,128)(2,1)S(1)}) custom-call(bf16[8,2176]{1,0:T(8,128)(2,1)S(1)} %collective-permute-done.refs_0_, bf16[8,2176]{1,0:T(8,128)(2,1)S(1)} %collective-permute-done.2.refs_1_, bf16[8,2176]{1,0:T(8,128)(2,1)S(1)} %collective-permute-done.4.refs_2_, ...), custom_call_target="tpu_custom_call" | custom-call | flops 109051904 | tf_op jit(solution)/shard_map/pallas_call | solution.py:204
  14.1 1.5 %collective-permute-start.8 = (bf16[32,1664]{1,0:T(8,128)(2,1)S(1)}, bf16[32,1664]{1,0:T(8,128)(2,1)S(1)}, u32[]{:S(2)}, u32[]{:S(2)}) collective-permute-start(bf16[32,1664]{1,0:T(8,128)(2,1)S(1)} %get-tuple-element.41.own_ref), channel_id=1, source_target_pairs={{0,16},{8,24},{16,0},{24,8},{1,17},{9,25},{17,1},{25,9},{2,18},{10... | collective-permute-start | bytes 319496 | tf_op jit(solution)/shard_map/ppermute | solution.py:220
  15.7 0.4 %shard_map.126 = (bf16[64,1024]{1,0:T(8,128)(2,1)S(1)}, f32[64,128]{1,0:T(8,128)S(1)}) custom-call(bf16[8,2176]{1,0:T(8,128)(2,1)S(1)} %collective-permute-done.refs_0_, bf16[8,2176]{1,0:T(8,128)(2,1)S(1)} %collective-permute-done.2.refs_1_, bf16[8,2176]{1,0:T(8,128)(2,1)S(1)} %collective-permute-done.4.refs_2_, ...), custom_call_target="tpu_custom_call" | custom-call | tf_op jit(solution)/shard_map/pallas_call | solution.py:204
  16.1 1.5 %collective-permute-start.12 = (bf16[32,1664]{1,0:T(8,128)(2,1)S(1)}, bf16[32,1664]{1,0:T(8,128)(2,1)S(1)}, u32[]{:S(2)}, u32[]{:S(2)}) collective-permute-start(bf16[32,1664]{1,0:T(8,128)(2,1)S(1)} %get-tuple-element.45.own_ref), channel_id=1, source_target_pairs={{0,24},{8,16},{16,8},{24,0},{1,25},{9,17},{17,9},{25,1},{2,26},{10... | collective-permute-start | bytes 319496 | tf_op jit(solution)/shard_map/ppermute | solution.py:220
  17.6 0.5 %collective-permute-start.11 = (bf16[32,1664]{1,0:T(8,128)(2,1)S(1)}, bf16[32,1664]{1,0:T(8,128)(2,1)S(1)}, u32[]{:S(2)}, u32[]{:S(2)}) collective-permute-start(bf16[32,1664]{1,0:T(8,128)(2,1)S(1)} %get-tuple-element.45.own_ref), channel_id=1, source_target_pairs={{0,8},{8,0},{16,24},{24,16},{1,9},{9,1},{17,25},{25,17},{2,10},{10... | collective-permute-start | bytes 319496 | tf_op jit(solution)/shard_map/ppermute | solution.py:220
  18.1 1.5 %collective-permute-start.10 = (bf16[32,1664]{1,0:T(8,128)(2,1)S(1)}, bf16[32,1664]{1,0:T(8,128)(2,1)S(1)}, u32[]{:S(2)}, u32[]{:S(2)}) collective-permute-start(bf16[32,1664]{1,0:T(8,128)(2,1)S(1)} %get-tuple-element.45.own_ref), channel_id=1, source_target_pairs={{0,16},{8,24},{16,0},{24,8},{1,17},{9,25},{17,1},{25,9},{2,18},{10... | collective-permute-start | bytes 319496 | tf_op jit(solution)/shard_map/ppermute | solution.py:220
  19.6 1.1 %collective-permute-done.8.taken_ref = bf16[32,1664]{1,0:T(8,128)(2,1)S(1)} collective-permute-done((bf16[32,1664]{1,0:T(8,128)(2,1)S(1)}, bf16[32,1664]{1,0:T(8,128)(2,1)S(1)}, u32[]{:S(2)}, u32[]{:S(2)}) %collective-permute-start.8) | collective-permute-done | bytes 106528 | tf_op jit(solution)/shard_map/ppermute | solution.py:220
  20.8 1.6 %collective-permute-start.9 = (bf16[32,1664]{1,0:T(8,128)(2,1)S(1)}, bf16[32,1664]{1,0:T(8,128)(2,1)S(1)}, u32[]{:S(2)}, u32[]{:S(2)}) collective-permute-start(bf16[32,1664]{1,0:T(8,128)(2,1)S(1)} %shard_map.125.own_ref), channel_id=1, source_target_pairs={{0,8},{8,0},{16,24},{24,16},{1,9},{9,1},{17,25},{25,17},{2,10},{10... | collective-permute-start | bytes 319496 | tf_op jit(solution)/shard_map/ppermute | solution.py:220
  22.4 0.5 %collective-permute-done.12.third_ref = bf16[32,1664]{1,0:T(8,128)(2,1)S(1)} collective-permute-done((bf16[32,1664]{1,0:T(8,128)(2,1)S(1)}, bf16[32,1664]{1,0:T(8,128)(2,1)S(1)}, u32[]{:S(2)}, u32[]{:S(2)}) %collective-permute-start.12) | collective-permute-done | bytes 106528 | tf_op jit(solution)/shard_map/ppermute | solution.py:220
  22.9 1.3 %collective-permute-done.11.first_ref = bf16[32,1664]{1,0:T(8,128)(2,1)S(1)} collective-permute-done((bf16[32,1664]{1,0:T(8,128)(2,1)S(1)}, bf16[32,1664]{1,0:T(8,128)(2,1)S(1)}, u32[]{:S(2)}, u32[]{:S(2)}) %collective-permute-start.11) | collective-permute-done | bytes 106528 | tf_op jit(solution)/shard_map/ppermute | solution.py:220
  24.2 0.0 collective-permute-done.10.second_ref
  24.2 1.0 %shard_map.128 = (bf16[32,1088]{1,0:T(8,128)(2,1)S(1)}, bf16[32,1152]{1,0:T(8,128)(2,1)S(1)}, f32[32,128]{1,0:T(8,128)S(1)}) custom-call(bf16[32,1664]{1,0:T(8,128)(2,1)S(1)} %get-tuple-element.45.own_ref, bf16[32,1664]{1,0:T(8,128)(2,1)S(1)} %collective-permute-done.10.second_ref, bf16[32,1664]{1,0:T(8,128)(2,1)S(1)} %collective-permute-done.11.first_ref, ...), custom_call_target="tpu_custom_call" | custom-call | flops 20000000000 | tf_op jit(solution)/shard_map/pallas_call | solution.py:204
  25.2 0.1 collective-permute-start.13
  25.3 0.3 collective-permute-done.9.pair_ref
  25.6 1.0 %shard_map.127 = (f32[32,1024]{1,0:T(8,128)S(1)}, f32[32,64]{1,0:T(8,128)S(1)}, bf16[32,1152]{1,0:T(8,128)(2,1)S(1)}, f32[32,128]{1,0:T(8,128)S(1)}) custom-call(bf16[32,1664]{1,0:T(8,128)(2,1)S(1)} %shard_map.125.own_ref, bf16[32,1664]{1,0:T(8,128)(2,1)S(1)} %collective-permute-done.9.pair_ref, f32[64,128]{1,0:T(8,128)S(1)} %get-tuple-element.42.refs_0_, ...), custom_call_target="tpu_custom_call" | custom-call | flops 20000000000 | tf_op jit(solution)/shard_map/pallas_call | solution.py:204
  26.5 0.3 collective-permute-start.17
  26.8 0.0 collective-permute-done.13.taken_ref
  26.8 2.1 %collective-permute-start.14 = (bf16[8,1024]{1,0:T(8,128)(2,1)S(1)}, bf16[8,1024]{1,0:T(8,128)(2,1)S(1)}, u32[]{:S(2)}, u32[]{:S(2)}) collective-permute-start(bf16[8,1024]{1,0:T(8,128)(2,1)S(1)} %get-tuple-element.48), channel_id=1, source_target_pairs={{0,6},{1,7},{2,4},{3,5},{4,2},{5,3},{6,0},{7,1},{8,14},{9,15},{10,... | collective-permute-start | bytes 49160 | tf_op jit(solution)/shard_map/ppermute | solution.py:220
  28.9 0.0 collective-permute-start.15
  28.9 2.4 %collective-permute-start.16 = (bf16[8,1024]{1,0:T(8,128)(2,1)S(1)}, bf16[8,1024]{1,0:T(8,128)(2,1)S(1)}, u32[]{:S(2)}, u32[]{:S(2)}) collective-permute-start(bf16[8,1024]{1,0:T(8,128)(2,1)S(1)} %get-tuple-element.50), channel_id=1, source_target_pairs={{0,2},{1,3},{2,0},{3,1},{4,6},{5,7},{6,4},{7,5},{8,10},{9,11},{10,... | collective-permute-start | bytes 49160 | tf_op jit(solution)/shard_map/ppermute | solution.py:220
  31.3 0.0 collective-permute-done.17.rest_taken_ref
  31.3 1.2 %shard_map.131 = (f32[128,512]{1,0:T(8,128)}, f32[64,1024]{1,0:T(8,128)}) custom-call(bf16[32,1152]{1,0:T(8,128)(2,1)S(1)} %get-tuple-element.51.rows_ref, bf16[32,1152]{1,0:T(8,128)(2,1)S(1)} %get-tuple-element.52.rest_rows_ref, f32[32,128]{1,0:T(8,128)S(1)} %get-tuple-element.53.back_ref, f32[32,128]{1,0:T(8,128)S(1)} %get-tuple-element.54.rest_back_ref, ...), custom_call_target="tpu_custom_call" | custom-call | flops 20000000000 | tf_op jit(solution)/shard_map/pallas_call | solution.py:204
  32.5 0.0 collective-permute-done.14.third_ref
  32.5 1.0 %collective-permute-done.15.second_ref = bf16[8,1024]{1,0:T(8,128)(2,1)S(1)} collective-permute-done((bf16[8,1024]{1,0:T(8,128)(2,1)S(1)}, bf16[8,1024]{1,0:T(8,128)(2,1)S(1)}, u32[]{:S(2)}, u32[]{:S(2)}) %collective-permute-start.15) | collective-permute-done | bytes 16416 | tf_op jit(solution)/shard_map/ppermute | solution.py:220
  33.5 0.0 collective-permute-done.16.first_ref
  33.6 0.6 %shard_map.130 = bf16[8,1024]{1,0:T(8,128)(2,1)} custom-call(f32[8,1024]{1,0:T(8,128)S(1)} %get-tuple-element.47.own_ref, bf16[8,1024]{1,0:T(8,128)(2,1)S(1)} %collective-permute-done.14.third_ref, bf16[8,1024]{1,0:T(8,128)(2,1)S(1)} %collective-permute-done.15.second_ref, bf16[8,1024]{1,0:T(8,128)(2,1)S(1)} %collective-permute-done.16.first_ref), custom_call_target="tpu_custom_call" | custom-call | tf_op jit(solution)/shard_map/pallas_call | solution.py:204
  (2 shorter events, 0.0 us)
Async XLA Ops:
  0.6 11.4 %collective-permute-start.7 = (bf16[64,1024]{1,0:T(8,128)(2,1)}, bf16[64,1024]{1,0:T(8,128)(2,1)S(1)}, u32[]{:S(2)}, u32[]{:S(2)}) collective-permute-start(bf16[64,1024]{1,0:T(8,128)(2,1)} %bitcast.22), channel_id=1, source_target_pairs={{0,1},{1,0},{2,3},{3,2},{4,5},{5,4},{6,7},{7,6},{8,9},{9,8},{10,11... | collective-permute-start | bytes 393224 | tf_op jit(solution)/shard_map/ppermute | solution.py:220
  2.0 7.4 %collective-permute-start.5 = (bf16[8,2176]{1,0:T(8,128)(2,1)S(1)}, bf16[8,2176]{1,0:T(8,128)(2,1)S(1)}, u32[]{:S(2)}, u32[]{:S(2)}) collective-permute-start(bf16[8,2176]{1,0:T(8,128)(2,1)S(1)} %shard_map.121.refs_0_.refs_4_), channel_id=1, source_target_pairs={{0,6},{1,7},{2,4},{3,5},{4,2},{5,3},{6,0},{7,1},{8,14},{9,15},{10,... | collective-permute-start | bytes 104456 | tf_op jit(solution)/shard_map/ppermute | solution.py:220
  6.7 4.8 %collective-permute-start.3 = (bf16[8,2176]{1,0:T(8,128)(2,1)S(1)}, bf16[8,2176]{1,0:T(8,128)(2,1)S(1)}, u32[]{:S(2)}, u32[]{:S(2)}) collective-permute-start(bf16[8,2176]{1,0:T(8,128)(2,1)S(1)} %shard_map.121.refs_0_.refs_4_), channel_id=1, source_target_pairs={{0,4},{1,5},{2,6},{3,7},{4,0},{5,1},{6,2},{7,3},{8,12},{9,13},{10,... | collective-permute-start | bytes 104456 | tf_op jit(solution)/shard_map/ppermute | solution.py:220
  6.7 4.8 %collective-permute-start.1 = (bf16[8,2176]{1,0:T(8,128)(2,1)S(1)}, bf16[8,2176]{1,0:T(8,128)(2,1)S(1)}, u32[]{:S(2)}, u32[]{:S(2)}) collective-permute-start(bf16[8,2176]{1,0:T(8,128)(2,1)S(1)} %shard_map.121.refs_0_.refs_4_), channel_id=1, source_target_pairs={{0,2},{1,3},{2,0},{3,1},{4,6},{5,7},{6,4},{7,5},{8,10},{9,11},{10,... | collective-permute-start | bytes 104456 | tf_op jit(solution)/shard_map/ppermute | solution.py:220
  7.3 5.6 %collective-permute-start = (bf16[8,2176]{1,0:T(8,128)(2,1)S(1)}, bf16[8,2176]{1,0:T(8,128)(2,1)S(1)}, u32[]{:S(2)}, u32[]{:S(2)}) collective-permute-start(bf16[8,2176]{1,0:T(8,128)(2,1)S(1)} %shard_map.121.refs_0_.refs_4_), channel_id=1, source_target_pairs={{0,1},{1,0},{2,3},{3,2},{4,5},{5,4},{6,7},{7,6},{8,9},{9,8},{10,11... | collective-permute-start | bytes 104456 | tf_op jit(solution)/shard_map/ppermute | solution.py:220
  11.5 1.4 %collective-permute-start.4 = (bf16[8,2176]{1,0:T(8,128)(2,1)S(1)}, bf16[8,2176]{1,0:T(8,128)(2,1)S(1)}, u32[]{:S(2)}, u32[]{:S(2)}) collective-permute-start(bf16[8,2176]{1,0:T(8,128)(2,1)S(1)} %collective-permute-done.3.refs_2_.refs_6_), channel_id=1, source_target_pairs={{0,1},{1,0},{2,3},{3,2},{4,5},{5,4},{6,7},{7,6},{8,9},{9,8},{10,11... | collective-permute-start | bytes 104456 | tf_op jit(solution)/shard_map/ppermute | solution.py:220
  11.5 1.4 %collective-permute-start.2 = (bf16[8,2176]{1,0:T(8,128)(2,1)S(1)}, bf16[8,2176]{1,0:T(8,128)(2,1)S(1)}, u32[]{:S(2)}, u32[]{:S(2)}) collective-permute-start(bf16[8,2176]{1,0:T(8,128)(2,1)S(1)} %collective-permute-done.1.refs_1_.refs_5_), channel_id=1, source_target_pairs={{0,1},{1,0},{2,3},{3,2},{4,5},{5,4},{6,7},{7,6},{8,9},{9,8},{10,11... | collective-permute-start | bytes 104456 | tf_op jit(solution)/shard_map/ppermute | solution.py:220
  12.0 1.2 %collective-permute-start.6 = (bf16[8,2176]{1,0:T(8,128)(2,1)S(1)}, bf16[8,2176]{1,0:T(8,128)(2,1)S(1)}, u32[]{:S(2)}, u32[]{:S(2)}) collective-permute-start(bf16[8,2176]{1,0:T(8,128)(2,1)S(1)} %collective-permute-done.5.refs_3_.refs_7_), channel_id=1, source_target_pairs={{0,1},{1,0},{2,3},{3,2},{4,5},{5,4},{6,7},{7,6},{8,9},{9,8},{10,11... | collective-permute-start | bytes 104456 | tf_op jit(solution)/shard_map/ppermute | solution.py:220
  14.1 6.6 %collective-permute-start.8 = (bf16[32,1664]{1,0:T(8,128)(2,1)S(1)}, bf16[32,1664]{1,0:T(8,128)(2,1)S(1)}, u32[]{:S(2)}, u32[]{:S(2)}) collective-permute-start(bf16[32,1664]{1,0:T(8,128)(2,1)S(1)} %get-tuple-element.41.own_ref), channel_id=1, source_target_pairs={{0,16},{8,24},{16,0},{24,8},{1,17},{9,25},{17,1},{25,9},{2,18},{10... | collective-permute-start | bytes 319496 | tf_op jit(solution)/shard_map/ppermute | solution.py:220
  16.1 6.8 %collective-permute-start.12 = (bf16[32,1664]{1,0:T(8,128)(2,1)S(1)}, bf16[32,1664]{1,0:T(8,128)(2,1)S(1)}, u32[]{:S(2)}, u32[]{:S(2)}) collective-permute-start(bf16[32,1664]{1,0:T(8,128)(2,1)S(1)} %get-tuple-element.45.own_ref), channel_id=1, source_target_pairs={{0,24},{8,16},{16,8},{24,0},{1,25},{9,17},{17,9},{25,1},{2,26},{10... | collective-permute-start | bytes 319496 | tf_op jit(solution)/shard_map/ppermute | solution.py:220
  17.6 6.6 %collective-permute-start.11 = (bf16[32,1664]{1,0:T(8,128)(2,1)S(1)}, bf16[32,1664]{1,0:T(8,128)(2,1)S(1)}, u32[]{:S(2)}, u32[]{:S(2)}) collective-permute-start(bf16[32,1664]{1,0:T(8,128)(2,1)S(1)} %get-tuple-element.45.own_ref), channel_id=1, source_target_pairs={{0,8},{8,0},{16,24},{24,16},{1,9},{9,1},{17,25},{25,17},{2,10},{10... | collective-permute-start | bytes 319496 | tf_op jit(solution)/shard_map/ppermute | solution.py:220
  18.1 6.1 %collective-permute-start.10 = (bf16[32,1664]{1,0:T(8,128)(2,1)S(1)}, bf16[32,1664]{1,0:T(8,128)(2,1)S(1)}, u32[]{:S(2)}, u32[]{:S(2)}) collective-permute-start(bf16[32,1664]{1,0:T(8,128)(2,1)S(1)} %get-tuple-element.45.own_ref), channel_id=1, source_target_pairs={{0,16},{8,24},{16,0},{24,8},{1,17},{9,25},{17,1},{25,9},{2,18},{10... | collective-permute-start | bytes 319496 | tf_op jit(solution)/shard_map/ppermute | solution.py:220
  20.8 4.8 %collective-permute-start.9 = (bf16[32,1664]{1,0:T(8,128)(2,1)S(1)}, bf16[32,1664]{1,0:T(8,128)(2,1)S(1)}, u32[]{:S(2)}, u32[]{:S(2)}) collective-permute-start(bf16[32,1664]{1,0:T(8,128)(2,1)S(1)} %shard_map.125.own_ref), channel_id=1, source_target_pairs={{0,8},{8,0},{16,24},{24,16},{1,9},{9,1},{17,25},{25,17},{2,10},{10... | collective-permute-start | bytes 319496 | tf_op jit(solution)/shard_map/ppermute | solution.py:220
  25.2 1.6 %collective-permute-start.13 = (bf16[32,1088]{1,0:T(8,128)(2,1)S(1)}, bf16[32,1088]{1,0:T(8,128)(2,1)S(1)}, u32[]{:S(2)}, u32[]{:S(2)}) collective-permute-start(bf16[32,1088]{1,0:T(8,128)(2,1)S(1)} %get-tuple-element.46), channel_id=1, source_target_pairs={{0,1},{1,0},{2,3},{3,2},{4,5},{5,4},{6,7},{7,6},{8,9},{9,8},{10,11... | collective-permute-start | bytes 208904 | tf_op jit(solution)/shard_map/ppermute | solution.py:220
  26.5 4.7 %collective-permute-start.17 = (f32[32,64]{1,0:T(8,128)S(1)}, f32[32,64]{1,0:T(8,128)S(1)}, u32[]{:S(2)}, u32[]{:S(2)}) collective-permute-start(f32[32,64]{1,0:T(8,128)S(1)} %get-tuple-element.55), channel_id=1, source_target_pairs={{0,1},{1,0},{2,3},{3,2},{4,5},{5,4},{6,7},{7,6},{8,9},{9,8},{10,11... | collective-permute-start | bytes 24584 | tf_op jit(solution)/shard_map/ppermute | solution.py:220
  26.8 5.7 %collective-permute-start.14 = (bf16[8,1024]{1,0:T(8,128)(2,1)S(1)}, bf16[8,1024]{1,0:T(8,128)(2,1)S(1)}, u32[]{:S(2)}, u32[]{:S(2)}) collective-permute-start(bf16[8,1024]{1,0:T(8,128)(2,1)S(1)} %get-tuple-element.48), channel_id=1, source_target_pairs={{0,6},{1,7},{2,4},{3,5},{4,2},{5,3},{6,0},{7,1},{8,14},{9,15},{10,... | collective-permute-start | bytes 49160 | tf_op jit(solution)/shard_map/ppermute | solution.py:220
  28.9 4.6 %collective-permute-start.15 = (bf16[8,1024]{1,0:T(8,128)(2,1)S(1)}, bf16[8,1024]{1,0:T(8,128)(2,1)S(1)}, u32[]{:S(2)}, u32[]{:S(2)}) collective-permute-start(bf16[8,1024]{1,0:T(8,128)(2,1)S(1)} %get-tuple-element.49), channel_id=1, source_target_pairs={{0,4},{1,5},{2,6},{3,7},{4,0},{5,1},{6,2},{7,3},{8,12},{9,13},{10,... | collective-permute-start | bytes 49160 | tf_op jit(solution)/shard_map/ppermute | solution.py:220
  28.9 4.6 %collective-permute-start.16 = (bf16[8,1024]{1,0:T(8,128)(2,1)S(1)}, bf16[8,1024]{1,0:T(8,128)(2,1)S(1)}, u32[]{:S(2)}, u32[]{:S(2)}) collective-permute-start(bf16[8,1024]{1,0:T(8,128)(2,1)S(1)} %get-tuple-element.50), channel_id=1, source_target_pairs={{0,2},{1,3},{2,0},{3,1},{4,6},{5,7},{6,4},{7,5},{8,10},{9,11},{10,... | collective-permute-start | bytes 49160 | tf_op jit(solution)/shard_map/ppermute | solution.py:220

commit v5 on v4

--- a/solution.py
+++ b/solution.py
@@ -418,38 +418,20 @@
     out_ref[...] = total.astype(BF16)
 
 
-def maps_grad_body(
-    rows_ref,
-    rest_rows_ref,
-    back_ref,
-    rest_back_ref,
-    taken_ref,
-    rest_taken_ref,
-    x_ref,
-    maps_out_ref,
-    inputs_out_ref,
-    maps,
-    inputs,
-    arrived,
-):
-    lanes, hidden = maps.shape
+def maps_grad_body(rows_ref, rest_rows_ref, out_ref):
+    lanes, hidden = out_ref.shape
     half = lanes // 2
-    width = x_ref.shape[1]
-    copies = [
-        pltpu.make_async_copy(maps, maps_out_ref, arrived.at[0]),
-        pltpu.make_async_copy(inputs, inputs_out_ref, arrived.at[1]),
-    ]
+    rows = jnp.concatenate([rows_ref[...], rest_rows_ref[...]], axis=0)
+    low = dot_plain(rows[:, 2 * hidden :], rank_order(lanes, True)).astype(BF16)
+    out_ref[:half] = ADAPTER_SCALE * product_leading(low[:, :half], rows[:, :hidden])
+    out_ref[half:] = ADAPTER_SCALE * product_leading(low[:, half:], rows[:, hidden : 2 * hidden])
+
+
+def input_maps_grad_body(back_ref, rest_back_ref, taken_ref, rest_taken_ref, x_ref, out_ref):
+    half, width = out_ref.shape
     taken = jnp.concatenate([rest_taken_ref[...], taken_ref[:, width:].astype(F32)], axis=0)
     back = jnp.concatenate([back_ref[:, :half], rest_back_ref[:, :half]], axis=0)
-    inputs[...] = product_leading((back + taken).astype(BF16), x_ref[...])
-    copies[1].start()
-    rows = jnp.concatenate([rows_ref[...], rest_rows_ref[...]], axis=0)
-    low = dot_plain(rows[:, 2 * hidden :], rank_order(lanes, True)).astype(BF16)
-    maps[:half] = ADAPTER_SCALE * product_leading(low[:, :half], rows[:, :hidden])
-    maps[half:] = ADAPTER_SCALE * product_leading(low[:, half:], rows[:, hidden : 2 * hidden])
-    copies[0].start()
-    for copy in copies:
-        copy.wait()
+    out_ref[...] = product_leading((back + taken).astype(BF16), x_ref[...])
 
 
 def dense_shards(
@@ -514,24 +496,28 @@
         (*same_core, *weights),
         flops=slots * width * columns,
     )
-    own, mine = local_call(
-        forward_rest_body,
-        [((slots // 2, columns), BF16)] * 2,
-        (*other_core, *weights, before),
+    mine, other_core = lax.optimization_barrier((before, other_core))
+    (own,) = local_call(
+        forward_body,
+        [((slots // 2, columns), BF16)],
+        (*other_core, *weights),
         flops=slots * width * columns,
     )
     sums = [own] + [swap(own, "dp", k) for k in (2, 1, 3)]
+    taken = swap(mine, "dp", 2)
     (pair,) = local_call(
         pair_body,
         [((slots // 2, columns), BF16)],
-        (mine, swap(mine, "dp", 2)),
+        (mine, taken),
         flops=LONG,
     )
     rest_sums = [pair, swap(pair, "dp", 1)]
+    blocks, _ = lax.optimization_barrier(((*other_core, *same_core), taken))
     x, tags = local_call(
         functools.partial(tags_body, topk),
         [((slots, width), BF16), ((slots, 128), F32)],
-        (*other_core, *same_core),
+        blocks,
+        flops=LONG,
     )
     shared = (tags, gate, up, mine_cols, other_cols, maps)
     outs = [((slots // 2, 2 * hidden + lanes), BF16), ((slots // 2, lanes), F32)]
@@ -556,17 +542,11 @@
     )
     third, second = swap(third, "expert", 6), swap(second, "expert", 4)
     returned = [own, third, second, swap(first, "expert", 2)]
-    maps_grad, input_maps_grad = local_call(
-        maps_grad_body,
-        [((lanes, hidden), F32), ((lanes // 2, width), F32)],
-        (rows, rest_rows, back, rest_back, taken, back_taken, x),
-        scratch=[
-            pltpu.VMEM((lanes, hidden), F32),
-            pltpu.VMEM((lanes // 2, width), F32),
-            pltpu.SemaphoreType.DMA((2,)),
-        ],
-        far_outs=2,
-        flops=LONG,
+    (maps_grad,) = local_call(maps_grad_body, [((lanes, hidden), F32)], (rows, rest_rows))
+    (input_maps_grad,) = local_call(
+        input_maps_grad_body,
+        [((lanes // 2, width), F32)],
+        (back, rest_back, taken, back_taken, x),
     )
     (input_grad,) = local_call(finish_body, [((count, width), BF16)], returned)
     adapter_a_grad = (

time: 34.4 us -> 33.7 us (0.980)
  waiting for transfers between devices: 6.7 us -> 5.49 us
  Pallas kernels: 8.99 us -> 9.78 us
    ppermute x18, waiting for transfers between devices: 6.7 us -> 5.49 us  [swap(): lax.ppermute(array, axis, [(i, i ^ offset) for i in range(lax.axis_size(a...]
    pallas_call x11 -> x12, Pallas kernels: 8.99 us -> 9.78 us  [local_call(): pl.pallas_call(body, out_shape=[jax.ShapeDtypeStruct(shape, kind) for sha...]
  transfers between devices with their start and end apart: 18 -> 18, of which waited for: 7 -> 7; matrix products, arithmetic and copies ran while one was open for 0% -> 0% of each run, Pallas kernels for 22% -> 27%
where the time goes in v5:
time: 33.7 us; the launch traced here: 33.5 us
  starting transfers between devices  17.5 us (52%)
  Pallas kernels  9.78 us (29%)
  waiting for transfers between devices  5.49 us (16%)
  between operations  0.73 us (2%)
    ppermute x18, starting transfers between devices, swap(): lax.ppermute(array, axis, [(i, i ^ offset) for i in range(lax.axis_size(a...  17.5 us
    pallas_call x12, Pallas kernels, local_call(): pl.pallas_call(body, out_shape=[jax.ShapeDtypeStruct(shape, kind) for sha...  9.78 us
    ppermute x18, waiting for transfers between devices, swap(): lax.ppermute(array, axis, [(i, i ^ offset) for i in range(lax.axis_size(a...  5.49 us
  transfers between devices with their start and end apart: 18, of which 7 were waited for; matrix products, arithmetic and copies ran while one was open for 0% of the time, Pallas kernels for 27%

profile of v5, /device:TPU:0, one launch (start us, length us, event | category | flops | bytes accessed | tf_op | source)
XLA Modules:
  0.0 33.5 jit_solution(8209368813501748448)
XLA Ops:
  0.6 0.5 %collective-permute-start.3 = (bf16[64,1024]{1,0:T(8,128)(2,1)}, bf16[64,1024]{1,0:T(8,128)(2,1)S(1)}, u32[]{:S(2)}, u32[]{:S(2)}) collective-permute-start(bf16[64,1024]{1,0:T(8,128)(2,1)} %bitcast.24), channel_id=1, source_target_pairs={{0,1},{1,0},{2,3},{3,2},{4,5},{5,4},{6,7},{7,6},{8,9},{9,8},{10,11... | collective-permute-start | bytes 393224 | tf_op jit(solution)/shard_map/ppermute | solution.py:220
  1.1 0.8 %shard_map.121.refs_0_.refs_4_ = bf16[8,2176]{1,0:T(8,128)(2,1)S(1)} custom-call(bf16[8,1024]{1,0:T(8,128)(2,1)} %x_ref.1, bf16[8,1024]{1,0:T(8,128)(2,1)} %dy_ref.1, s32[2,8]{1,0:T(2,128)} %bitcast.26, bf16[2,8]{1,0:T(2,128)(2,1)} %bitcast.27, s32[1,8]{1,0:T(1,128)} %bitcast.28), custom_call_target="tpu_custom_call" | custom-call | tf_op jit(solution)/shard_map/pallas_call | solution.py:204
  2.0 4.7 %collective-permute-start.2 = (bf16[8,2176]{1,0:T(8,128)(2,1)S(1)}, bf16[8,2176]{1,0:T(8,128)(2,1)S(1)}, u32[]{:S(2)}, u32[]{:S(2)}) collective-permute-start(bf16[8,2176]{1,0:T(8,128)(2,1)S(1)} %shard_map.121.refs_0_.refs_4_), channel_id=1, source_target_pairs={{0,6},{1,7},{2,4},{3,5},{4,2},{5,3},{6,0},{7,1},{8,14},{9,15},{10,... | collective-permute-start | bytes 104456 | tf_op jit(solution)/shard_map/ppermute | solution.py:220
  6.7 0.0 collective-permute-start.1
  6.7 0.6 %collective-permute-start = (bf16[8,2176]{1,0:T(8,128)(2,1)S(1)}, bf16[8,2176]{1,0:T(8,128)(2,1)S(1)}, u32[]{:S(2)}, u32[]{:S(2)}) collective-permute-start(bf16[8,2176]{1,0:T(8,128)(2,1)S(1)} %shard_map.121.refs_0_.refs_4_), channel_id=1, source_target_pairs={{0,2},{1,3},{2,0},{3,1},{4,6},{5,7},{6,4},{7,5},{8,10},{9,11},{10,... | collective-permute-start | bytes 104456 | tf_op jit(solution)/shard_map/ppermute | solution.py:220
  7.3 0.0 collective-permute-start.4
  7.3 2.1 %shard_map.122 = (bf16[1024,512]{1,0:T(8,128)(2,1)S(1)}, bf16[1024,512]{1,0:T(8,128)(2,1)S(1)}, bf16[512,1024]{1,0:T(8,128)(2,1)S(1)}, bf16[64,1024]{1,0:T(8,128)(2,1)S(1)}, bf16[128,512]{1,0:T(8,128)(2,1)S(1)}) custom-call(bf16[1024,512]{1,0:T(8,128)(2,1)} %bitcast.18, bf16[1024,512]{1,0:T(8,128)(2,1)} %bitcast.19, bf16[512,1024]{1,0:T(8,128)(2,1)} %bitcast.20, ...), custom_call_target="tpu_custom_call" | custom-call | bytes 3407872 | tf_op jit(solution)/shard_map/pallas_call | solution.py:204
  9.4 0.0 collective-permute-done.2.refs_3_.refs_7_
  9.4 2.1 %collective-permute-done.1.refs_2_.refs_6_ = bf16[8,2176]{1,0:T(8,128)(2,1)S(1)} collective-permute-done((bf16[8,2176]{1,0:T(8,128)(2,1)S(1)}, bf16[8,2176]{1,0:T(8,128)(2,1)S(1)}, u32[]{:S(2)}, u32[]{:S(2)}) %collective-permute-start.1) | collective-permute-done | bytes 34848 | tf_op jit(solution)/shard_map/ppermute | solution.py:220
  11.5 0.0 collective-permute-start.6
  11.5 0.0 collective-permute-done.refs_1_.refs_5_
  11.5 0.5 %collective-permute-start.5 = (bf16[8,2176]{1,0:T(8,128)(2,1)S(1)}, bf16[8,2176]{1,0:T(8,128)(2,1)S(1)}, u32[]{:S(2)}, u32[]{:S(2)}) collective-permute-start(bf16[8,2176]{1,0:T(8,128)(2,1)S(1)} %collective-permute-done.refs_1_.refs_5_), channel_id=1, source_target_pairs={{0,1},{1,0},{2,3},{3,2},{4,5},{5,4},{6,7},{7,6},{8,9},{9,8},{10,11... | collective-permute-start | bytes 104456 | tf_op jit(solution)/shard_map/ppermute | solution.py:220
  12.0 0.0 collective-permute-start.7
  12.0 0.0 collective-permute-done.3.refs_8_.refs_4_
  12.0 0.9 %shard_map.123.own_ref = bf16[32,1664]{1,0:T(8,128)(2,1)S(1)} custom-call(bf16[8,2176]{1,0:T(8,128)(2,1)S(1)} %shard_map.121.refs_0_.refs_4_, bf16[8,2176]{1,0:T(8,128)(2,1)S(1)} %collective-permute-done.refs_1_.refs_5_, bf16[8,2176]{1,0:T(8,128)(2,1)S(1)} %collective-permute-done.1.refs_2_.refs_6_, ...), custom_call_target="tpu_custom_call" | custom-call | flops 109051904 | tf_op jit(solution)/shard_map/pallas_call | solution.py:204
  12.9 0.0 collective-permute-done.4.refs_0_
  12.9 0.0 collective-permute-done.6.refs_2_
  12.9 0.0 collective-permute-done.5.refs_1_
  13.0 0.3 collective-permute-done.7.refs_3_
  13.2 1.5 %collective-permute-start.8 = (bf16[32,1664]{1,0:T(8,128)(2,1)S(1)}, bf16[32,1664]{1,0:T(8,128)(2,1)S(1)}, u32[]{:S(2)}, u32[]{:S(2)}) collective-permute-start(bf16[32,1664]{1,0:T(8,128)(2,1)S(1)} %shard_map.123.own_ref), channel_id=1, source_target_pairs={{0,16},{8,24},{16,0},{24,8},{1,17},{9,25},{17,1},{25,9},{2,18},{10... | collective-permute-start | bytes 319496 | tf_op jit(solution)/shard_map/ppermute | solution.py:220
  14.7 0.9 %shard_map.127.own_ref = bf16[32,1664]{1,0:T(8,128)(2,1)S(1)} custom-call(bf16[8,2176]{1,0:T(8,128)(2,1)S(1)} %collective-permute-done.4.refs_0_, bf16[8,2176]{1,0:T(8,128)(2,1)S(1)} %collective-permute-done.5.refs_1_, bf16[8,2176]{1,0:T(8,128)(2,1)S(1)} %collective-permute-done.6.refs_2_, bf16[8,2176]{1,0:T(8,128)(2,1)S(1)} %collective-permute-done.7.refs_3_, ...), custom_call_target="tpu_custom_call" | custom-call | flops 109051904 | tf_op jit(solution)/shard_map/pallas_call | solution.py:204
  15.6 1.5 %collective-permute-start.12 = (bf16[32,1664]{1,0:T(8,128)(2,1)S(1)}, bf16[32,1664]{1,0:T(8,128)(2,1)S(1)}, u32[]{:S(2)}, u32[]{:S(2)}) collective-permute-start(bf16[32,1664]{1,0:T(8,128)(2,1)S(1)} %shard_map.127.own_ref), channel_id=1, source_target_pairs={{0,24},{8,16},{16,8},{24,0},{1,25},{9,17},{17,9},{25,1},{2,26},{10... | collective-permute-start | bytes 319496 | tf_op jit(solution)/shard_map/ppermute | solution.py:220
  17.1 0.5 %collective-permute-start.11 = (bf16[32,1664]{1,0:T(8,128)(2,1)S(1)}, bf16[32,1664]{1,0:T(8,128)(2,1)S(1)}, u32[]{:S(2)}, u32[]{:S(2)}) collective-permute-start(bf16[32,1664]{1,0:T(8,128)(2,1)S(1)} %shard_map.127.own_ref), channel_id=1, source_target_pairs={{0,8},{8,0},{16,24},{24,16},{1,9},{9,1},{17,25},{25,17},{2,10},{10... | collective-permute-start | bytes 319496 | tf_op jit(solution)/shard_map/ppermute | solution.py:220
  17.6 1.5 %collective-permute-start.10 = (bf16[32,1664]{1,0:T(8,128)(2,1)S(1)}, bf16[32,1664]{1,0:T(8,128)(2,1)S(1)}, u32[]{:S(2)}, u32[]{:S(2)}) collective-permute-start(bf16[32,1664]{1,0:T(8,128)(2,1)S(1)} %shard_map.127.own_ref), channel_id=1, source_target_pairs={{0,16},{8,24},{16,0},{24,8},{1,17},{9,25},{17,1},{25,9},{2,18},{10... | collective-permute-start | bytes 319496 | tf_op jit(solution)/shard_map/ppermute | solution.py:220
  19.2 0.0 collective-permute-done.8.taken_ref
  19.2 1.6 %collective-permute-start.9 = (bf16[32,1664]{1,0:T(8,128)(2,1)S(1)}, bf16[32,1664]{1,0:T(8,128)(2,1)S(1)}, u32[]{:S(2)}, u32[]{:S(2)}) collective-permute-start(bf16[32,1664]{1,0:T(8,128)(2,1)S(1)} %shard_map.124.own_ref), channel_id=1, source_target_pairs={{0,8},{8,0},{16,24},{24,16},{1,9},{9,1},{17,25},{25,17},{2,10},{10... | collective-permute-start | bytes 319496 | tf_op jit(solution)/shard_map/ppermute | solution.py:220
  20.8 0.4 %shard_map.125 = (bf16[64,1024]{1,0:T(8,128)(2,1)S(1)}, f32[64,128]{1,0:T(8,128)S(1)}) custom-call(bf16[8,2176]{1,0:T(8,128)(2,1)S(1)} %collective-permute-done.4.refs_0_, bf16[8,2176]{1,0:T(8,128)(2,1)S(1)} %collective-permute-done.5.refs_1_, bf16[8,2176]{1,0:T(8,128)(2,1)S(1)} %collective-permute-done.6.refs_2_, ...), custom_call_target="tpu_custom_call" | custom-call | flops 20000000000 | tf_op jit(solution)/shard_map/pallas_call | solution.py:204
  21.2 1.2 %collective-permute-done.12.third_ref = bf16[32,1664]{1,0:T(8,128)(2,1)S(1)} collective-permute-done((bf16[32,1664]{1,0:T(8,128)(2,1)S(1)}, bf16[32,1664]{1,0:T(8,128)(2,1)S(1)}, u32[]{:S(2)}, u32[]{:S(2)}) %collective-permute-start.12) | collective-permute-done | bytes 106528 | tf_op jit(solution)/shard_map/ppermute | solution.py:220
  22.4 1.4 %collective-permute-done.11.first_ref = bf16[32,1664]{1,0:T(8,128)(2,1)S(1)} collective-permute-done((bf16[32,1664]{1,0:T(8,128)(2,1)S(1)}, bf16[32,1664]{1,0:T(8,128)(2,1)S(1)}, u32[]{:S(2)}, u32[]{:S(2)}) %collective-permute-start.11) | collective-permute-done | bytes 106528 | tf_op jit(solution)/shard_map/ppermute | solution.py:220
  23.8 0.0 collective-permute-done.10.second_ref
  23.8 1.0 %shard_map.128 = (bf16[32,1088]{1,0:T(8,128)(2,1)S(1)}, bf16[32,1152]{1,0:T(8,128)(2,1)S(1)}, f32[32,128]{1,0:T(8,128)S(1)}) custom-call(bf16[32,1664]{1,0:T(8,128)(2,1)S(1)} %shard_map.127.own_ref, bf16[32,1664]{1,0:T(8,128)(2,1)S(1)} %collective-permute-done.10.second_ref, bf16[32,1664]{1,0:T(8,128)(2,1)S(1)} %collective-permute-done.11.first_ref, ...), custom_call_target="tpu_custom_call" | custom-call | flops 20000000000 | tf_op jit(solution)/shard_map/pallas_call | solution.py:204
  24.7 0.1 collective-permute-start.13
  24.8 0.3 collective-permute-done.9.pair_ref
  25.1 1.0 %shard_map.126 = (f32[32,1024]{1,0:T(8,128)S(1)}, f32[32,64]{1,0:T(8,128)S(1)}, bf16[32,1152]{1,0:T(8,128)(2,1)S(1)}, f32[32,128]{1,0:T(8,128)S(1)}) custom-call(bf16[32,1664]{1,0:T(8,128)(2,1)S(1)} %shard_map.124.own_ref, bf16[32,1664]{1,0:T(8,128)(2,1)S(1)} %collective-permute-done.9.pair_ref, f32[64,128]{1,0:T(8,128)S(1)} %get-tuple-element.63.refs_0_, ...), custom_call_target="tpu_custom_call" | custom-call | flops 20000000000 | tf_op jit(solution)/shard_map/pallas_call | solution.py:204
  26.1 0.0 collective-permute-done.13.taken_ref
  26.1 2.1 %collective-permute-start.14 = (bf16[8,1024]{1,0:T(8,128)(2,1)S(1)}, bf16[8,1024]{1,0:T(8,128)(2,1)S(1)}, u32[]{:S(2)}, u32[]{:S(2)}) collective-permute-start(bf16[8,1024]{1,0:T(8,128)(2,1)S(1)} %get-tuple-element.68), channel_id=1, source_target_pairs={{0,6},{1,7},{2,4},{3,5},{4,2},{5,3},{6,0},{7,1},{8,14},{9,15},{10,... | collective-permute-start | bytes 49160 | tf_op jit(solution)/shard_map/ppermute | solution.py:220
  28.2 0.0 collective-permute-start.15
  28.2 2.4 %collective-permute-start.16 = (bf16[8,1024]{1,0:T(8,128)(2,1)S(1)}, bf16[8,1024]{1,0:T(8,128)(2,1)S(1)}, u32[]{:S(2)}, u32[]{:S(2)}) collective-permute-start(bf16[8,1024]{1,0:T(8,128)(2,1)S(1)} %get-tuple-element.70), channel_id=1, source_target_pairs={{0,2},{1,3},{2,0},{3,1},{4,6},{5,7},{6,4},{7,5},{8,10},{9,11},{10,... | collective-permute-start | bytes 49160 | tf_op jit(solution)/shard_map/ppermute | solution.py:220
  30.6 0.0 collective-permute-start.17
  30.6 1.1 %shard_map.132 = f32[128,512]{1,0:T(8,128)} custom-call(bf16[32,1152]{1,0:T(8,128)(2,1)S(1)} %get-tuple-element.75.rows_ref, bf16[32,1152]{1,0:T(8,128)(2,1)S(1)} %get-tuple-element.76.rest_rows_ref), custom_call_target="tpu_custom_call" | custom-call | tf_op jit(solution)/shard_map/pallas_call | solution.py:204
  31.7 0.1 collective-permute-done.17.rest_taken_ref
  31.8 0.9 %shard_map.131 = f32[64,1024]{1,0:T(8,128)} custom-call(f32[32,128]{1,0:T(8,128)S(1)} %get-tuple-element.71.back_ref, f32[32,128]{1,0:T(8,128)S(1)} %get-tuple-element.72.rest_back_ref, bf16[32,1088]{1,0:T(8,128)(2,1)S(1)} %collective-permute-done.13.taken_ref, f32[32,64]{1,0:T(8,128)S(1)} %collective-permute-done.17.rest_taken_ref, ...), custom_call_target="tpu_custom_call" | custom-call | tf_op jit(solution)/shard_map/pallas_call | solution.py:204
  32.7 0.0 collective-permute-done.14.third_ref
  32.7 0.2 collective-permute-done.15.second_ref
  32.9 0.0 collective-permute-done.16.first_ref
  32.9 0.6 %shard_map.130 = bf16[8,1024]{1,0:T(8,128)(2,1)} custom-call(f32[8,1024]{1,0:T(8,128)S(1)} %get-tuple-element.67.own_ref, bf16[8,1024]{1,0:T(8,128)(2,1)S(1)} %collective-permute-done.14.third_ref, bf16[8,1024]{1,0:T(8,128)(2,1)S(1)} %collective-permute-done.15.second_ref, bf16[8,1024]{1,0:T(8,128)(2,1)S(1)} %collective-permute-done.16.first_ref), custom_call_target="tpu_custom_call" | custom-call | tf_op jit(solution)/shard_map/pallas_call | solution.py:204
  (2 shorter events, 0.1 us)
Async XLA Ops:
  0.6 11.4 %collective-permute-start.3 = (bf16[64,1024]{1,0:T(8,128)(2,1)}, bf16[64,1024]{1,0:T(8,128)(2,1)S(1)}, u32[]{:S(2)}, u32[]{:S(2)}) collective-permute-start(bf16[64,1024]{1,0:T(8,128)(2,1)} %bitcast.24), channel_id=1, source_target_pairs={{0,1},{1,0},{2,3},{3,2},{4,5},{5,4},{6,7},{7,6},{8,9},{9,8},{10,11... | collective-permute-start | bytes 393224 | tf_op jit(solution)/shard_map/ppermute | solution.py:220
  2.0 7.4 %collective-permute-start.2 = (bf16[8,2176]{1,0:T(8,128)(2,1)S(1)}, bf16[8,2176]{1,0:T(8,128)(2,1)S(1)}, u32[]{:S(2)}, u32[]{:S(2)}) collective-permute-start(bf16[8,2176]{1,0:T(8,128)(2,1)S(1)} %shard_map.121.refs_0_.refs_4_), channel_id=1, source_target_pairs={{0,6},{1,7},{2,4},{3,5},{4,2},{5,3},{6,0},{7,1},{8,14},{9,15},{10,... | collective-permute-start | bytes 104456 | tf_op jit(solution)/shard_map/ppermute | solution.py:220
  6.7 4.8 %collective-permute-start.1 = (bf16[8,2176]{1,0:T(8,128)(2,1)S(1)}, bf16[8,2176]{1,0:T(8,128)(2,1)S(1)}, u32[]{:S(2)}, u32[]{:S(2)}) collective-permute-start(bf16[8,2176]{1,0:T(8,128)(2,1)S(1)} %shard_map.121.refs_0_.refs_4_), channel_id=1, source_target_pairs={{0,4},{1,5},{2,6},{3,7},{4,0},{5,1},{6,2},{7,3},{8,12},{9,13},{10,... | collective-permute-start | bytes 104456 | tf_op jit(solution)/shard_map/ppermute | solution.py:220
  6.7 4.8 %collective-permute-start = (bf16[8,2176]{1,0:T(8,128)(2,1)S(1)}, bf16[8,2176]{1,0:T(8,128)(2,1)S(1)}, u32[]{:S(2)}, u32[]{:S(2)}) collective-permute-start(bf16[8,2176]{1,0:T(8,128)(2,1)S(1)} %shard_map.121.refs_0_.refs_4_), channel_id=1, source_target_pairs={{0,2},{1,3},{2,0},{3,1},{4,6},{5,7},{6,4},{7,5},{8,10},{9,11},{10,... | collective-permute-start | bytes 104456 | tf_op jit(solution)/shard_map/ppermute | solution.py:220
  7.3 5.6 %collective-permute-start.4 = (bf16[8,2176]{1,0:T(8,128)(2,1)S(1)}, bf16[8,2176]{1,0:T(8,128)(2,1)S(1)}, u32[]{:S(2)}, u32[]{:S(2)}) collective-permute-start(bf16[8,2176]{1,0:T(8,128)(2,1)S(1)} %shard_map.121.refs_0_.refs_4_), channel_id=1, source_target_pairs={{0,1},{1,0},{2,3},{3,2},{4,5},{5,4},{6,7},{7,6},{8,9},{9,8},{10,11... | collective-permute-start | bytes 104456 | tf_op jit(solution)/shard_map/ppermute | solution.py:220
  11.5 1.4 %collective-permute-start.6 = (bf16[8,2176]{1,0:T(8,128)(2,1)S(1)}, bf16[8,2176]{1,0:T(8,128)(2,1)S(1)}, u32[]{:S(2)}, u32[]{:S(2)}) collective-permute-start(bf16[8,2176]{1,0:T(8,128)(2,1)S(1)} %collective-permute-done.1.refs_2_.refs_6_), channel_id=1, source_target_pairs={{0,1},{1,0},{2,3},{3,2},{4,5},{5,4},{6,7},{7,6},{8,9},{9,8},{10,11... | collective-permute-start | bytes 104456 | tf_op jit(solution)/shard_map/ppermute | solution.py:220
  11.5 1.4 %collective-permute-start.5 = (bf16[8,2176]{1,0:T(8,128)(2,1)S(1)}, bf16[8,2176]{1,0:T(8,128)(2,1)S(1)}, u32[]{:S(2)}, u32[]{:S(2)}) collective-permute-start(bf16[8,2176]{1,0:T(8,128)(2,1)S(1)} %collective-permute-done.refs_1_.refs_5_), channel_id=1, source_target_pairs={{0,1},{1,0},{2,3},{3,2},{4,5},{5,4},{6,7},{7,6},{8,9},{9,8},{10,11... | collective-permute-start | bytes 104456 | tf_op jit(solution)/shard_map/ppermute | solution.py:220
  12.0 1.2 %collective-permute-start.7 = (bf16[8,2176]{1,0:T(8,128)(2,1)S(1)}, bf16[8,2176]{1,0:T(8,128)(2,1)S(1)}, u32[]{:S(2)}, u32[]{:S(2)}) collective-permute-start(bf16[8,2176]{1,0:T(8,128)(2,1)S(1)} %collective-permute-done.2.refs_3_.refs_7_), channel_id=1, source_target_pairs={{0,1},{1,0},{2,3},{3,2},{4,5},{5,4},{6,7},{7,6},{8,9},{9,8},{10,11... | collective-permute-start | bytes 104456 | tf_op jit(solution)/shard_map/ppermute | solution.py:220
  13.2 5.9 %collective-permute-start.8 = (bf16[32,1664]{1,0:T(8,128)(2,1)S(1)}, bf16[32,1664]{1,0:T(8,128)(2,1)S(1)}, u32[]{:S(2)}, u32[]{:S(2)}) collective-permute-start(bf16[32,1664]{1,0:T(8,128)(2,1)S(1)} %shard_map.123.own_ref), channel_id=1, source_target_pairs={{0,16},{8,24},{16,0},{24,8},{1,17},{9,25},{17,1},{25,9},{2,18},{10... | collective-permute-start | bytes 319496 | tf_op jit(solution)/shard_map/ppermute | solution.py:220
  15.6 6.8 %collective-permute-start.12 = (bf16[32,1664]{1,0:T(8,128)(2,1)S(1)}, bf16[32,1664]{1,0:T(8,128)(2,1)S(1)}, u32[]{:S(2)}, u32[]{:S(2)}) collective-permute-start(bf16[32,1664]{1,0:T(8,128)(2,1)S(1)} %shard_map.127.own_ref), channel_id=1, source_target_pairs={{0,24},{8,16},{16,8},{24,0},{1,25},{9,17},{17,9},{25,1},{2,26},{10... | collective-permute-start | bytes 319496 | tf_op jit(solution)/shard_map/ppermute | solution.py:220
  17.1 6.7 %collective-permute-start.11 = (bf16[32,1664]{1,0:T(8,128)(2,1)S(1)}, bf16[32,1664]{1,0:T(8,128)(2,1)S(1)}, u32[]{:S(2)}, u32[]{:S(2)}) collective-permute-start(bf16[32,1664]{1,0:T(8,128)(2,1)S(1)} %shard_map.127.own_ref), channel_id=1, source_target_pairs={{0,8},{8,0},{16,24},{24,16},{1,9},{9,1},{17,25},{25,17},{2,10},{10... | collective-permute-start | bytes 319496 | tf_op jit(solution)/shard_map/ppermute | solution.py:220
  17.6 6.1 %collective-permute-start.10 = (bf16[32,1664]{1,0:T(8,128)(2,1)S(1)}, bf16[32,1664]{1,0:T(8,128)(2,1)S(1)}, u32[]{:S(2)}, u32[]{:S(2)}) collective-permute-start(bf16[32,1664]{1,0:T(8,128)(2,1)S(1)} %shard_map.127.own_ref), channel_id=1, source_target_pairs={{0,16},{8,24},{16,0},{24,8},{1,17},{9,25},{17,1},{25,9},{2,18},{10... | collective-permute-start | bytes 319496 | tf_op jit(solution)/shard_map/ppermute | solution.py:220
  19.2 5.9 %collective-permute-start.9 = (bf16[32,1664]{1,0:T(8,128)(2,1)S(1)}, bf16[32,1664]{1,0:T(8,128)(2,1)S(1)}, u32[]{:S(2)}, u32[]{:S(2)}) collective-permute-start(bf16[32,1664]{1,0:T(8,128)(2,1)S(1)} %shard_map.124.own_ref), channel_id=1, source_target_pairs={{0,8},{8,0},{16,24},{24,16},{1,9},{9,1},{17,25},{25,17},{2,10},{10... | collective-permute-start | bytes 319496 | tf_op jit(solution)/shard_map/ppermute | solution.py:220
  24.7 1.4 %collective-permute-start.13 = (bf16[32,1088]{1,0:T(8,128)(2,1)S(1)}, bf16[32,1088]{1,0:T(8,128)(2,1)S(1)}, u32[]{:S(2)}, u32[]{:S(2)}) collective-permute-start(bf16[32,1088]{1,0:T(8,128)(2,1)S(1)} %get-tuple-element.66), channel_id=1, source_target_pairs={{0,1},{1,0},{2,3},{3,2},{4,5},{5,4},{6,7},{7,6},{8,9},{9,8},{10,11... | collective-permute-start | bytes 208904 | tf_op jit(solution)/shard_map/ppermute | solution.py:220
  26.1 6.6 %collective-permute-start.14 = (bf16[8,1024]{1,0:T(8,128)(2,1)S(1)}, bf16[8,1024]{1,0:T(8,128)(2,1)S(1)}, u32[]{:S(2)}, u32[]{:S(2)}) collective-permute-start(bf16[8,1024]{1,0:T(8,128)(2,1)S(1)} %get-tuple-element.68), channel_id=1, source_target_pairs={{0,6},{1,7},{2,4},{3,5},{4,2},{5,3},{6,0},{7,1},{8,14},{9,15},{10,... | collective-permute-start | bytes 49160 | tf_op jit(solution)/shard_map/ppermute | solution.py:220
  28.2 4.6 %collective-permute-start.15 = (bf16[8,1024]{1,0:T(8,128)(2,1)S(1)}, bf16[8,1024]{1,0:T(8,128)(2,1)S(1)}, u32[]{:S(2)}, u32[]{:S(2)}) collective-permute-start(bf16[8,1024]{1,0:T(8,128)(2,1)S(1)} %get-tuple-element.69), channel_id=1, source_target_pairs={{0,4},{1,5},{2,6},{3,7},{4,0},{5,1},{6,2},{7,3},{8,12},{9,13},{10,... | collective-permute-start | bytes 49160 | tf_op jit(solution)/shard_map/ppermute | solution.py:220
  28.2 4.6 %collective-permute-start.16 = (bf16[8,1024]{1,0:T(8,128)(2,1)S(1)}, bf16[8,1024]{1,0:T(8,128)(2,1)S(1)}, u32[]{:S(2)}, u32[]{:S(2)}) collective-permute-start(bf16[8,1024]{1,0:T(8,128)(2,1)S(1)} %get-tuple-element.70), channel_id=1, source_target_pairs={{0,2},{1,3},{2,0},{3,1},{4,6},{5,7},{6,4},{7,5},{8,10},{9,11},{10,... | collective-permute-start | bytes 49160 | tf_op jit(solution)/shard_map/ppermute | solution.py:220
  30.6 1.2 %collective-permute-start.17 = (f32[32,64]{1,0:T(8,128)S(1)}, f32[32,64]{1,0:T(8,128)S(1)}, u32[]{:S(2)}, u32[]{:S(2)}) collective-permute-start(f32[32,64]{1,0:T(8,128)S(1)} %get-tuple-element.73), channel_id=1, source_target_pairs={{0,1},{1,0},{2,3},{3,2},{4,5},{5,4},{6,7},{7,6},{8,9},{9,8},{10,11... | collective-permute-start | bytes 24584 | tf_op jit(solution)/shard_map/ppermute | solution.py:220

commit v6 on v5

--- a/solution.py
+++ b/solution.py
@@ -390,8 +390,8 @@
         second_ref[...].astype(F32) + third_ref[...].astype(F32)
     )
     total = backward_rows(ranks, slice(0, count), total, *refs[:-3], rows_ref, back_ref)
-    give_ref[:, :width] = total.astype(BF16)
-    give_ref[:, width:] = back_ref[:, lanes // 2 :].astype(BF16)
+    give_ref[:, :width] = total
+    give_ref[:, width:] = back_ref[:, lanes // 2 :]
 
 
 def backward_rest_body(ranks, own_ref, pair_ref, *refs):
@@ -455,7 +455,6 @@
     lanes = 2 * tenants * rank
     slots = devices * count
     mine_cols = adapter_input_maps[0].transpose(1, 2, 3, 0).reshape(lanes // 2, width)
-    other_cols = swap(mine_cols, "expert", 1)
     (packed,) = local_call(
         pack_body,
         [((count, 2 * width + 128), BF16)],
@@ -468,6 +467,8 @@
         ],
         far=5,
     )
+    packed, late_cols = lax.optimization_barrier((packed, mine_cols))
+    other_cols = swap(late_cols, "expert", 1)
     stored = (
         gate_weight[0],
         up_weight[0],
@@ -523,7 +524,7 @@
     outs = [((slots // 2, 2 * hidden + lanes), BF16), ((slots // 2, lanes), F32)]
     give, rows, back = local_call(
         functools.partial(backward_body, ranks),
-        [((slots // 2, width + lanes // 2), BF16)] + outs,
+        [((slots // 2, width + lanes // 2), F32)] + outs,
         (*sums, *shared),
         flops=LONG,
     )

time: 33.7 us -> 33.8 us (level)
  transfers between devices with their start and end apart: 18 -> 18, of which waited for: 7 -> 8; matrix products, arithmetic and copies ran while one was open for 0% -> 0% of each run, Pallas kernels for 27% -> 25%
where the time goes in v6:
time: 33.8 us; the launch traced here: 33.6 us
  starting transfers between devices  17.5 us (52%)
  Pallas kernels  9.79 us (29%)
  waiting for transfers between devices  5.61 us (17%)
  between operations  0.71 us (2%)
    ppermute x18, starting transfers between devices, swap(): lax.ppermute(array, axis, [(i, i ^ offset) for i in range(lax.axis_size(a...  17.5 us
    pallas_call x12, Pallas kernels, local_call(): pl.pallas_call(body, out_shape=[jax.ShapeDtypeStruct(shape, kind) for sha...  9.79 us
    ppermute x18, waiting for transfers between devices, swap(): lax.ppermute(array, axis, [(i, i ^ offset) for i in range(lax.axis_size(a...  5.61 us
  transfers between devices with their start and end apart: 18, of which 8 were waited for; matrix products, arithmetic and copies ran while one was open for 0% of the time, Pallas kernels for 25%

profile of v6, /device:TPU:0, one launch (start us, length us, event | category | flops | bytes accessed | tf_op | source)
XLA Modules:
  0.0 33.6 jit_solution(5341558917096702328)
XLA Ops:
  0.6 0.8 %shard_map.121.refs_0_.refs_4_ = bf16[8,2176]{1,0:T(8,128)(2,1)S(1)} custom-call(bf16[8,1024]{1,0:T(8,128)(2,1)} %x_ref.1, bf16[8,1024]{1,0:T(8,128)(2,1)} %dy_ref.1, s32[2,8]{1,0:T(2,128)} %bitcast.26, bf16[2,8]{1,0:T(2,128)(2,1)} %bitcast.27, s32[1,8]{1,0:T(1,128)} %bitcast.28), custom_call_target="tpu_custom_call" | custom-call | tf_op jit(solution)/shard_map/pallas_call | solution.py:204
  1.5 0.5 %collective-permute-start.3 = (bf16[64,1024]{1,0:T(8,128)(2,1)}, bf16[64,1024]{1,0:T(8,128)(2,1)S(1)}, u32[]{:S(2)}, u32[]{:S(2)}) collective-permute-start(bf16[64,1024]{1,0:T(8,128)(2,1)} %bitcast.24), channel_id=1, source_target_pairs={{0,1},{1,0},{2,3},{3,2},{4,5},{5,4},{6,7},{7,6},{8,9},{9,8},{10,11... | collective-permute-start | bytes 393224 | tf_op jit(solution)/shard_map/ppermute | solution.py:220
  2.0 4.7 %collective-permute-start.2 = (bf16[8,2176]{1,0:T(8,128)(2,1)S(1)}, bf16[8,2176]{1,0:T(8,128)(2,1)S(1)}, u32[]{:S(2)}, u32[]{:S(2)}) collective-permute-start(bf16[8,2176]{1,0:T(8,128)(2,1)S(1)} %shard_map.121.refs_0_.refs_4_), channel_id=1, source_target_pairs={{0,6},{1,7},{2,4},{3,5},{4,2},{5,3},{6,0},{7,1},{8,14},{9,15},{10,... | collective-permute-start | bytes 104456 | tf_op jit(solution)/shard_map/ppermute | solution.py:220
  6.7 0.0 collective-permute-start.1
  6.7 0.6 %collective-permute-start = (bf16[8,2176]{1,0:T(8,128)(2,1)S(1)}, bf16[8,2176]{1,0:T(8,128)(2,1)S(1)}, u32[]{:S(2)}, u32[]{:S(2)}) collective-permute-start(bf16[8,2176]{1,0:T(8,128)(2,1)S(1)} %shard_map.121.refs_0_.refs_4_), channel_id=1, source_target_pairs={{0,2},{1,3},{2,0},{3,1},{4,6},{5,7},{6,4},{7,5},{8,10},{9,11},{10,... | collective-permute-start | bytes 104456 | tf_op jit(solution)/shard_map/ppermute | solution.py:220
  7.3 0.0 collective-permute-start.4
  7.3 2.1 %shard_map.122 = (bf16[1024,512]{1,0:T(8,128)(2,1)S(1)}, bf16[1024,512]{1,0:T(8,128)(2,1)S(1)}, bf16[512,1024]{1,0:T(8,128)(2,1)S(1)}, bf16[64,1024]{1,0:T(8,128)(2,1)S(1)}, bf16[128,512]{1,0:T(8,128)(2,1)S(1)}) custom-call(bf16[1024,512]{1,0:T(8,128)(2,1)} %bitcast.18, bf16[1024,512]{1,0:T(8,128)(2,1)} %bitcast.19, bf16[512,1024]{1,0:T(8,128)(2,1)} %bitcast.20, ...), custom_call_target="tpu_custom_call" | custom-call | bytes 3407872 | tf_op jit(solution)/shard_map/pallas_call | solution.py:204
  9.4 0.0 collective-permute-done.2.refs_3_.refs_7_
  9.4 2.1 %collective-permute-done.1.refs_2_.refs_6_ = bf16[8,2176]{1,0:T(8,128)(2,1)S(1)} collective-permute-done((bf16[8,2176]{1,0:T(8,128)(2,1)S(1)}, bf16[8,2176]{1,0:T(8,128)(2,1)S(1)}, u32[]{:S(2)}, u32[]{:S(2)}) %collective-permute-start.1) | collective-permute-done | bytes 34848 | tf_op jit(solution)/shard_map/ppermute | solution.py:220
  11.5 0.0 collective-permute-start.6
  11.5 0.0 collective-permute-done.refs_1_.refs_5_
  11.5 0.5 %collective-permute-start.5 = (bf16[8,2176]{1,0:T(8,128)(2,1)S(1)}, bf16[8,2176]{1,0:T(8,128)(2,1)S(1)}, u32[]{:S(2)}, u32[]{:S(2)}) collective-permute-start(bf16[8,2176]{1,0:T(8,128)(2,1)S(1)} %collective-permute-done.refs_1_.refs_5_), channel_id=1, source_target_pairs={{0,1},{1,0},{2,3},{3,2},{4,5},{5,4},{6,7},{7,6},{8,9},{9,8},{10,11... | collective-permute-start | bytes 104456 | tf_op jit(solution)/shard_map/ppermute | solution.py:220
  12.0 0.0 collective-permute-start.7
  12.0 0.0 collective-permute-done.3.refs_8_.refs_4_
  12.0 0.9 %shard_map.123.own_ref = bf16[32,1664]{1,0:T(8,128)(2,1)S(1)} custom-call(bf16[8,2176]{1,0:T(8,128)(2,1)S(1)} %shard_map.121.refs_0_.refs_4_, bf16[8,2176]{1,0:T(8,128)(2,1)S(1)} %collective-permute-done.refs_1_.refs_5_, bf16[8,2176]{1,0:T(8,128)(2,1)S(1)} %collective-permute-done.1.refs_2_.refs_6_, ...), custom_call_target="tpu_custom_call" | custom-call | flops 109051904 | tf_op jit(solution)/shard_map/pallas_call | solution.py:204
  12.9 0.0 collective-permute-done.4.refs_0_
  12.9 0.0 collective-permute-done.6.refs_2_
  12.9 0.0 collective-permute-done.5.refs_1_
  13.0 0.3 collective-permute-done.7.refs_3_
  13.2 1.5 %collective-permute-start.8 = (bf16[32,1664]{1,0:T(8,128)(2,1)S(1)}, bf16[32,1664]{1,0:T(8,128)(2,1)S(1)}, u32[]{:S(2)}, u32[]{:S(2)}) collective-permute-start(bf16[32,1664]{1,0:T(8,128)(2,1)S(1)} %shard_map.123.own_ref), channel_id=1, source_target_pairs={{0,16},{8,24},{16,0},{24,8},{1,17},{9,25},{17,1},{25,9},{2,18},{10... | collective-permute-start | bytes 319496 | tf_op jit(solution)/shard_map/ppermute | solution.py:220
  14.7 0.9 %shard_map.127.own_ref = bf16[32,1664]{1,0:T(8,128)(2,1)S(1)} custom-call(bf16[8,2176]{1,0:T(8,128)(2,1)S(1)} %collective-permute-done.4.refs_0_, bf16[8,2176]{1,0:T(8,128)(2,1)S(1)} %collective-permute-done.5.refs_1_, bf16[8,2176]{1,0:T(8,128)(2,1)S(1)} %collective-permute-done.6.refs_2_, bf16[8,2176]{1,0:T(8,128)(2,1)S(1)} %collective-permute-done.7.refs_3_, ...), custom_call_target="tpu_custom_call" | custom-call | flops 109051904 | tf_op jit(solution)/shard_map/pallas_call | solution.py:204
  15.6 1.5 %collective-permute-start.12 = (bf16[32,1664]{1,0:T(8,128)(2,1)S(1)}, bf16[32,1664]{1,0:T(8,128)(2,1)S(1)}, u32[]{:S(2)}, u32[]{:S(2)}) collective-permute-start(bf16[32,1664]{1,0:T(8,128)(2,1)S(1)} %shard_map.127.own_ref), channel_id=1, source_target_pairs={{0,24},{8,16},{16,8},{24,0},{1,25},{9,17},{17,9},{25,1},{2,26},{10... | collective-permute-start | bytes 319496 | tf_op jit(solution)/shard_map/ppermute | solution.py:220
  17.1 0.5 %collective-permute-start.11 = (bf16[32,1664]{1,0:T(8,128)(2,1)S(1)}, bf16[32,1664]{1,0:T(8,128)(2,1)S(1)}, u32[]{:S(2)}, u32[]{:S(2)}) collective-permute-start(bf16[32,1664]{1,0:T(8,128)(2,1)S(1)} %shard_map.127.own_ref), channel_id=1, source_target_pairs={{0,8},{8,0},{16,24},{24,16},{1,9},{9,1},{17,25},{25,17},{2,10},{10... | collective-permute-start | bytes 319496 | tf_op jit(solution)/shard_map/ppermute | solution.py:220
  17.6 1.5 %collective-permute-start.10 = (bf16[32,1664]{1,0:T(8,128)(2,1)S(1)}, bf16[32,1664]{1,0:T(8,128)(2,1)S(1)}, u32[]{:S(2)}, u32[]{:S(2)}) collective-permute-start(bf16[32,1664]{1,0:T(8,128)(2,1)S(1)} %shard_map.127.own_ref), channel_id=1, source_target_pairs={{0,16},{8,24},{16,0},{24,8},{1,17},{9,25},{17,1},{25,9},{2,18},{10... | collective-permute-start | bytes 319496 | tf_op jit(solution)/shard_map/ppermute | solution.py:220
  19.2 0.0 collective-permute-done.8.taken_ref
  19.2 1.6 %collective-permute-start.9 = (bf16[32,1664]{1,0:T(8,128)(2,1)S(1)}, bf16[32,1664]{1,0:T(8,128)(2,1)S(1)}, u32[]{:S(2)}, u32[]{:S(2)}) collective-permute-start(bf16[32,1664]{1,0:T(8,128)(2,1)S(1)} %shard_map.124.own_ref), channel_id=1, source_target_pairs={{0,8},{8,0},{16,24},{24,16},{1,9},{9,1},{17,25},{25,17},{2,10},{10... | collective-permute-start | bytes 319496 | tf_op jit(solution)/shard_map/ppermute | solution.py:220
  20.8 0.4 %shard_map.125 = (bf16[64,1024]{1,0:T(8,128)(2,1)S(1)}, f32[64,128]{1,0:T(8,128)S(1)}) custom-call(bf16[8,2176]{1,0:T(8,128)(2,1)S(1)} %collective-permute-done.4.refs_0_, bf16[8,2176]{1,0:T(8,128)(2,1)S(1)} %collective-permute-done.5.refs_1_, bf16[8,2176]{1,0:T(8,128)(2,1)S(1)} %collective-permute-done.6.refs_2_, ...), custom_call_target="tpu_custom_call" | custom-call | flops 20000000000 | tf_op jit(solution)/shard_map/pallas_call | solution.py:204
  21.2 1.2 %collective-permute-done.12.third_ref = bf16[32,1664]{1,0:T(8,128)(2,1)S(1)} collective-permute-done((bf16[32,1664]{1,0:T(8,128)(2,1)S(1)}, bf16[32,1664]{1,0:T(8,128)(2,1)S(1)}, u32[]{:S(2)}, u32[]{:S(2)}) %collective-permute-start.12) | collective-permute-done | bytes 106528 | tf_op jit(solution)/shard_map/ppermute | solution.py:220
  22.4 1.4 %collective-permute-done.11.first_ref = bf16[32,1664]{1,0:T(8,128)(2,1)S(1)} collective-permute-done((bf16[32,1664]{1,0:T(8,128)(2,1)S(1)}, bf16[32,1664]{1,0:T(8,128)(2,1)S(1)}, u32[]{:S(2)}, u32[]{:S(2)}) %collective-permute-start.11) | collective-permute-done | bytes 106528 | tf_op jit(solution)/shard_map/ppermute | solution.py:220
  23.8 0.0 collective-permute-done.10.second_ref
  23.8 1.0 %shard_map.128 = (f32[32,1088]{1,0:T(8,128)S(1)}, bf16[32,1152]{1,0:T(8,128)(2,1)S(1)}, f32[32,128]{1,0:T(8,128)S(1)}) custom-call(bf16[32,1664]{1,0:T(8,128)(2,1)S(1)} %shard_map.127.own_ref, bf16[32,1664]{1,0:T(8,128)(2,1)S(1)} %collective-permute-done.10.second_ref, bf16[32,1664]{1,0:T(8,128)(2,1)S(1)} %collective-permute-done.11.first_ref, ...), custom_call_target="tpu_custom_call" | custom-call | flops 20000000000 | tf_op jit(solution)/shard_map/pallas_call | solution.py:204
  24.7 0.1 collective-permute-start.13
  24.8 0.3 collective-permute-done.9.pair_ref
  25.1 1.0 %shard_map.126 = (f32[32,1024]{1,0:T(8,128)S(1)}, f32[32,64]{1,0:T(8,128)S(1)}, bf16[32,1152]{1,0:T(8,128)(2,1)S(1)}, f32[32,128]{1,0:T(8,128)S(1)}) custom-call(bf16[32,1664]{1,0:T(8,128)(2,1)S(1)} %shard_map.124.own_ref, bf16[32,1664]{1,0:T(8,128)(2,1)S(1)} %collective-permute-done.9.pair_ref, f32[64,128]{1,0:T(8,128)S(1)} %get-tuple-element.67.refs_0_, ...), custom_call_target="tpu_custom_call" | custom-call | flops 20000000000 | tf_op jit(solution)/shard_map/pallas_call | solution.py:204
  26.1 0.1 collective-permute-done.13.taken_ref
  26.2 2.1 %collective-permute-start.14 = (bf16[8,1024]{1,0:T(8,128)(2,1)S(1)}, bf16[8,1024]{1,0:T(8,128)(2,1)S(1)}, u32[]{:S(2)}, u32[]{:S(2)}) collective-permute-start(bf16[8,1024]{1,0:T(8,128)(2,1)S(1)} %get-tuple-element.72), channel_id=1, source_target_pairs={{0,6},{1,7},{2,4},{3,5},{4,2},{5,3},{6,0},{7,1},{8,14},{9,15},{10,... | collective-permute-start | bytes 49160 | tf_op jit(solution)/shard_map/ppermute | solution.py:220
  28.3 0.0 collective-permute-start.15
  28.3 2.3 %collective-permute-start.16 = (bf16[8,1024]{1,0:T(8,128)(2,1)S(1)}, bf16[8,1024]{1,0:T(8,128)(2,1)S(1)}, u32[]{:S(2)}, u32[]{:S(2)}) collective-permute-start(bf16[8,1024]{1,0:T(8,128)(2,1)S(1)} %get-tuple-element.74), channel_id=1, source_target_pairs={{0,2},{1,3},{2,0},{3,1},{4,6},{5,7},{6,4},{7,5},{8,10},{9,11},{10,... | collective-permute-start | bytes 49160 | tf_op jit(solution)/shard_map/ppermute | solution.py:220
  30.7 0.0 collective-permute-start.17
  30.7 1.1 %shard_map.132 = f32[128,512]{1,0:T(8,128)} custom-call(bf16[32,1152]{1,0:T(8,128)(2,1)S(1)} %get-tuple-element.79.rows_ref, bf16[32,1152]{1,0:T(8,128)(2,1)S(1)} %get-tuple-element.80.rest_rows_ref), custom_call_target="tpu_custom_call" | custom-call | tf_op jit(solution)/shard_map/pallas_call | solution.py:204
  31.8 0.1 collective-permute-done.17.rest_taken_ref
  31.8 0.9 %shard_map.131 = f32[64,1024]{1,0:T(8,128)} custom-call(f32[32,128]{1,0:T(8,128)S(1)} %get-tuple-element.75.back_ref, f32[32,128]{1,0:T(8,128)S(1)} %get-tuple-element.76.rest_back_ref, f32[32,1088]{1,0:T(8,128)S(1)} %collective-permute-done.13.taken_ref, f32[32,64]{1,0:T(8,128)S(1)} %collective-permute-done.17.rest_taken_ref, ...), custom_call_target="tpu_custom_call" | custom-call | tf_op jit(solution)/shard_map/pallas_call | solution.py:204
  32.8 0.0 collective-permute-done.14.third_ref
  32.8 0.2 collective-permute-done.15.second_ref
  33.0 0.0 collective-permute-done.16.first_ref
  33.0 0.6 %shard_map.130 = bf16[8,1024]{1,0:T(8,128)(2,1)} custom-call(f32[8,1024]{1,0:T(8,128)S(1)} %get-tuple-element.71.own_ref, bf16[8,1024]{1,0:T(8,128)(2,1)S(1)} %collective-permute-done.14.third_ref, bf16[8,1024]{1,0:T(8,128)(2,1)S(1)} %collective-permute-done.15.second_ref, bf16[8,1024]{1,0:T(8,128)(2,1)S(1)} %collective-permute-done.16.first_ref), custom_call_target="tpu_custom_call" | custom-call | tf_op jit(solution)/shard_map/pallas_call | solution.py:204
  (2 shorter events, 0.1 us)
Async XLA Ops:
  1.5 10.6 %collective-permute-start.3 = (bf16[64,1024]{1,0:T(8,128)(2,1)}, bf16[64,1024]{1,0:T(8,128)(2,1)S(1)}, u32[]{:S(2)}, u32[]{:S(2)}) collective-permute-start(bf16[64,1024]{1,0:T(8,128)(2,1)} %bitcast.24), channel_id=1, source_target_pairs={{0,1},{1,0},{2,3},{3,2},{4,5},{5,4},{6,7},{7,6},{8,9},{9,8},{10,11... | collective-permute-start | bytes 393224 | tf_op jit(solution)/shard_map/ppermute | solution.py:220
  2.0 7.4 %collective-permute-start.2 = (bf16[8,2176]{1,0:T(8,128)(2,1)S(1)}, bf16[8,2176]{1,0:T(8,128)(2,1)S(1)}, u32[]{:S(2)}, u32[]{:S(2)}) collective-permute-start(bf16[8,2176]{1,0:T(8,128)(2,1)S(1)} %shard_map.121.refs_0_.refs_4_), channel_id=1, source_target_pairs={{0,6},{1,7},{2,4},{3,5},{4,2},{5,3},{6,0},{7,1},{8,14},{9,15},{10,... | collective-permute-start | bytes 104456 | tf_op jit(solution)/shard_map/ppermute | solution.py:220
  6.7 4.8 %collective-permute-start.1 = (bf16[8,2176]{1,0:T(8,128)(2,1)S(1)}, bf16[8,2176]{1,0:T(8,128)(2,1)S(1)}, u32[]{:S(2)}, u32[]{:S(2)}) collective-permute-start(bf16[8,2176]{1,0:T(8,128)(2,1)S(1)} %shard_map.121.refs_0_.refs_4_), channel_id=1, source_target_pairs={{0,4},{1,5},{2,6},{3,7},{4,0},{5,1},{6,2},{7,3},{8,12},{9,13},{10,... | collective-permute-start | bytes 104456 | tf_op jit(solution)/shard_map/ppermute | solution.py:220
  6.7 4.8 %collective-permute-start = (bf16[8,2176]{1,0:T(8,128)(2,1)S(1)}, bf16[8,2176]{1,0:T(8,128)(2,1)S(1)}, u32[]{:S(2)}, u32[]{:S(2)}) collective-permute-start(bf16[8,2176]{1,0:T(8,128)(2,1)S(1)} %shard_map.121.refs_0_.refs_4_), channel_id=1, source_target_pairs={{0,2},{1,3},{2,0},{3,1},{4,6},{5,7},{6,4},{7,5},{8,10},{9,11},{10,... | collective-permute-start | bytes 104456 | tf_op jit(solution)/shard_map/ppermute | solution.py:220
  7.3 5.6 %collective-permute-start.4 = (bf16[8,2176]{1,0:T(8,128)(2,1)S(1)}, bf16[8,2176]{1,0:T(8,128)(2,1)S(1)}, u32[]{:S(2)}, u32[]{:S(2)}) collective-permute-start(bf16[8,2176]{1,0:T(8,128)(2,1)S(1)} %shard_map.121.refs_0_.refs_4_), channel_id=1, source_target_pairs={{0,1},{1,0},{2,3},{3,2},{4,5},{5,4},{6,7},{7,6},{8,9},{9,8},{10,11... | collective-permute-start | bytes 104456 | tf_op jit(solution)/shard_map/ppermute | solution.py:220
  11.5 1.4 %collective-permute-start.6 = (bf16[8,2176]{1,0:T(8,128)(2,1)S(1)}, bf16[8,2176]{1,0:T(8,128)(2,1)S(1)}, u32[]{:S(2)}, u32[]{:S(2)}) collective-permute-start(bf16[8,2176]{1,0:T(8,128)(2,1)S(1)} %collective-permute-done.1.refs_2_.refs_6_), channel_id=1, source_target_pairs={{0,1},{1,0},{2,3},{3,2},{4,5},{5,4},{6,7},{7,6},{8,9},{9,8},{10,11... | collective-permute-start | bytes 104456 | tf_op jit(solution)/shard_map/ppermute | solution.py:220
  11.5 1.4 %collective-permute-start.5 = (bf16[8,2176]{1,0:T(8,128)(2,1)S(1)}, bf16[8,2176]{1,0:T(8,128)(2,1)S(1)}, u32[]{:S(2)}, u32[]{:S(2)}) collective-permute-start(bf16[8,2176]{1,0:T(8,128)(2,1)S(1)} %collective-permute-done.refs_1_.refs_5_), channel_id=1, source_target_pairs={{0,1},{1,0},{2,3},{3,2},{4,5},{5,4},{6,7},{7,6},{8,9},{9,8},{10,11... | collective-permute-start | bytes 104456 | tf_op jit(solution)/shard_map/ppermute | solution.py:220
  12.0 1.2 %collective-permute-start.7 = (bf16[8,2176]{1,0:T(8,128)(2,1)S(1)}, bf16[8,2176]{1,0:T(8,128)(2,1)S(1)}, u32[]{:S(2)}, u32[]{:S(2)}) collective-permute-start(bf16[8,2176]{1,0:T(8,128)(2,1)S(1)} %collective-permute-done.2.refs_3_.refs_7_), channel_id=1, source_target_pairs={{0,1},{1,0},{2,3},{3,2},{4,5},{5,4},{6,7},{7,6},{8,9},{9,8},{10,11... | collective-permute-start | bytes 104456 | tf_op jit(solution)/shard_map/ppermute | solution.py:220
  13.2 5.9 %collective-permute-start.8 = (bf16[32,1664]{1,0:T(8,128)(2,1)S(1)}, bf16[32,1664]{1,0:T(8,128)(2,1)S(1)}, u32[]{:S(2)}, u32[]{:S(2)}) collective-permute-start(bf16[32,1664]{1,0:T(8,128)(2,1)S(1)} %shard_map.123.own_ref), channel_id=1, source_target_pairs={{0,16},{8,24},{16,0},{24,8},{1,17},{9,25},{17,1},{25,9},{2,18},{10... | collective-permute-start | bytes 319496 | tf_op jit(solution)/shard_map/ppermute | solution.py:220
  15.6 6.8 %collective-permute-start.12 = (bf16[32,1664]{1,0:T(8,128)(2,1)S(1)}, bf16[32,1664]{1,0:T(8,128)(2,1)S(1)}, u32[]{:S(2)}, u32[]{:S(2)}) collective-permute-start(bf16[32,1664]{1,0:T(8,128)(2,1)S(1)} %shard_map.127.own_ref), channel_id=1, source_target_pairs={{0,24},{8,16},{16,8},{24,0},{1,25},{9,17},{17,9},{25,1},{2,26},{10... | collective-permute-start | bytes 319496 | tf_op jit(solution)/shard_map/ppermute | solution.py:220
  17.1 6.7 %collective-permute-start.11 = (bf16[32,1664]{1,0:T(8,128)(2,1)S(1)}, bf16[32,1664]{1,0:T(8,128)(2,1)S(1)}, u32[]{:S(2)}, u32[]{:S(2)}) collective-permute-start(bf16[32,1664]{1,0:T(8,128)(2,1)S(1)} %shard_map.127.own_ref), channel_id=1, source_target_pairs={{0,8},{8,0},{16,24},{24,16},{1,9},{9,1},{17,25},{25,17},{2,10},{10... | collective-permute-start | bytes 319496 | tf_op jit(solution)/shard_map/ppermute | solution.py:220
  17.6 6.1 %collective-permute-start.10 = (bf16[32,1664]{1,0:T(8,128)(2,1)S(1)}, bf16[32,1664]{1,0:T(8,128)(2,1)S(1)}, u32[]{:S(2)}, u32[]{:S(2)}) collective-permute-start(bf16[32,1664]{1,0:T(8,128)(2,1)S(1)} %shard_map.127.own_ref), channel_id=1, source_target_pairs={{0,16},{8,24},{16,0},{24,8},{1,17},{9,25},{17,1},{25,9},{2,18},{10... | collective-permute-start | bytes 319496 | tf_op jit(solution)/shard_map/ppermute | solution.py:220
  19.2 5.9 %collective-permute-start.9 = (bf16[32,1664]{1,0:T(8,128)(2,1)S(1)}, bf16[32,1664]{1,0:T(8,128)(2,1)S(1)}, u32[]{:S(2)}, u32[]{:S(2)}) collective-permute-start(bf16[32,1664]{1,0:T(8,128)(2,1)S(1)} %shard_map.124.own_ref), channel_id=1, source_target_pairs={{0,8},{8,0},{16,24},{24,16},{1,9},{9,1},{17,25},{25,17},{2,10},{10... | collective-permute-start | bytes 319496 | tf_op jit(solution)/shard_map/ppermute | solution.py:220
  24.7 1.4 %collective-permute-start.13 = (f32[32,1088]{1,0:T(8,128)S(1)}, f32[32,1088]{1,0:T(8,128)S(1)}, u32[]{:S(2)}, u32[]{:S(2)}) collective-permute-start(f32[32,1088]{1,0:T(8,128)S(1)} %get-tuple-element.70), channel_id=1, source_target_pairs={{0,1},{1,0},{2,3},{3,2},{4,5},{5,4},{6,7},{7,6},{8,9},{9,8},{10,11... | collective-permute-start | bytes 417800 | tf_op jit(solution)/shard_map/ppermute | solution.py:220
  26.2 6.5 %collective-permute-start.14 = (bf16[8,1024]{1,0:T(8,128)(2,1)S(1)}, bf16[8,1024]{1,0:T(8,128)(2,1)S(1)}, u32[]{:S(2)}, u32[]{:S(2)}) collective-permute-start(bf16[8,1024]{1,0:T(8,128)(2,1)S(1)} %get-tuple-element.72), channel_id=1, source_target_pairs={{0,6},{1,7},{2,4},{3,5},{4,2},{5,3},{6,0},{7,1},{8,14},{9,15},{10,... | collective-permute-start | bytes 49160 | tf_op jit(solution)/shard_map/ppermute | solution.py:220
  28.3 4.6 %collective-permute-start.15 = (bf16[8,1024]{1,0:T(8,128)(2,1)S(1)}, bf16[8,1024]{1,0:T(8,128)(2,1)S(1)}, u32[]{:S(2)}, u32[]{:S(2)}) collective-permute-start(bf16[8,1024]{1,0:T(8,128)(2,1)S(1)} %get-tuple-element.73), channel_id=1, source_target_pairs={{0,4},{1,5},{2,6},{3,7},{4,0},{5,1},{6,2},{7,3},{8,12},{9,13},{10,... | collective-permute-start | bytes 49160 | tf_op jit(solution)/shard_map/ppermute | solution.py:220
  28.3 4.6 %collective-permute-start.16 = (bf16[8,1024]{1,0:T(8,128)(2,1)S(1)}, bf16[8,1024]{1,0:T(8,128)(2,1)S(1)}, u32[]{:S(2)}, u32[]{:S(2)}) collective-permute-start(bf16[8,1024]{1,0:T(8,128)(2,1)S(1)} %get-tuple-element.74), channel_id=1, source_target_pairs={{0,2},{1,3},{2,0},{3,1},{4,6},{5,7},{6,4},{7,5},{8,10},{9,11},{10,... | collective-permute-start | bytes 49160 | tf_op jit(solution)/shard_map/ppermute | solution.py:220
  30.7 1.2 %collective-permute-start.17 = (f32[32,64]{1,0:T(8,128)S(1)}, f32[32,64]{1,0:T(8,128)S(1)}, u32[]{:S(2)}, u32[]{:S(2)}) collective-permute-start(f32[32,64]{1,0:T(8,128)S(1)} %get-tuple-element.77), channel_id=1, source_target_pairs={{0,1},{1,0},{2,3},{3,2},{4,5},{5,4},{6,7},{7,6},{8,9},{9,8},{10,11... | collective-permute-start | bytes 24584 | tf_op jit(solution)/shard_map/ppermute | solution.py:220
